TPU v7x, 32 devices: a whole 2x2x4 slice. The times are simulated.
32 devices in a mesh: region: 8 (over z, x), order: 4 (over y, core).
Axes of the slice: x: 2, y: 2, z: 4, core: 2. Of those that a mesh axis runs over, the one named last changes fastest.
Arguments:
- runoff: float32 [240, 32, 1024], P(None, None, ('region', 'order')), may hold values from 0.01 to 2
- send_rows: int32 [8, 4, 32], P('region', 'order'), may hold values from 0 to 31
- remap_index: int32 [4096, 4], P(('region', 'order')), may hold values from 0 to 31
- remap_weight: float32 [4096, 4], P(('region', 'order')), may hold values from 0.05 to 1
- class_id: int32 [4096, 1], P(('region', 'order')), may hold values from 0 to 7; in each aligned block of 128 rows (0 to 127, 128 to 255, ...) at most 32 rows name the same one
- kernel_shape: float32 [8, 240], replicated, may hold values from 0.5 to 2
- kernel_rate: float32 [8], replicated, may hold values from 0.01 to 0.3
- outlets: int32 [8, 4, 32], P('region', 'order'), may hold values from 0 to 127, as said below
- incidence: int32 [8, 4, 32, 128], P('region', 'order'), may hold values from 0 to 1, as said below
Outputs:
- outflow: bfloat16 [240, 32, 4096], P(None, None, ('region', 'order'))
Inputs may be any that keep to these rules, and one draw needn't show every extreme that they name: `send_rows`: row of the sending device's own grid rows. `class_id`: no class is named by more than 32 reaches of one device; on some device a class has exactly 32. `outlets`: the 32 outlet numbers of one device are distinct. `incidence`: each row has exactly one 1; no column of one device has more than one 1.
All inputs are finite; a program needn't handle non-finite values.
Results may differ from a plain program's by a relative error of at most 0.0038.
Values may be sent and summed in bfloat16 or wider, within the bound.
No kernel may reach another device: no remote copies, remote signals or barrier semaphores. Data moves between devices by JAX's collectives and lax.ppermute only.
A program may use at most 128 MiB of HBM per device.

v0:
```python
import jax
import jax.numpy as jnp
from jax import lax
from jax.sharding import PartitionSpec as P


def shifted(value, axis, steps):
    count = lax.axis_size(axis)
    initial, last = (max(0, -steps), min(count, count - steps))
    return lax.ppermute(value, axis, [(source, source + steps) for source in range(initial, last)])


def toeplitz_table(kernel_shape, kernel_rate, hour_count):
    lag_hours = jnp.arange(hour_count, dtype=jnp.float32)
    kernel = (
        kernel_rate[:, None] * kernel_shape * jnp.exp(-kernel_rate[:, None] * lag_hours[None, :])
    )
    kernel = kernel.astype(jnp.bfloat16)
    steps_apart = jnp.arange(hour_count)[:, None] - jnp.arange(hour_count)[None, :]
    lagged = jnp.take(kernel, jnp.clip(steps_apart, 0, hour_count - 1), axis=1)
    return jnp.where(steps_apart[None] >= 0, lagged, jnp.zeros((), jnp.bfloat16))


def local(
    runoff,
    send_rows,
    remap_index,
    remap_weight,
    class_id,
    kernel_shape,
    kernel_rate,
    outlets,
    incidence,
):
    hour_count = runoff.shape[0]
    class_count = kernel_shape.shape[0]
    reach_count = remap_index.shape[0]
    capacity = reach_count // 4
    toeplitz = toeplitz_table(kernel_shape, kernel_rate, hour_count)
    outgoing = jnp.take(runoff, send_rows.reshape(-1), axis=2)
    recv_count = outgoing.shape[2]
    classes = class_id[:, 0]
    class_hits = (classes[:, None] == jnp.arange(class_count)[None, :]).astype(jnp.int32)
    class_rank = jnp.sum((jnp.cumsum(class_hits, axis=0) - 1) * class_hits, axis=1)
    slot_of = classes * capacity + class_rank
    slot_match = (slot_of[:, None] == jnp.arange(class_count * capacity)[None, :]).astype(
        jnp.float32
    )
    reach_weights = jnp.zeros((recv_count, reach_count), jnp.float32)
    for column in range(remap_index.shape[1]):
        hits = remap_index[:, column][None, :] == jnp.arange(recv_count)[:, None]
        reach_weights = reach_weights + jnp.where(hits, remap_weight[:, column][None, :], 0.0)
    slot_weights = jnp.dot(reach_weights, slot_match, precision=lax.Precision.HIGHEST)
    received = lax.all_to_all(outgoing, "region", split_axis=2, concat_axis=2, tiled=True)
    member_count = received.shape[1]
    slotted = jnp.einsum(
        "tmr,rs->tms", received, slot_weights, precision=lax.Precision.HIGHEST
    ).astype(jnp.bfloat16)
    grouped = slotted.reshape(hour_count, member_count, class_count, capacity)
    convolved = jnp.einsum("kts,smkp->tmkp", toeplitz, grouped, preferred_element_type=jnp.float32)
    flat_slots = convolved.reshape(hour_count, member_count, class_count * capacity)
    base_flow = jnp.take(flat_slots, slot_of, axis=2)
    outlet_ids = outlets.reshape(-1)
    links = incidence.reshape(incidence.shape[2], incidence.shape[3])
    target_class = jnp.sum(links * classes[None, :], axis=1)
    class_pick = (target_class[:, None] == jnp.arange(class_count)[None, :]).astype(jnp.bfloat16)
    panel_toeplitz = jnp.einsum(
        "jk,kts->jts", class_pick, toeplitz, preferred_element_type=jnp.float32
    ).astype(jnp.bfloat16)
    outlet_pick = (outlet_ids[None, :] == jnp.arange(reach_count)[:, None]).astype(jnp.float32)
    link_float = links.astype(jnp.float32)
    passing = jnp.dot(link_float, outlet_pick, precision=lax.Precision.HIGHEST)
    outlet_base = jnp.take(base_flow, outlet_ids, axis=2)
    panel = outlet_base.astype(jnp.bfloat16)
    inflow = jnp.zeros_like(panel)
    for repeat in range(lax.axis_size("order") - 1):
        inflow = shifted(panel, "order", 1)
        arriving = jnp.einsum(
            "jts,smj->tmj", panel_toeplitz, inflow, preferred_element_type=jnp.float32
        )
        panel = (
            outlet_base
            + jnp.einsum("tmj,ji->tmi", arriving, passing, precision=lax.Precision.HIGHEST)
        ).astype(jnp.bfloat16)
    arriving = jnp.einsum(
        "jts,smj->tmj", panel_toeplitz, inflow, preferred_element_type=jnp.float32
    )
    total = base_flow + jnp.einsum(
        "tmj,jc->tmc", arriving, link_float, precision=lax.Precision.HIGHEST
    )
    return total.astype(jnp.bfloat16)


def solution(mesh):
    return jax.shard_map(
        local,
        mesh=mesh,
        in_specs=(
            P(None, None, ("region", "order")),
            P("region", "order", None),
            P(("region", "order"), None),
            P(("region", "order"), None),
            P(("region", "order"), None),
            P(),
            P(),
            P("region", "order", None),
            P("region", "order", None, None),
        ),
        out_specs=P(None, None, ("region", "order")),
        check_vma=False,
    )
```

profile of v0, /device:TPU:1, one launch (start us, length us, event | category | flops | bytes accessed | tf_op | source)
XLA Modules:
  0.0 251.4 jit_solution(14128759159430004170)
XLA Ops:
  0.0 0.7 fusion.62
  0.8 0.7 compare_and_fusion.1
  1.4 2.1 gather_fusion
  3.8 1.6 copy.52
  5.3 6.4 %all-to-all-start = ((f32[240,32,32]{0,1,2:T(8,128)}), f32[240,32,32]{0,1,2:T(8,128)S(1)}, u32[]{:S(2)}, u32[]{:S(2)}) async-start(f32[240,32,32]{0,1,2:T(8,128)} %copy.52), calls=%async_computation | async-start | bytes 2097152 | tf_op jit(solution)/shard_map/all_to_all | solution.py:54
  12.7 115.6 %gather_fusion.1 = bf16[57600,8]{1,0:T(8,128)(2,1)} fusion(bf16[8,240]{0,1:T(8,128)(2,1)S(1)} %copy.55, s32[58368]{0:T(1024)S(1)} %pad_clamp_fusion), kind=kCustom, calls=%fused_computation.1 | custom fusion | bytes 2073600 | tf_op jit(solution)/shard_map/jit(_take)/gather | solution.py:20
  128.4 10.0 %copy.56 = bf16[240,240,8]{1,2,0:T(8,128)(2,1)S(1)} copy(bf16[240,240,8]{2,1,0:T(8,128)(2,1)} %bitcast.96) | data formatting | bytes 1843200 | tf_op jit(solution)/shard_map/jit(_take)/gather | solution.py:20
  139.3 3.7 %copy.53 = f32[240,32,32]{2,1,0:T(8,128)} copy(f32[240,32,32]{0,1,2:T(8,128)S(1)} %all-to-all-done) | data formatting | bytes 1966080 | tf_op jit(solution)/shard_map/all_to_all | solution.py:54
  143.0 9.4 %convolution_convert_fusion.1 = bf16[240,32,256]{2,1,0:T(8,128)(2,1)} fusion(f32[240,32,32]{2,1,0:T(8,128)} %copy.53, f32[32,256,1]{1,0,2:T(8,128)S(1)} %convolution_bitcast_fusion), kind=kOutput, calls=%fused_computation.16 | convolution fusion | flops 756940800 | bytes 4947968 | tf_op jit(solution)/shard_map/tmr,rs->tms/dot_general | solution.py:56
  152.4 7.4 %copy.54 = bf16[240,32,256]{0,2,1:T(8,128)(2,1)} copy(bf16[240,32,256]{2,1,0:T(8,128)(2,1)} %convolution_convert_fusion.1) | data formatting | bytes 7864320 | tf_op jit(solution)/shard_map/convert_element_type | solution.py:58
  159.8 3.5 %fusion.2 = f32[240,32,8,32]{0,3,1,2:T(8,128)S(1)} fusion(bf16[240,32,8,32]{0,3,2,1:T(8,128)(2,1)} %bitcast.95, bf16[8,240,240,1]{2,0,1,3:T(8,128)(2,1)S(1)} %fusion.26), kind=kOutput, calls=%fused_computation.8 | convolution fusion | flops 943718400 | bytes 12718080 | tf_op jit(solution)/shard_map/kts,smkp->tmkp/dot_general | solution.py:60
  163.3 1.7 copy.59
  165.0 8.1 %copy.60 = f32[240,32,256]{0,1,2:T(8,128)} copy(f32[240,32,256]{0,2,1:T(8,128)S(1)} %bitcast.94) | data formatting | bytes 15728640 | tf_op jit(solution)/shard_map/reshape | solution.py:61
  173.1 6.2 %gather_fusion.2 = f32[128,240,32]{1,2,0:T(8,128)} fusion(f32[240,32,256]{0,1,2:T(8,128)} %copy.60, s32[1024]{0:T(1024)S(1)} %pad_clamp_fusion.2), kind=kCustom, calls=%fused_computation.2 | custom fusion | bytes 7864832 | tf_op jit(solution)/shard_map/jit(_take)/gather | solution.py:62
  179.2 5.6 %copy.61 = f32[128,240,32]{0,2,1:T(8,128)} copy(f32[128,240,32]{1,2,0:T(8,128)} %gather_fusion.2) | data formatting | bytes 7864320 | tf_op jit(solution)/shard_map/jit(_take)/gather | solution.py:62
  184.8 4.4 %select_bitcast_fusion = f32[240,32,128]{2,1,0:T(8,128)} fusion(f32[128,240,32]{0,2,1:T(8,128)} %copy.61, pred[128]{0:T(512)(128)(4,1)S(1)} %and_bitcast_fusion), kind=kLoop, calls=%fused_computation.6 | loop fusion | flops 983040 | bytes 7864448 | tf_op jit(solution)/shard_map/jit(_take)/select_n | solution.py:62
  189.3 5.6 %copy.62 = f32[240,32,128]{0,1,2:T(8,128)} copy(f32[240,32,128]{2,1,0:T(8,128)} %select_bitcast_fusion) | data formatting | bytes 7864320 | tf_op jit(solution)/shard_map/jit(_take)/select_n | solution.py:62
  194.9 2.8 %gather_fusion.3 = f32[32,240,32]{1,2,0:T(8,128)S(1)} fusion(f32[240,32,128]{0,1,2:T(8,128)} %copy.62, s32[1024]{0:T(1024)S(1)} %pad_clamp_fusion.1), kind=kCustom, calls=%fused_computation.3 | custom fusion | bytes 1966208 | tf_op jit(solution)/shard_map/jit(_take)/gather | solution.py:73
  198.3 4.2 %collective-permute-start = (bf16[240,32,32]{0,2,1:T(8,128)(2,1)S(1)}, bf16[240,32,32]{0,2,1:T(8,128)(2,1)S(1)}, u32[]{:S(2)}, u32[]{:S(2)}) collective-permute-start(bf16[240,32,32]{0,2,1:T(8,128)(2,1)S(1)} %bitcast_convert_fusion), channel_id=1, source_target_pairs={{0,1},{1,2},{2,3},{4,5},{5,6},{6,7},{8,9},{9,10},{10,11},{12,13},{... | collective-permute-start | bytes 1474568 | tf_op jit(solution)/shard_map/ppermute | solution.py:10
  202.8 1.2 convolution_convert_fusion
  204.0 4.3 %collective-permute-done = bf16[240,32,32]{0,2,1:T(8,128)(2,1)S(1)} collective-permute-done((bf16[240,32,32]{0,2,1:T(8,128)(2,1)S(1)}, bf16[240,32,32]{0,2,1:T(8,128)(2,1)S(1)}, u32[]{:S(2)}, u32[]{:S(2)}) %collective-permute-start) | collective-permute-done | bytes 491552 | tf_op jit(solution)/shard_map/ppermute | solution.py:10
  208.4 2.4 fusion.11
  210.8 2.2 fusion.20
  213.1 4.4 %collective-permute-start.1 = (bf16[240,32,32]{0,2,1:T(8,128)(2,1)S(1)}, bf16[240,32,32]{0,2,1:T(8,128)(2,1)S(1)}, u32[]{:S(2)}, u32[]{:S(2)}) collective-permute-start(bf16[240,32,32]{0,2,1:T(8,128)(2,1)S(1)} %fusion.20), channel_id=1, source_target_pairs={{0,1},{1,2},{2,3},{4,5},{5,6},{6,7},{8,9},{9,10},{10,11},{12,13},{... | collective-permute-start | bytes 1474568 | tf_op jit(solution)/shard_map/ppermute | solution.py:10
  217.5 6.1 %collective-permute-done.1 = bf16[240,32,32]{0,2,1:T(8,128)(2,1)S(1)} collective-permute-done((bf16[240,32,32]{0,2,1:T(8,128)(2,1)S(1)}, bf16[240,32,32]{0,2,1:T(8,128)(2,1)S(1)}, u32[]{:S(2)}, u32[]{:S(2)}) %collective-permute-start.1) | collective-permute-done | bytes 491552 | tf_op jit(solution)/shard_map/ppermute | solution.py:10
  223.6 2.4 fusion.14
  226.0 2.2 fusion.21
  228.3 4.7 %collective-permute-start.2 = (bf16[240,32,32]{0,2,1:T(8,128)(2,1)S(1)}, bf16[240,32,32]{0,2,1:T(8,128)(2,1)S(1)}, u32[]{:S(2)}, u32[]{:S(2)}) collective-permute-start(bf16[240,32,32]{0,2,1:T(8,128)(2,1)S(1)} %fusion.21), channel_id=1, source_target_pairs={{0,1},{1,2},{2,3},{4,5},{5,6},{6,7},{8,9},{9,10},{10,11},{12,13},{... | collective-permute-start | bytes 1474568 | tf_op jit(solution)/shard_map/ppermute | solution.py:10
  232.9 5.8 %collective-permute-done.2 = bf16[240,32,32]{0,2,1:T(8,128)(2,1)S(1)} collective-permute-done((bf16[240,32,32]{0,2,1:T(8,128)(2,1)S(1)}, bf16[240,32,32]{0,2,1:T(8,128)(2,1)S(1)}, u32[]{:S(2)}, u32[]{:S(2)}) %collective-permute-start.2) | collective-permute-done | bytes 491552 | tf_op jit(solution)/shard_map/ppermute | solution.py:10
  238.8 2.4 fusion.17
  241.2 3.7 %copy.72 = f32[240,32,32]{2,1,0:T(8,128)} copy(f32[240,32,32]{0,1,2:T(8,128)S(1)} %fusion.17) | data formatting | bytes 1966080 | tf_op jit(solution)/shard_map/jts,smj->tmj/transpose | solution.py:85
  244.9 6.5 %add_convert_fusion = bf16[240,32,128]{2,1,0:T(8,128)(2,1)} fusion(f32[240,32,128]{2,1,0:T(8,128)} %select_bitcast_fusion, f32[240,32,32]{2,1,0:T(8,128)} %copy.72, s32[1,1,32,128]{3,2,1,0:T(8,128)S(1)} %copy-done.2), kind=kOutput, calls=%fused_computation.7 | convolution fusion | flops 379457536 | bytes 6897664 | tf_op jit(solution)/shard_map/tmj,jc->tmc/dot_general | solution.py:88
  (43 shorter events, 3.0 us)
Async XLA Ops:
  0.0 1.4 copy-start
  3.5 8.2 %copy-start.3 = (s32[128,1]{0,1:T(1,128)S(1)}, s32[128,1]{0,1:T(1,128)}, u32[]{:S(2)}) copy-start(s32[128,1]{0,1:T(1,128)} %param.13) | copy-start | bytes 1540
  3.5 8.7 %copy-start.8 = (f32[8]{0:T(128)S(1)}, f32[8]{0:T(128)}, u32[]{:S(2)}) copy-start(f32[8]{0:T(128)} %param.15) | copy-start | bytes 100
  3.5 9.0 %copy-start.4 = (f32[8,240]{1,0:T(8,128)S(1)}, f32[8,240]{1,0:T(8,128)}, u32[]{:S(2)}) copy-start(f32[8,240]{1,0:T(8,128)} %param.14) | copy-start | bytes 23044
  3.6 9.0 %copy-start.5 = (s32[128,4]{0,1:T(4,128)S(1)}, s32[128,4]{0,1:T(4,128)}, u32[]{:S(2)}) copy-start(s32[128,4]{0,1:T(4,128)} %param.11) | copy-start | bytes 6148
  5.3 134.0 %all-to-all-start = ((f32[240,32,32]{0,1,2:T(8,128)}), f32[240,32,32]{0,1,2:T(8,128)S(1)}, u32[]{:S(2)}, u32[]{:S(2)}) async-start(f32[240,32,32]{0,1,2:T(8,128)} %copy.52), calls=%async_computation | async-start | bytes 2097152 | tf_op jit(solution)/shard_map/all_to_all | solution.py:54
  128.4 10.0 %copy-start.7 = (s32[1,1,32]{2,1,0:T(1,128)S(1)}, s32[1,1,32]{2,1,0:T(1,128)}, u32[]{:S(2)}) copy-start(s32[1,1,32]{2,1,0:T(1,128)} %param.16) | copy-start | bytes 388
  128.4 10.0 %copy-start.6 = (f32[128,4]{0,1:T(4,128)S(1)}, f32[128,4]{0,1:T(4,128)}, u32[]{:S(2)}) copy-start(f32[128,4]{0,1:T(4,128)} %param.12) | copy-start | bytes 6148
  194.9 7.6 %copy-start.2 = (s32[1,1,32,128]{3,2,1,0:T(8,128)S(1)}, s32[1,1,32,128]{3,2,1,0:T(8,128)}, u32[]{:S(2)}) copy-start(s32[1,1,32,128]{3,2,1,0:T(8,128)} %param.17) | copy-start | bytes 49156
  198.3 10.1 %collective-permute-start = (bf16[240,32,32]{0,2,1:T(8,128)(2,1)S(1)}, bf16[240,32,32]{0,2,1:T(8,128)(2,1)S(1)}, u32[]{:S(2)}, u32[]{:S(2)}) collective-permute-start(bf16[240,32,32]{0,2,1:T(8,128)(2,1)S(1)} %bitcast_convert_fusion), channel_id=1, source_target_pairs={{0,1},{1,2},{2,3},{4,5},{5,6},{6,7},{8,9},{9,10},{10,11},{12,13},{... | collective-permute-start | bytes 1474568 | tf_op jit(solution)/shard_map/ppermute | solution.py:10
  213.1 10.5 %collective-permute-start.1 = (bf16[240,32,32]{0,2,1:T(8,128)(2,1)S(1)}, bf16[240,32,32]{0,2,1:T(8,128)(2,1)S(1)}, u32[]{:S(2)}, u32[]{:S(2)}) collective-permute-start(bf16[240,32,32]{0,2,1:T(8,128)(2,1)S(1)} %fusion.20), channel_id=1, source_target_pairs={{0,1},{1,2},{2,3},{4,5},{5,6},{6,7},{8,9},{9,10},{10,11},{12,13},{... | collective-permute-start | bytes 1474568 | tf_op jit(solution)/shard_map/ppermute | solution.py:10
  228.3 10.5 %collective-permute-start.2 = (bf16[240,32,32]{0,2,1:T(8,128)(2,1)S(1)}, bf16[240,32,32]{0,2,1:T(8,128)(2,1)S(1)}, u32[]{:S(2)}, u32[]{:S(2)}) collective-permute-start(bf16[240,32,32]{0,2,1:T(8,128)(2,1)S(1)} %fusion.21), channel_id=1, source_target_pairs={{0,1},{1,2},{2,3},{4,5},{5,6},{6,7},{8,9},{9,10},{10,11},{12,13},{... | collective-permute-start | bytes 1474568 | tf_op jit(solution)/shard_map/ppermute | solution.py:10
  241.2 10.2 %copy-start.1 = (f32[240,32,32]{0,2,1:T(8,128)S(1)}, f32[240,32,32]{0,2,1:T(8,128)}, u32[]{:S(2)}) copy-start(f32[240,32,32]{0,2,1:T(8,128)} %param.9) | copy-start | bytes 2949124
where the time goes:
time: 253 us; the launch traced here: 251 us
  local copies, waits for them, and re-layouts  174 us (69%)
  matrix products  32.9 us (13%)
  starting transfers between devices  19.6 us (8%)
  waiting for transfers between devices  16.3 us (6%)
  other arithmetic  7.97 us (3%)
    gather x2, local copies, waits for them, and re-layouts, toeplitz_table(): lagged = jnp.take(kernel, jnp.clip(steps_apart, 0, hour_count - 1), axis=1)  126 us
    ppermute x3, waiting for transfers between devices, shifted(): lax.ppermute(value, axis, [(source, source + steps) for source in range(i...  16.3 us
    ppermute x3, starting transfers between devices, shifted(): lax.ppermute(value, axis, [(source, source + steps) for source in range(i...  13.2 us
    gather x2, local copies, waits for them, and re-layouts, local(): base_flow = jnp.take(flat_slots, slot_of, axis=2)  11.8 us
    dot_general x1, matrix products, local(): jnp.einsum('tmr,rs->tms', received, slot_weights, precision=lax.Precision...  9.39 us
    reshape x1, local copies, waits for them, and re-layouts, local(): convolved.reshape(hour_count, member_count, class_count * capacity)  8.09 us
    convert_element_type x1, local copies, waits for them, and re-layouts, local(): slotted = jnp.einsum('tmr,rs->tms', received, slot_weights, precision=lax...  7.42 us
    dot_general x3, matrix products, local(): jnp.einsum('jts,smj->tmj', panel_toeplitz, inflow, preferred_element_type...  7.34 us
  transfers between devices with their start and end apart: 4, of which 3 were waited for; matrix products, arithmetic and copies ran while one was open for 51% of the time, Pallas kernels for 0%

commit v1 on v0

v1 whole, which is shorter than its diff:
```python
import functools
import jax
import jax.numpy as jnp
from jax import lax
from jax.experimental import pallas as pl
from jax.experimental.pallas import tpu as pltpu
from jax.sharding import Mesh, PartitionSpec as P

BF = jnp.bfloat16
F32 = jnp.float32
MB = 8
LANES = 128
VMEM_LIMIT = 56 * 1024 * 1024


def iota(shape, dim):
    return lax.broadcasted_iota(jnp.int32, shape, dim)


def mm(a, b):
    return jnp.dot(a, b, preferred_element_type=F32)


def tmm(a, b):
    return lax.dot_general(a, b, (((0,), (0,)), ((), ())), preferred_element_type=F32)


def one_hot(condition):
    return jnp.where(condition, 1.0, 0.0).astype(BF)


def split(value):
    high = value.astype(BF)
    return high, (value - high.astype(F32)).astype(BF)


def call(kernel, out_shape, flops, **extra):
    nbytes = sum(s.size * s.dtype.itemsize for s in jax.tree.leaves(out_shape))
    return pl.pallas_call(
        kernel,
        out_shape=out_shape,
        compiler_params=pltpu.CompilerParams(vmem_limit_bytes=VMEM_LIMIT),
        cost_estimate=pl.CostEstimate(flops=flops, bytes_accessed=2 * nbytes, transcendentals=0),
        **extra,
    )


def vmem(count):
    return [pl.BlockSpec(memory_space=pltpu.VMEM)] * count


SCALAR = pl.BlockSpec(memory_space=pltpu.SMEM)


def convolve(table, value, classes, class_count, padded):
    pad = padded - value.shape[0]
    if pad:
        value = jnp.concatenate([value, jnp.zeros((pad, value.shape[1]), BF)], axis=0)
    parts = [value * one_hot(classes == float(k)) for k in range(class_count)]
    return mm(table, jnp.concatenate(parts, axis=0))


def pack_kernel(slot, x_ref, rows_ref, idx_ref, w_ref, cls_ref, outl_ref, inc_ref, send_ref, raw_ref):
    members, grid, hours = x_ref.shape
    regions = send_ref.shape[0]
    per = MB * slot
    count = regions * per
    recv = rows_ref.shape[1]
    row = iota((count, recv), 0)
    wanted = (row // per) * slot + row % slot
    rows = rows_ref[...].astype(F32)
    chosen = jnp.sum(jnp.where(iota((count, recv), 1) == wanted, rows, 0.0), axis=1, keepdims=True)
    lane = iota((count, MB * grid), 1)
    member = (iota((count, MB * grid), 0) // slot) % MB
    select = one_hot((lane // grid == member) & ((lane % grid).astype(F32) == chosen))
    half = members // 2
    for block in range(members // MB):
        x = x_ref[block * MB : (block + 1) * MB].reshape(MB * grid, hours).astype(BF)
        y = mm(select, x).astype(BF).reshape(regions, per, hours)
        core, inner = divmod(block, half // MB)
        send_ref[:, core, inner * per : (inner + 1) * per, :] = y
    raw_ref[...] = jnp.zeros_like(raw_ref)
    raw_ref[0 : idx_ref.shape[0], :] = idx_ref[...].astype(F32)
    raw_ref[8 : 8 + w_ref.shape[0], :] = w_ref[...]
    raw_ref[16:17, :] = cls_ref[...].astype(F32)
    raw_ref[24:25, 0 : outl_ref.shape[1]] = outl_ref[...].astype(F32)
    raw_ref[32:, :] = inc_ref[...].astype(F32)


def prep_kernel(
    slot, columns, core_ref, own_ref, other_ref, rate_ref, shape_ref,
    table_ref, mix_ref, pass_ref, cls_out_ref, wide_ref, link_ref, cls_target_ref, cls_own_ref,
):
    core = core_ref[0]
    class_count, hours = shape_ref.shape
    padded = table_ref.shape[1] // class_count
    kap = mix_ref.shape[2]
    recv = kap // MB
    per = MB * slot
    outs = own_ref.shape[0] - 32
    reaches = own_ref.shape[1]
    wide = MB * outs

    lag = iota((class_count, hours), 1).astype(F32)
    rate = rate_ref[...]
    hydro = (rate * shape_ref[...] * jnp.exp(-rate * lag)).astype(BF)
    reverse = one_hot((iota((hours, padded), 0) + iota((hours, padded), 1)) % padded == 0)
    turned = mm(hydro, reverse)
    early = iota((padded, padded), 0)
    late = iota((padded, padded), 1)
    for k in range(class_count):
        rolled = pltpu.roll(
            jnp.broadcast_to(turned[k : k + 1, :], (padded, padded)), 0, 1, stride=1, stride_axis=0
        )
        rolled = jnp.where(late <= early, rolled, 0.0)
        table_ref[:, k * padded : (k + 1) * padded] = rolled[:hours].astype(BF)

    row_p = iota((kap, recv), 0)
    expand = one_hot((row_p // per) * slot + row_p % slot == iota((kap, recv), 1))
    tile = one_hot(iota((reaches, wide), 0) == iota((reaches, wide), 1) % outs)
    member = (iota((kap, wide), 0) // slot) % MB
    lane_member = iota((kap, wide), 1) // outs

    def weights(raw):
        total = jnp.zeros((recv, reaches), F32)
        for j in range(columns):
            hit = iota((recv, reaches), 0).astype(F32) == raw[j : j + 1, :]
            total = total + jnp.where(hit, raw[8 + j : 9 + j, :], 0.0)
        return split(total)

    for level in range(2):
        mine = core == level
        raw = jnp.where(mine, own_ref[...], other_ref[...])
        outlet_lanes = mm(raw[24:32, :].astype(BF), tile)[0:1, :]
        pick = one_hot(iota((reaches, wide), 0).astype(F32) == outlet_lanes)
        for part, weight in enumerate(weights(raw)):
            spread = mm(expand, mm(weight, pick).astype(BF))
            mix_ref[level, part] = jnp.where(member == lane_member, spread, 0.0).astype(BF)
        moved = mm(raw[32:, :].astype(BF), pick)
        moved = jnp.concatenate([moved] * MB, axis=0)
        here = iota((wide, wide), 0) // outs == iota((wide, wide), 1) // outs
        pass_ref[level] = jnp.where(here, moved, 0.0).astype(BF)
        cls_out_ref[level] = mm(raw[16:24, :].astype(BF), pick)

    own = own_ref[...]
    for part, weight in enumerate(weights(own)):
        spread = mm(expand, weight)
        owner = (iota((kap, reaches), 0) // slot) % MB
        for m in range(MB):
            wide_ref[part, :, m * reaches : (m + 1) * reaches] = jnp.where(owner == m, spread, 0.0).astype(BF)
    links = own[32:, :].astype(BF)
    cls_own_ref[...] = own[16:24, :]
    target = lax.dot_general(
        own[16:24, :].astype(BF),
        jnp.concatenate([links] * MB, axis=0),
        (((1,), (1,)), ((), ())),
        preferred_element_type=F32,
    )
    cls_target_ref[...] = target
    group = link_ref.shape[0] // outs
    stacked = jnp.concatenate([own[32:, :]] * group, axis=0)
    owner = iota((group * outs, reaches), 0) // outs
    for m in range(group):
        link_ref[:, m * reaches : (m + 1) * reaches] = jnp.where(owner == m, stacked, 0.0).astype(BF)


def head_kernel(
    class_count, core_ref, rows_ref, table_ref, mix_ref, pass_ref, cls_ref,
    even_ref, odd_ref, panel_ref, own_ref, send_ref,
):
    core = core_ref[0]
    padded = table_ref.shape[1] // class_count
    regions, _, total, hours = rows_ref.shape
    blocks = even_ref.shape[0]
    per = total // blocks
    for block in range(blocks):
        rows = []
        lateral = []
        for level in range(2):
            one = rows_ref[:, level, block * per : (block + 1) * per, :].reshape(regions * per, hours)
            rows.append(one)
            lateral.append((tmm(one, mix_ref[level, 0]) + tmm(one, mix_ref[level, 1])).astype(BF))
        first = core == 0
        own_ref[block] = jnp.where(first, rows[0], rows[1])
        send_ref[block] = jnp.where(first, rows[1], rows[0])
        even = convolve(table_ref[...], lateral[0], cls_ref[0, 0:1, :], class_count, padded)
        odd = convolve(table_ref[...], lateral[1], cls_ref[1, 0:1, :], class_count, padded)
        even_ref[block] = even
        odd_ref[block] = odd
        inflow = mm(even.astype(BF), pass_ref[1]).astype(BF)
        panel = odd + convolve(table_ref[...], inflow, cls_ref[1, 0:1, :], class_count, padded)
        panel_ref[block] = panel.astype(BF)


def hop_kernel(
    class_count, core_ref, inflow_ref, table_ref, pass_ref, cls_ref, even_ref, odd_ref,
    panel_ref, own_ref, send_ref,
):
    core = core_ref[0]
    padded = table_ref.shape[1] // class_count
    for block in range(even_ref.shape[0]):
        arrived = inflow_ref[block]
        moved = mm(arrived, pass_ref[0]).astype(BF)
        even = even_ref[block] + convolve(table_ref[...], moved, cls_ref[0, 0:1, :], class_count, padded)
        even = even.astype(BF)
        first = core == 0
        own_ref[block] = jnp.where(first, arrived, even)
        send_ref[block] = jnp.where(first, even, arrived)
        if panel_ref is not None:
            moved = mm(even, pass_ref[1]).astype(BF)
            odd = odd_ref[block] + convolve(
                table_ref[...], moved, cls_ref[1, 0:1, :], class_count, padded
            )
            panel_ref[block] = odd.astype(BF)


def last_hop_kernel(
    class_count, core_ref, inflow_ref, table_ref, pass_ref, cls_ref, even_ref, own_ref, send_ref
):
    hop_kernel(
        class_count, core_ref, inflow_ref, table_ref, pass_ref, cls_ref, even_ref, None,
        None, own_ref, send_ref,
    )


def base_kernel(class_count, rows_ref, table_ref, wide_ref, cls_ref, base_ref):
    padded = table_ref.shape[1] // class_count
    reaches = cls_ref.shape[1]
    rows = rows_ref[0]
    classes = cls_ref[0:1, :]
    pair = max(1, 256 // reaches)
    width = pair * reaches
    classes = jnp.concatenate([classes] * pair, axis=1)
    for start in range(0, base_ref.shape[2], width):
        lateral = tmm(rows, wide_ref[0, :, start : start + width])
        lateral = lateral + tmm(rows, wide_ref[1, :, start : start + width])
        base_ref[0, :, start : start + width] = convolve(
            table_ref[...], lateral.astype(BF), classes, class_count, padded
        )


def final_kernel(class_count, place_ref, inflow_ref, base_ref, table_ref, link_ref, cls_ref, *rest):
    out_ref, scratch = rest[-2:]
    padded = table_ref.shape[1] // class_count
    blocks, hours, _ = inflow_ref.shape
    members = out_ref.shape[1]
    reaches = out_ref.shape[2]
    lanes, width = link_ref.shape
    links = jnp.concatenate([link_ref[...]] * 2, axis=0)
    for block in range(blocks):
        routed = convolve(table_ref[...], inflow_ref[block], cls_ref[0:1, :], class_count, padded)
        high, low = split(routed)
        for part in range(routed.shape[1] // lanes):
            cut = slice(part * lanes, (part + 1) * lanes)
            spread = mm(jnp.concatenate([high[:, cut], low[:, cut]], axis=1), links)
            total = spread + base_ref[block, :, part * width : (part + 1) * width]
            for j in range(width // reaches):
                member = block * MB + part * (width // reaches) + j
                scratch[pl.ds(member, hours, stride=members), :] = total[
                    :, j * reaches : (j + 1) * reaches
                ]
    out_ref[...] = scratch[...].reshape(hours, members, reaches).astype(BF)


def local(
    runoff, send_rows, remap_index, remap_weight, class_id, kernel_shape, kernel_rate, outlets, incidence
):
    hours, members, grid = runoff.shape
    regions = lax.axis_size("region")
    pairs = lax.axis_size("pair")
    class_count = kernel_shape.shape[0]
    reaches, columns = remap_index.shape
    recv = send_rows.size
    slot = recv // regions
    outs = outlets.size
    half = members // 2
    blocks = half // MB
    padded = -(-hours // LANES) * LANES
    per = MB * slot
    kap = regions * per
    wide = MB * outs
    group = max(1, LANES // outs)
    core = lax.axis_index("core").astype(jnp.int32)
    core_arg = core.reshape(1)
    swap = [(0, 1), (1, 0)]

    def struct(shape, dtype):
        return jax.ShapeDtypeStruct(shape, dtype)

    send, raw = call(
        functools.partial(pack_kernel, slot),
        (struct((regions, 2, blocks * per, hours), BF), struct((32 + outs, reaches), F32)),
        2 * kap * MB * grid * hours * blocks * 2,
        in_specs=vmem(7),
        out_specs=tuple(vmem(2)),
    )(
        jnp.transpose(runoff, (1, 2, 0)),
        send_rows.reshape(1, recv),
        remap_index.T,
        remap_weight.T,
        class_id.T,
        outlets.reshape(1, outs),
        incidence.reshape(outs, reaches),
    )
    received = lax.all_to_all(
        send.reshape(regions * 2, blocks * per, hours), ("region", "core"), 0, 0
    ).reshape(regions, 2, blocks * per, hours)
    other = lax.ppermute(raw, "core", swap)
    table, mix, passing, cls_out, wide_mix, link, cls_target, cls_own = call(
        functools.partial(prep_kernel, slot, columns),
        (
            struct((hours, class_count * padded), BF),
            struct((2, 2, kap, wide), BF),
            struct((2, wide, wide), BF),
            struct((2, 8, wide), F32),
            struct((2, kap, MB * reaches), BF),
            struct((group * outs, group * reaches), BF),
            struct((8, wide), F32),
            struct((8, reaches), F32),
        ),
        10_000_000,
        in_specs=[SCALAR] + vmem(4),
        out_specs=tuple(vmem(8)),
    )(core_arg, raw, other, kernel_rate.reshape(class_count, 1), kernel_shape)

    conv_flops = 2 * hours * class_count * padded * wide
    panel_shape = struct((blocks, hours, wide), BF)
    even, odd, panel, rows_own, rows_send = call(
        functools.partial(head_kernel, class_count),
        (
            struct((blocks, hours, wide), F32),
            struct((blocks, hours, wide), F32),
            panel_shape,
            struct((blocks, kap, hours), BF),
            struct((blocks, kap, hours), BF),
        ),
        3 * blocks * conv_flops,
        in_specs=[SCALAR] + vmem(5),
        out_specs=tuple(vmem(5)),
    )(core_arg, received, table, mix, passing, cls_out)

    inflow = jnp.zeros(panel_shape.shape, BF)
    own = given = None
    for step in range(pairs - 1):
        arrived = lax.ppermute(panel, "pair", [(step, step + 1)])
        inflow = arrived if step == 0 else inflow + arrived
        if step < pairs - 2:
            panel, own, given = call(
                functools.partial(hop_kernel, class_count),
                (panel_shape, panel_shape, panel_shape),
                2 * blocks * conv_flops,
                in_specs=[SCALAR] + vmem(6),
                out_specs=tuple(vmem(3)),
            )(core_arg, inflow, table, passing, cls_out, even, odd)
    if pairs == 1:
        inflow = jnp.zeros(panel_shape.shape, BF)
    rows_other = lax.ppermute(rows_send, "core", swap)

    def base(rows):
        return call(
            functools.partial(base_kernel, class_count),
            struct((blocks, hours, MB * reaches), F32),
            blocks * conv_flops * reaches // outs,
            grid=(blocks,),
            in_specs=[pl.BlockSpec((1, kap, hours), lambda b: (b, 0, 0))] + vmem(3),
            out_specs=pl.BlockSpec((1, hours, MB * reaches), lambda b: (b, 0, 0)),
        )(rows, table, wide_mix, cls_own)

    base_own = base(rows_own)
    base_other = base(rows_other)
    own, given = call(
        functools.partial(last_hop_kernel, class_count),
        (panel_shape, panel_shape),
        blocks * conv_flops,
        in_specs=[SCALAR] + vmem(5),
        out_specs=tuple(vmem(2)),
    )(core_arg, inflow, table, passing, cls_out, even)
    gotten = lax.ppermute(given, "core", swap)

    def final(place, panel_rows, base_flow, before):
        extra = [] if before is None else [before]
        return pl.pallas_call(
            functools.partial(final_kernel, class_count),
            out_shape=struct((hours, members, reaches), BF),
            grid_spec=pltpu.PrefetchScalarGridSpec(
                num_scalar_prefetch=1,
                grid=(1,),
                in_specs=vmem(5) + [pl.BlockSpec(memory_space=pl.ANY)] * len(extra),
                out_specs=pl.BlockSpec((hours, half, reaches), lambda g, place: (0, place[0], 0)),
                scratch_shapes=[pltpu.VMEM((hours * half, reaches), F32)],
            ),
            input_output_aliases={6: 0} if extra else {},
            compiler_params=pltpu.CompilerParams(vmem_limit_bytes=VMEM_LIMIT),
            cost_estimate=pl.CostEstimate(
                flops=2 * blocks * conv_flops, bytes_accessed=6_000_000, transcendentals=0
            ),
        )(place, panel_rows, base_flow, table, link, cls_target, *extra)

    out = final(core_arg, own, base_own, None)
    return final(1 - core_arg, gotten, base_other, out)


def solution(mesh):
    regions, orders = mesh.shape["region"], mesh.shape["order"]
    split_mesh = Mesh(mesh.devices.reshape(regions, orders // 2, 2), ("region", "pair", "core"))
    order = ("pair", "core")
    every = ("region", "pair", "core")
    return jax.shard_map(
        local,
        mesh=split_mesh,
        in_specs=(
            P(None, None, every),
            P("region", order, None),
            P(every, None),
            P(every, None),
            P(every, None),
            P(),
            P(),
            P("region", order, None),
            P("region", order, None, None),
        ),
        out_specs=P(None, None, every),
        check_vma=False,
    )
```

time: 253 us -> 61.8 us (0.24)
  local copies, waits for them, and re-layouts: 174 us -> 4.15 us
  Pallas kernels: 0 us -> 35.6 us
  matrix products: 32.9 us -> 0 us
  starting transfers between devices: 19.6 us -> 11.5 us
  other arithmetic: 7.97 us -> 0 us
  waiting for transfers between devices: 16.3 us -> 9.6 us
    gather x6 -> x0, local copies, waits for them, and re-layouts: 142 us -> none  [the longest x2 126 us: toeplitz_table(): lagged = jnp.take(kernel, jnp.clip(steps_apart, 0, hour_count - 1), axis=1)]
    pallas_call x0 -> x8, Pallas kernels: none -> 35.6 us  [the longest x2 12.2 us: base(): call(functools.partial(base_kernel, class_count), struct((blocks, hours,...]
    dot_general x11 -> x0, matrix products: 32.9 us -> none  [the longest x1 9.39 us: local(): jnp.einsum('tmr,rs->tms', received, slot_weights, precision=lax.Precision...]
    ppermute x3 -> x4, waiting for transfers between devices: 16.3 us -> 0.59 us  [the longest x1 0.58 us: local(): other = lax.ppermute(raw, 'core', swap)]
    ppermute x3 -> x4, starting transfers between devices: 13.2 us -> 4.18 us  [the longest x1 3.15 us: local(): arrived = lax.ppermute(panel, 'pair', [(step, step + 1)])]
    all_to_all x1, waiting for transfers between devices: 0.01 us -> 9.01 us  [local(): lax.all_to_all(send.reshape(regions * 2, blocks * per, hours), ('region',...]
    convert_element_type x2 -> x0, local copies, waits for them, and re-layouts: 7.57 us -> none  [the longest x1 7.42 us: local(): slotted = jnp.einsum('tmr,rs->tms', received, slot_weights, precision=lax...]
    reshape x1, local copies, waits for them, and re-layouts: 8.09 us -> 0.67 us  [local(): kernel_rate.reshape(class_count, 1)]
  transfers between devices with their start and end apart: 4 -> 5, of which waited for: 3 -> 2; matrix products, arithmetic and copies ran while one was open for 51% -> 1% of each run, Pallas kernels for 0% -> 38%
where the time goes in v1:
time: 61.8 us; the launch traced here: 60.9 us
  Pallas kernels  35.6 us (58%)
  starting transfers between devices  11.5 us (19%)
  waiting for transfers between devices  9.6 us (16%)
  local copies, waits for them, and re-layouts  4.15 us (7%)
    pallas_call x2, Pallas kernels, base(): call(functools.partial(base_kernel, class_count), struct((blocks, hours,...  12.2 us
    pallas_call x2, Pallas kernels, final(): pl.pallas_call(functools.partial(final_kernel, class_count), out_shape=st...  10 us
    all_to_all x1, waiting for transfers between devices, local(): lax.all_to_all(send.reshape(regions * 2, blocks * per, hours), ('region',...  9.01 us
    all_to_all x1, starting transfers between devices, local(): lax.all_to_all(send.reshape(regions * 2, blocks * per, hours), ('region',...  7.32 us
    pallas_call x1, Pallas kernels, local(): call(functools.partial(head_kernel, class_count), (struct((blocks, hours,...  4.79 us
    unnamed x12, local copies, waits for them, and re-layouts  3.48 us
    pallas_call x1, Pallas kernels, local(): call(functools.partial(last_hop_kernel, class_count), (panel_shape, panel...  3.15 us
    ppermute x1, starting transfers between devices, local(): arrived = lax.ppermute(panel, 'pair', [(step, step + 1)])  3.15 us
  transfers between devices with their start and end apart: 5, of which 2 were waited for; matrix products, arithmetic and copies ran while one was open for 1% of the time, Pallas kernels for 38%

profile of v1, /device:TPU:1, one launch (start us, length us, event | category | flops | bytes accessed | tf_op | source)
XLA Modules:
  0.0 60.9 jit_solution(14540536536117173165)
XLA Ops:
  0.0 0.0 copy-start.4
  0.0 2.4 %shard_map.91 = (bf16[8,2,64,240]{3,2,1,0:T(8,128)(2,1)}, f32[64,128]{1,0:T(8,128)}) custom-call(f32[32,32,240]{2,1,0:T(8,128)} %bitcast.11, s32[1,32]{1,0:T(1,128)} %bitcast.17, s32[4,128]{1,0:T(4,128)} %bitcast.15, f32[4,128]{1,0:T(4,128)} %bitcast.16, s32[1,128]{1,0:T(1,128)} %bitcast.18, s32[1,32]{1,0:T(1,128)} %bitcast.19, s32[32,128]{1,0:T(8,128)} %bitcast.14), custom_call_target="tpu_custom_call" | custom-call | flops 125829120 | bytes 1048576 | tf_op jit(solution)/shard_map/pallas_call | solution.py:290
  2.4 7.3 %all-to-all-start = ((bf16[16,64,240]{2,1,0:T(8,128)(2,1)}), bf16[16,64,240]{2,1,0:T(8,128)(2,1)S(1)}, u32[]{:S(2)}, u32[]{:S(2)}) async-start(bf16[16,64,240]{2,1,0:T(8,128)(2,1)} %bitcast.13), calls=%async_computation | async-start | bytes 1048576 | tf_op jit(solution)/shard_map/all_to_all | solution.py:305
  9.8 0.2 collective-permute-start
  9.9 0.0 copy-done.4
  9.9 0.7 %copy.11.rate_ref = f32[8,1]{1,0:T(8,128)} copy(f32[8,1]{0,1:T(1,128)S(1)} %bitcast.20) | data formatting | bytes 64 | tf_op jit(solution)/shard_map/reshape | solution.py:324
  10.6 0.6 collective-permute-done.other_ref
  11.2 0.0 copy-start.3
  11.2 0.6 copy-done.3
  11.8 3.0 %shard_map.92 = (bf16[240,2048]{1,0:T(8,128)(2,1)}, bf16[2,2,256,256]{3,2,1,0:T(8,128)(2,1)}, bf16[2,256,256]{2,1,0:T(8,128)(2,1)}, f32[2,8,256]{2,1,0:T(8,128)}...) custom-call(s32[1]{0:T(128)} %bitcast.core_ref.place_ref, ...), custom_call_target="tpu_custom_call" | custom-call | flops 10000000 | bytes 5955584 | tf_op jit(solution)/shard_map/pallas_call | solution.py:309
  14.8 9.0 %all-to-all-done = bf16[16,64,240]{2,1,0:T(8,128)(2,1)S(1)} async-done(((bf16[16,64,240]{2,1,0:T(8,128)(2,1)}), bf16[16,64,240]{2,1,0:T(8,128)(2,1)S(1)}, u32[]{:S(2)}, u32[]{:S(2)}) %all-to-all-start) | async-done | bytes 491552 | tf_op jit(solution)/shard_map/all_to_all | solution.py:305
  23.8 0.0 copy-start
  23.8 0.8 %copy-done = bf16[16,64,240]{2,1,0:T(8,128)(2,1)} copy-done((bf16[16,64,240]{2,1,0:T(8,128)(2,1)}, bf16[16,64,240]{2,1,0:T(8,128)(2,1)S(1)}, u32[]{:S(2)}) %copy-start) | copy-done | bytes 491544
  24.6 4.8 %shard_map.93 = (f32[2,240,256]{2,1,0:T(8,128)}, f32[2,240,256]{2,1,0:T(8,128)}, bf16[2,240,256]{2,1,0:T(8,128)(2,1)}, bf16[2,256,240]{2,1,0:T(8,128)(2,1)}, bf16[2,256,240]{2,1,0:T(8,128)(2,1)}) custom-call(s32[1]{0:T(128)} %bitcast.core_ref.place_ref, bf16[8,2,64,240]{3,2,1,0:T(8,128)(2,1)} %bitcast.12, bf16[240,2048]{1,0:T(8,128)(2,1)} %get-tuple-element.23.table_ref, ...), custom_call_target="tpu_custom_call" | custom-call | flops 1509949440 | bytes 3440640 | tf_op jit(solution)/shard_map/pallas_call | solution.py:328
  29.4 3.1 %collective-permute-start.1 = (bf16[2,240,256]{2,1,0:T(8,128)(2,1)}, bf16[2,240,256]{2,1,0:T(8,128)(2,1)S(1)}, u32[]{:S(2)}, u32[]{:S(2)}) collective-permute-start(bf16[2,240,256]{2,1,0:T(8,128)(2,1)} %get-tuple-element.27), channel_id=1, source_target_pairs={{0,2},{1,3},{4,6},{5,7},{8,10},{9,11},{12,14},{13,15},{16,18},{17,... | collective-permute-start | bytes 737288 | tf_op jit(solution)/shard_map/ppermute | solution.py:345
  32.6 0.8 %collective-permute-start.3 = (bf16[2,256,240]{2,1,0:T(8,128)(2,1)}, bf16[2,256,240]{2,1,0:T(8,128)(2,1)S(1)}, u32[]{:S(2)}, u32[]{:S(2)}) collective-permute-start(bf16[2,256,240]{2,1,0:T(8,128)(2,1)} %get-tuple-element.30), channel_id=1, source_target_pairs={{0,1},{1,0},{2,3},{3,2},{4,5},{5,4},{6,7},{7,6},{8,9},{9,8},{10,11... | collective-permute-start | bytes 737288 | tf_op jit(solution)/shard_map/ppermute | solution.py:357
  33.4 6.1 %shard_map.96.base_ref = f32[2,240,1024]{2,1,0:T(8,128)} custom-call(bf16[2,256,240]{2,1,0:T(8,128)(2,1)} %get-tuple-element.36.rows_ref, bf16[240,2048]{1,0:T(8,128)(2,1)} %get-tuple-element.23.table_ref, bf16[2,256,1024]{2,1,0:T(8,128)(2,1)} %get-tuple-element.31.wide_ref, f32[8,128]{1,0:T(8,128)} %get-tuple-element.32.cls_ref), custom_call_target="tpu_custom_call" | custom-call | flops 2013265920 | bytes 3932160 | tf_op jit(solution)/shard_map/pallas_call | solution.py:360
  39.5 0.0 collective-permute-done.1.inflow_ref
  39.5 0.0 copy-start.2
  39.5 0.7 %copy-done.2 = bf16[2,240,256]{2,1,0:T(8,128)(2,1)} copy-done((bf16[2,240,256]{2,1,0:T(8,128)(2,1)}, bf16[2,240,256]{2,1,0:T(8,128)(2,1)S(1)}, u32[]{:S(2)}) %copy-start.2) | copy-done | bytes 245784
  40.2 3.2 %shard_map.94 = (bf16[2,240,256]{2,1,0:T(8,128)(2,1)}, bf16[2,240,256]{2,1,0:T(8,128)(2,1)}) custom-call(s32[1]{0:T(128)} %bitcast.core_ref.place_ref, bf16[2,240,256]{2,1,0:T(8,128)(2,1)} %copy-done.2, bf16[240,2048]{1,0:T(8,128)(2,1)} %get-tuple-element.23.table_ref, bf16[2,256,256]{2,1,0:T(8,128)(2,1)} %get-tuple-element.25.pass_ref, ...), custom_call_target="tpu_custom_call" | custom-call | flops 503316480 | bytes 983040 | tf_op jit(solution)/shard_map/pallas_call | solution.py:371
  43.4 0.0 collective-permute-start.2
  43.4 5.0 %shard_map.97.rest_0_ = bf16[240,32,128]{2,1,0:T(8,128)(2,1)} custom-call(s32[1]{0:T(128)} %bitcast.core_ref.place_ref, bf16[2,240,256]{2,1,0:T(8,128)(2,1)} %get-tuple-element.35.inflow_ref, f32[2,240,1024]{2,1,0:T(8,128)} %shard_map.96.base_ref, bf16[240,2048]{1,0:T(8,128)(2,1)} %get-tuple-element.23.table_ref, ...), custom_call_target="tpu_custom_call" | custom-call | flops 1006632960 | bytes 6000000 | tf_op jit(solution)/shard_map/pallas_call | solution.py:382
  48.4 0.0 collective-permute-done.3.rows_ref
  48.4 0.0 copy-start.5
  48.4 0.7 %copy-done.5 = bf16[2,256,240]{2,1,0:T(8,128)(2,1)} copy-done((bf16[2,256,240]{2,1,0:T(8,128)(2,1)}, bf16[2,256,240]{2,1,0:T(8,128)(2,1)S(1)}, u32[]{:S(2)}) %copy-start.5) | copy-done | bytes 245784
  49.1 6.1 %shard_map.95.base_ref = f32[2,240,1024]{2,1,0:T(8,128)} custom-call(bf16[2,256,240]{2,1,0:T(8,128)(2,1)} %copy-done.5, bf16[240,2048]{1,0:T(8,128)(2,1)} %get-tuple-element.23.table_ref, bf16[2,256,1024]{2,1,0:T(8,128)(2,1)} %get-tuple-element.31.wide_ref, f32[8,128]{1,0:T(8,128)} %get-tuple-element.32.cls_ref), custom_call_target="tpu_custom_call" | custom-call | flops 2013265920 | bytes 3932160 | tf_op jit(solution)/shard_map/pallas_call | solution.py:360
  55.2 0.0 collective-permute-done.2.inflow_ref
  55.2 0.0 copy-start.1
  55.2 0.7 %copy-done.1 = bf16[2,240,256]{2,1,0:T(8,128)(2,1)} copy-done((bf16[2,240,256]{2,1,0:T(8,128)(2,1)}, bf16[2,240,256]{2,1,0:T(8,128)(2,1)S(1)}, u32[]{:S(2)}) %copy-start.1) | copy-done | bytes 245784
  55.9 5.0 %shard_map.98 = bf16[240,32,128]{2,1,0:T(8,128)(2,1)} custom-call(s32[1]{0:T(128)S(6)} %sub.3.place_ref, bf16[2,240,256]{2,1,0:T(8,128)(2,1)} %copy-done.1, f32[2,240,1024]{2,1,0:T(8,128)} %shard_map.95.base_ref, bf16[240,2048]{1,0:T(8,128)(2,1)} %get-tuple-element.23.table_ref, ...), custom_call_target="tpu_custom_call", output_to_operand_aliasing={{}: (6, {})} | custom-call | flops 1006632960 | bytes 6000000 | tf_op jit(solution)/shard_map/pallas_call | solution.py:382
Async XLA Ops:
  0.0 9.9 %copy-start.4 = (f32[8]{0:T(128)S(1)}, f32[8]{0:T(128)}, u32[]{:S(2)}) copy-start(f32[8]{0:T(128)} %param.15) | copy-start | bytes 100
  2.4 21.4 %all-to-all-start = ((bf16[16,64,240]{2,1,0:T(8,128)(2,1)}), bf16[16,64,240]{2,1,0:T(8,128)(2,1)S(1)}, u32[]{:S(2)}, u32[]{:S(2)}) async-start(bf16[16,64,240]{2,1,0:T(8,128)(2,1)} %bitcast.13), calls=%async_computation | async-start | bytes 1048576 | tf_op jit(solution)/shard_map/all_to_all | solution.py:305
  9.8 1.4 %collective-permute-start = (f32[64,128]{1,0:T(8,128)}, f32[64,128]{1,0:T(8,128)S(1)}, u32[]{:S(2)}, u32[]{:S(2)}) collective-permute-start(f32[64,128]{1,0:T(8,128)} %get-tuple-element.22.own_ref), channel_id=1, source_target_pairs={{0,1},{1,0},{2,3},{3,2},{4,5},{5,4},{6,7},{7,6},{8,9},{9,8},{10,11... | collective-permute-start | bytes 98312 | tf_op jit(solution)/shard_map/ppermute | solution.py:308
  11.2 0.6 copy-start.3
  23.8 0.8 %copy-start = (bf16[16,64,240]{2,1,0:T(8,128)(2,1)}, bf16[16,64,240]{2,1,0:T(8,128)(2,1)S(1)}, u32[]{:S(2)}) copy-start(bf16[16,64,240]{2,1,0:T(8,128)(2,1)S(1)} %all-to-all-done) | copy-start | bytes 1474564
  29.4 10.1 %collective-permute-start.1 = (bf16[2,240,256]{2,1,0:T(8,128)(2,1)}, bf16[2,240,256]{2,1,0:T(8,128)(2,1)S(1)}, u32[]{:S(2)}, u32[]{:S(2)}) collective-permute-start(bf16[2,240,256]{2,1,0:T(8,128)(2,1)} %get-tuple-element.27), channel_id=1, source_target_pairs={{0,2},{1,3},{4,6},{5,7},{8,10},{9,11},{12,14},{13,15},{16,18},{17,... | collective-permute-start | bytes 737288 | tf_op jit(solution)/shard_map/ppermute | solution.py:345
  32.6 15.8 %collective-permute-start.3 = (bf16[2,256,240]{2,1,0:T(8,128)(2,1)}, bf16[2,256,240]{2,1,0:T(8,128)(2,1)S(1)}, u32[]{:S(2)}, u32[]{:S(2)}) collective-permute-start(bf16[2,256,240]{2,1,0:T(8,128)(2,1)} %get-tuple-element.30), channel_id=1, source_target_pairs={{0,1},{1,0},{2,3},{3,2},{4,5},{5,4},{6,7},{7,6},{8,9},{9,8},{10,11... | collective-permute-start | bytes 737288 | tf_op jit(solution)/shard_map/ppermute | solution.py:357
  39.5 0.7 %copy-start.2 = (bf16[2,240,256]{2,1,0:T(8,128)(2,1)}, bf16[2,240,256]{2,1,0:T(8,128)(2,1)S(1)}, u32[]{:S(2)}) copy-start(bf16[2,240,256]{2,1,0:T(8,128)(2,1)S(1)} %collective-permute-done.1.inflow_ref) | copy-start | bytes 737284
  43.4 11.8 %collective-permute-start.2 = (bf16[2,240,256]{2,1,0:T(8,128)(2,1)}, bf16[2,240,256]{2,1,0:T(8,128)(2,1)S(1)}, u32[]{:S(2)}, u32[]{:S(2)}) collective-permute-start(bf16[2,240,256]{2,1,0:T(8,128)(2,1)} %get-tuple-element.29), channel_id=1, source_target_pairs={{0,1},{1,0},{2,3},{3,2},{4,5},{5,4},{6,7},{7,6},{8,9},{9,8},{10,11... | collective-permute-start | bytes 737288 | tf_op jit(solution)/shard_map/ppermute | solution.py:378
  48.4 0.7 %copy-start.5 = (bf16[2,256,240]{2,1,0:T(8,128)(2,1)}, bf16[2,256,240]{2,1,0:T(8,128)(2,1)S(1)}, u32[]{:S(2)}) copy-start(bf16[2,256,240]{2,1,0:T(8,128)(2,1)S(1)} %collective-permute-done.3.rows_ref) | copy-start | bytes 737284
  55.2 0.7 %copy-start.1 = (bf16[2,240,256]{2,1,0:T(8,128)(2,1)}, bf16[2,240,256]{2,1,0:T(8,128)(2,1)S(1)}, u32[]{:S(2)}) copy-start(bf16[2,240,256]{2,1,0:T(8,128)(2,1)S(1)} %collective-permute-done.2.inflow_ref) | copy-start | bytes 737284

commit v2 on v1

--- a/solution.py
+++ b/solution.py
@@ -10,7 +10,8 @@
 F32 = jnp.float32
 MB = 8
 LANES = 128
-VMEM_LIMIT = 56 * 1024 * 1024
+VMEM_LIMIT = 20 * 1024 * 1024
+WHOLE_VMEM = 56 * 1024 * 1024
 
 
 def iota(shape, dim):
@@ -34,12 +35,12 @@
     return high, (value - high.astype(F32)).astype(BF)
 
 
-def call(kernel, out_shape, flops, **extra):
+def call(kernel, out_shape, flops, limit=VMEM_LIMIT, **extra):
     nbytes = sum(s.size * s.dtype.itemsize for s in jax.tree.leaves(out_shape))
     return pl.pallas_call(
         kernel,
         out_shape=out_shape,
-        compiler_params=pltpu.CompilerParams(vmem_limit_bytes=VMEM_LIMIT),
+        compiler_params=pltpu.CompilerParams(vmem_limit_bytes=limit),
         cost_estimate=pl.CostEstimate(flops=flops, bytes_accessed=2 * nbytes, transcendentals=0),
         **extra,
     )
@@ -102,7 +103,8 @@
     wide = MB * outs
 
     lag = iota((class_count, hours), 1).astype(F32)
-    rate = rate_ref[...]
+    rate = jnp.where(iota((class_count, class_count), 0) == iota((class_count, class_count), 1), rate_ref[...], 0.0)
+    rate = jnp.sum(rate, axis=1, keepdims=True)
     hydro = (rate * shape_ref[...] * jnp.exp(-rate * lag)).astype(BF)
     reverse = one_hot((iota((hours, padded), 0) + iota((hours, padded), 1)) % padded == 0)
     turned = mm(hydro, reverse)
@@ -291,6 +293,7 @@
         functools.partial(pack_kernel, slot),
         (struct((regions, 2, blocks * per, hours), BF), struct((32 + outs, reaches), F32)),
         2 * kap * MB * grid * hours * blocks * 2,
+        limit=WHOLE_VMEM,
         in_specs=vmem(7),
         out_specs=tuple(vmem(2)),
     )(
@@ -321,7 +324,7 @@
         10_000_000,
         in_specs=[SCALAR] + vmem(4),
         out_specs=tuple(vmem(8)),
-    )(core_arg, raw, other, kernel_rate.reshape(class_count, 1), kernel_shape)
+    )(core_arg, raw, other, kernel_rate.reshape(1, class_count), kernel_shape)
 
     conv_flops = 2 * hours * class_count * padded * wide
     panel_shape = struct((blocks, hours, wide), BF)

time: 61.8 us -> 47.3 us (0.77)
  Pallas kernels: 35.6 us -> 20.5 us
  local copies, waits for them, and re-layouts: 4.15 us -> 0.77 us
  waiting for transfers between devices: 9.6 us -> 12.5 us
  starting transfers between devices: 11.5 us -> 12.9 us
    pallas_call x2, Pallas kernels: 12.2 us -> 6.98 us  [base(): call(functools.partial(base_kernel, class_count), struct((blocks, hours,...]
    pallas_call x2, Pallas kernels: 10 us -> 6.2 us  [final(): pl.pallas_call(functools.partial(final_kernel, class_count), out_shape=st...]
    unnamed x12 -> x6, local copies, waits for them, and re-layouts: 3.48 us -> 0.77 us
    pallas_call x1, Pallas kernels: 3.15 us -> 0.87 us  [local(): call(functools.partial(last_hop_kernel, class_count), (panel_shape, panel...]
    pallas_call x1, Pallas kernels: 3.05 us -> 1.05 us  [local(): call(functools.partial(prep_kernel, slot, columns), (struct((hours, class...]
    pallas_call x1, Pallas kernels: 4.79 us -> 2.92 us  [local(): call(functools.partial(head_kernel, class_count), (struct((blocks, hours,...]
    all_to_all x1, waiting for transfers between devices: 9.01 us -> 10.8 us  [local(): lax.all_to_all(send.reshape(regions * 2, blocks * per, hours), ('region',...]
    ppermute x1, starting transfers between devices: 0.03 us -> 1.4 us  [local(): gotten = lax.ppermute(given, 'core', swap)]
  transfers between devices with their start and end apart: 5 -> 5, of which waited for: 2 -> 3; matrix products, arithmetic and copies ran while one was open for 1% -> 0% of each run, Pallas kernels for 38% -> 26%
where the time goes in v2:
time: 47.3 us; the launch traced here: 46.7 us
  Pallas kernels  20.5 us (43%)
  starting transfers between devices  12.9 us (27%)
  waiting for transfers between devices  12.5 us (26%)
  local copies, waits for them, and re-layouts  0.77 us (2%)
    all_to_all x1, waiting for transfers between devices, local(): lax.all_to_all(send.reshape(regions * 2, blocks * per, hours), ('region',...  10.8 us
    all_to_all x1, starting transfers between devices, local(): lax.all_to_all(send.reshape(regions * 2, blocks * per, hours), ('region',...  7.32 us
    pallas_call x2, Pallas kernels, base(): call(functools.partial(base_kernel, class_count), struct((blocks, hours,...  6.98 us
    pallas_call x2, Pallas kernels, final(): pl.pallas_call(functools.partial(final_kernel, class_count), out_shape=st...  6.2 us
    ppermute x1, starting transfers between devices, local(): arrived = lax.ppermute(panel, 'pair', [(step, step + 1)])  3.15 us
    pallas_call x1, Pallas kernels, local(): call(functools.partial(head_kernel, class_count), (struct((blocks, hours,...  2.92 us
    pallas_call x1, Pallas kernels, local(): call(functools.partial(pack_kernel, slot), (struct((regions, 2, blocks *...  2.46 us
    ppermute x1, starting transfers between devices, local(): gotten = lax.ppermute(given, 'core', swap)  1.4 us
  transfers between devices with their start and end apart: 5, of which 3 were waited for; matrix products, arithmetic and copies ran while one was open for 0% of the time, Pallas kernels for 26%

profile of v2, /device:TPU:1, one launch (start us, length us, event | category | flops | bytes accessed | tf_op | source)
XLA Modules:
  0.0 46.7 jit_solution(6744079691972039096)
XLA Ops:
  0.0 0.0 copy-start.2
  0.0 0.0 copy-start.1
  0.0 2.5 %shard_map.91 = (bf16[8,2,64,240]{3,2,1,0:T(8,128)(2,1)}, f32[64,128]{1,0:T(8,128)}) custom-call(f32[32,32,240]{2,1,0:T(8,128)} %bitcast.13, s32[1,32]{1,0:T(1,128)} %bitcast.18, s32[4,128]{1,0:T(4,128)} %bitcast.16, f32[4,128]{1,0:T(4,128)} %bitcast.17, s32[1,128]{1,0:T(1,128)} %bitcast.19, s32[1,32]{1,0:T(1,128)} %bitcast.20, s32[32,128]{1,0:T(8,128)} %bitcast.15), custom_call_target="tpu_custom_call" | custom-call | flops 125829120 | bytes 1048576 | tf_op jit(solution)/shard_map/pallas_call | solution.py:292
  2.5 7.3 %all-to-all-start = ((bf16[16,64,240]{2,1,0:T(8,128)(2,1)}), bf16[16,64,240]{2,1,0:T(8,128)(2,1)S(1)}, u32[]{:S(2)}, u32[]{:S(2)}) async-start(bf16[16,64,240]{2,1,0:T(8,128)(2,1)} %bitcast.14), calls=%async_computation | async-start | bytes 1048576 | tf_op jit(solution)/shard_map/all_to_all | solution.py:308
  9.8 0.2 collective-permute-start
  10.0 1.3 %collective-permute-done.other_ref = f32[64,128]{1,0:T(8,128)S(1)} collective-permute-done((f32[64,128]{1,0:T(8,128)}, f32[64,128]{1,0:T(8,128)S(1)}, u32[]{:S(2)}, u32[]{:S(2)}) %collective-permute-start) | collective-permute-done | bytes 32800 | tf_op jit(solution)/shard_map/ppermute | solution.py:311
  11.2 0.0 copy-done.2
  11.2 0.0 copy-done.1
  11.2 0.0 copy-start
  11.2 0.8 %copy-done = f32[64,128]{1,0:T(8,128)S(1)} copy-done((f32[64,128]{1,0:T(8,128)S(1)}, f32[64,128]{1,0:T(8,128)}, u32[]{:S(2)}) %copy-start) | copy-done | bytes 32792
  12.0 1.1 %shard_map.92 = (bf16[240,2048]{1,0:T(8,128)(2,1)S(1)}, bf16[2,2,256,256]{3,2,1,0:T(8,128)(2,1)S(1)}, bf16[2,256,256]{2,1,0:T(8,128)(2,1)S(1)}, f32[2,8,256]{2,1...) custom-call(s32[1]{0:T(128)} %bitcast.core_ref.place_ref, ...), custom_call_target="tpu_custom_call" | custom-call | flops 10000000 | bytes 5955584 | tf_op jit(solution)/shard_map/pallas_call | solution.py:312
  13.0 10.8 %all-to-all-done = bf16[16,64,240]{2,1,0:T(8,128)(2,1)S(1)} async-done(((bf16[16,64,240]{2,1,0:T(8,128)(2,1)}), bf16[16,64,240]{2,1,0:T(8,128)(2,1)S(1)}, u32[]{:S(2)}, u32[]{:S(2)}) %all-to-all-start) | async-done | bytes 491552 | tf_op jit(solution)/shard_map/all_to_all | solution.py:308
  23.9 2.9 %shard_map.93 = (f32[2,240,256]{2,1,0:T(8,128)S(1)}, f32[2,240,256]{2,1,0:T(8,128)}, bf16[2,240,256]{2,1,0:T(8,128)(2,1)S(1)}, bf16[2,256,240]{2,1,0:T(8,128)(2,1)S(1)}, bf16[2,256,240]{2,1,0:T(8,128)(2,1)S(1)}) custom-call(s32[1]{0:T(128)} %bitcast.core_ref.place_ref, bf16[8,2,64,240]{3,2,1,0:T(8,128)(2,1)S(1)} %bitcast.11, ...), custom_call_target="tpu_custom_call" | custom-call | flops 1509949440 | bytes 3440640 | tf_op jit(solution)/shard_map/pallas_call | solution.py:331
  26.8 3.1 %collective-permute-start.1 = (bf16[2,240,256]{2,1,0:T(8,128)(2,1)S(1)}, bf16[2,240,256]{2,1,0:T(8,128)(2,1)S(1)}, u32[]{:S(2)}, u32[]{:S(2)}) collective-permute-start(bf16[2,240,256]{2,1,0:T(8,128)(2,1)S(1)} %get-tuple-element.27), channel_id=1, source_target_pairs={{0,2},{1,3},{4,6},{5,7},{8,10},{9,11},{12,14},{13,15},{16,18},{17,... | collective-permute-start | bytes 737288 | tf_op jit(solution)/shard_map/ppermute | solution.py:348
  29.9 0.8 %collective-permute-start.3 = (bf16[2,256,240]{2,1,0:T(8,128)(2,1)S(1)}, bf16[2,256,240]{2,1,0:T(8,128)(2,1)S(1)}, u32[]{:S(2)}, u32[]{:S(2)}) collective-permute-start(bf16[2,256,240]{2,1,0:T(8,128)(2,1)S(1)} %get-tuple-element.30), channel_id=1, source_target_pairs={{0,1},{1,0},{2,3},{3,2},{4,5},{5,4},{6,7},{7,6},{8,9},{9,8},{10,11... | collective-permute-start | bytes 737288 | tf_op jit(solution)/shard_map/ppermute | solution.py:360
  30.8 3.5 %shard_map.96.base_ref = f32[2,240,1024]{2,1,0:T(8,128)S(1)} custom-call(bf16[2,256,240]{2,1,0:T(8,128)(2,1)S(1)} %get-tuple-element.36.rows_ref, bf16[240,2048]{1,0:T(8,128)(2,1)S(1)} %get-tuple-element.23.table_ref, bf16[2,256,1024]{2,1,0:T(8,128)(2,1)S(1)} %get-tuple-element.31.wide_ref, f32[8,128]{1,0:T(8,128)S(1)} %get-tuple-element.32.cls_ref), custom_call_target="tpu_custom_call" | custom-call | flops 2013265920 | bytes 3932160 | tf_op jit(solution)/shard_map/pallas_call | solution.py:363
  34.3 0.5 collective-permute-done.1.inflow_ref
  34.7 0.9 %shard_map.94 = (bf16[2,240,256]{2,1,0:T(8,128)(2,1)S(1)}, bf16[2,240,256]{2,1,0:T(8,128)(2,1)S(1)}) custom-call(s32[1]{0:T(128)} %bitcast.core_ref.place_ref, bf16[2,240,256]{2,1,0:T(8,128)(2,1)S(1)} %collective-permute-done.1.inflow_ref, bf16[240,2048]{1,0:T(8,128)(2,1)S(1)} %get-tuple-element.23.table_ref, ...), custom_call_target="tpu_custom_call" | custom-call | flops 503316480 | bytes 983040 | tf_op jit(solution)/shard_map/pallas_call | solution.py:374
  35.6 1.4 %collective-permute-start.2 = (bf16[2,240,256]{2,1,0:T(8,128)(2,1)S(1)}, bf16[2,240,256]{2,1,0:T(8,128)(2,1)S(1)}, u32[]{:S(2)}, u32[]{:S(2)}) collective-permute-start(bf16[2,240,256]{2,1,0:T(8,128)(2,1)S(1)} %get-tuple-element.29), channel_id=1, source_target_pairs={{0,1},{1,0},{2,3},{3,2},{4,5},{5,4},{6,7},{7,6},{8,9},{9,8},{10,11... | collective-permute-start | bytes 737288 | tf_op jit(solution)/shard_map/ppermute | solution.py:381
  37.0 3.1 %shard_map.97.rest_0_ = bf16[240,32,128]{2,1,0:T(8,128)(2,1)} custom-call(s32[1]{0:T(128)} %bitcast.core_ref.place_ref, bf16[2,240,256]{2,1,0:T(8,128)(2,1)S(1)} %get-tuple-element.35.inflow_ref, f32[2,240,1024]{2,1,0:T(8,128)S(1)} %shard_map.96.base_ref, bf16[240,2048]{1,0:T(8,128)(2,1)S(1)} %get-tuple-element.23.table_ref, ...), custom_call_target="tpu_custom_call" | custom-call | flops 1006632960 | bytes 6000000 | tf_op jit(solution)/shard_map/pallas_call | solution.py:385
  40.1 0.0 collective-permute-done.3.rows_ref
  40.1 3.5 %shard_map.95.base_ref = f32[2,240,1024]{2,1,0:T(8,128)S(1)} custom-call(bf16[2,256,240]{2,1,0:T(8,128)(2,1)S(1)} %collective-permute-done.3.rows_ref, bf16[240,2048]{1,0:T(8,128)(2,1)S(1)} %get-tuple-element.23.table_ref, bf16[2,256,1024]{2,1,0:T(8,128)(2,1)S(1)} %get-tuple-element.31.wide_ref, f32[8,128]{1,0:T(8,128)S(1)} %get-tuple-element.32.cls_ref), custom_call_target="tpu_custom_call" | custom-call | flops 2013265920 | bytes 3932160 | tf_op jit(solution)/shard_map/pallas_call | solution.py:363
  43.6 0.0 collective-permute-done.2.inflow_ref
  43.6 3.1 %shard_map.98 = bf16[240,32,128]{2,1,0:T(8,128)(2,1)} custom-call(s32[1]{0:T(128)S(6)} %sub.3.place_ref, bf16[2,240,256]{2,1,0:T(8,128)(2,1)S(1)} %collective-permute-done.2.inflow_ref, f32[2,240,1024]{2,1,0:T(8,128)S(1)} %shard_map.95.base_ref, bf16[240,2048]{1,0:T(8,128)(2,1)S(1)} %get-tuple-element.23.table_ref, ...), custom_call_target="tpu_custom_call", output_to_operand_aliasing={{}: (6, {})} | custom-call | flops 1006632960 | bytes 6000000 | tf_op jit(solution)/shard_map/pallas_call | solution.py:385
Async XLA Ops:
  0.0 11.2 %copy-start.2 = (f32[8]{0:T(128)S(1)}, f32[8]{0:T(128)}, u32[]{:S(2)}) copy-start(f32[8]{0:T(128)} %param.15) | copy-start | bytes 100
  0.0 11.2 %copy-start.1 = (f32[8,240]{1,0:T(8,128)S(1)}, f32[8,240]{1,0:T(8,128)}, u32[]{:S(2)}) copy-start(f32[8,240]{1,0:T(8,128)} %shape_ref.1) | copy-start | bytes 23044
  2.5 21.4 %all-to-all-start = ((bf16[16,64,240]{2,1,0:T(8,128)(2,1)}), bf16[16,64,240]{2,1,0:T(8,128)(2,1)S(1)}, u32[]{:S(2)}, u32[]{:S(2)}) async-start(bf16[16,64,240]{2,1,0:T(8,128)(2,1)} %bitcast.14), calls=%async_computation | async-start | bytes 1048576 | tf_op jit(solution)/shard_map/all_to_all | solution.py:308
  9.8 1.4 %collective-permute-start = (f32[64,128]{1,0:T(8,128)}, f32[64,128]{1,0:T(8,128)S(1)}, u32[]{:S(2)}, u32[]{:S(2)}) collective-permute-start(f32[64,128]{1,0:T(8,128)} %get-tuple-element.22.own_ref), channel_id=1, source_target_pairs={{0,1},{1,0},{2,3},{3,2},{4,5},{5,4},{6,7},{7,6},{8,9},{9,8},{10,11... | collective-permute-start | bytes 98312 | tf_op jit(solution)/shard_map/ppermute | solution.py:311
  11.2 0.8 %copy-start = (f32[64,128]{1,0:T(8,128)S(1)}, f32[64,128]{1,0:T(8,128)}, u32[]{:S(2)}) copy-start(f32[64,128]{1,0:T(8,128)} %get-tuple-element.22.own_ref) | copy-start | bytes 98308
  26.8 8.0 %collective-permute-start.1 = (bf16[2,240,256]{2,1,0:T(8,128)(2,1)S(1)}, bf16[2,240,256]{2,1,0:T(8,128)(2,1)S(1)}, u32[]{:S(2)}, u32[]{:S(2)}) collective-permute-start(bf16[2,240,256]{2,1,0:T(8,128)(2,1)S(1)} %get-tuple-element.27), channel_id=1, source_target_pairs={{0,2},{1,3},{4,6},{5,7},{8,10},{9,11},{12,14},{13,15},{16,18},{17,... | collective-permute-start | bytes 737288 | tf_op jit(solution)/shard_map/ppermute | solution.py:348
  29.9 10.2 %collective-permute-start.3 = (bf16[2,256,240]{2,1,0:T(8,128)(2,1)S(1)}, bf16[2,256,240]{2,1,0:T(8,128)(2,1)S(1)}, u32[]{:S(2)}, u32[]{:S(2)}) collective-permute-start(bf16[2,256,240]{2,1,0:T(8,128)(2,1)S(1)} %get-tuple-element.30), channel_id=1, source_target_pairs={{0,1},{1,0},{2,3},{3,2},{4,5},{5,4},{6,7},{7,6},{8,9},{9,8},{10,11... | collective-permute-start | bytes 737288 | tf_op jit(solution)/shard_map/ppermute | solution.py:360
  35.6 8.0 %collective-permute-start.2 = (bf16[2,240,256]{2,1,0:T(8,128)(2,1)S(1)}, bf16[2,240,256]{2,1,0:T(8,128)(2,1)S(1)}, u32[]{:S(2)}, u32[]{:S(2)}) collective-permute-start(bf16[2,240,256]{2,1,0:T(8,128)(2,1)S(1)} %get-tuple-element.29), channel_id=1, source_target_pairs={{0,1},{1,0},{2,3},{3,2},{4,5},{5,4},{6,7},{7,6},{8,9},{9,8},{10,11... | collective-permute-start | bytes 737288 | tf_op jit(solution)/shard_map/ppermute | solution.py:381

commit v3 on v2

v3 whole, which is shorter than its diff:
```python
import functools
import jax
import jax.numpy as jnp
from jax import lax
from jax.experimental import pallas as pl
from jax.experimental.pallas import tpu as pltpu
from jax.sharding import Mesh, PartitionSpec as P

BF = jnp.bfloat16
F32 = jnp.float32
MB = 8
SUB = 4
LANES = 128
VMEM_LIMIT = 20 * 1024 * 1024
SEND_VMEM = 53760 * 1024


def iota(shape, dim):
    return lax.broadcasted_iota(jnp.int32, shape, dim)


def mm(a, b):
    return jnp.dot(a, b, preferred_element_type=F32)


def tmm(a, b):
    return lax.dot_general(a, b, (((0,), (0,)), ((), ())), preferred_element_type=F32)


def one_hot(condition):
    return jnp.where(condition, 1.0, 0.0).astype(BF)


def split(value):
    high = value.astype(BF)
    return high, (value - high.astype(F32)).astype(BF)


def call(kernel, out_shape, flops, limit=VMEM_LIMIT, **extra):
    nbytes = sum(s.size * s.dtype.itemsize for s in jax.tree.leaves(out_shape))
    return pl.pallas_call(
        kernel,
        out_shape=out_shape,
        compiler_params=pltpu.CompilerParams(vmem_limit_bytes=limit),
        cost_estimate=pl.CostEstimate(flops=flops, bytes_accessed=2 * nbytes, transcendentals=0),
        **extra,
    )


def vmem(count):
    return [pl.BlockSpec(memory_space=pltpu.VMEM)] * count


SCALAR = pl.BlockSpec(memory_space=pltpu.SMEM)


def convolve(table, value, classes, class_count):
    hours = table.shape[0]
    masks = [one_hot(classes == float(k)) for k in range(class_count)]
    total = None
    for start in range(0, hours, LANES):
        block = value[start : start + LANES]
        short = LANES - block.shape[0]
        if short:
            block = jnp.concatenate([block, jnp.zeros((short, block.shape[1]), BF)], axis=0)
        parts = jnp.concatenate([block * mask for mask in masks], axis=0)
        added = mm(table[: hours - start], parts)
        if start == 0:
            total = added
        else:
            total = jnp.concatenate([total[:start], total[start:] + added], axis=0)
    return total


def pack_kernel(slot, x_ref, rows_ref, send_ref):
    members, grid, hours = x_ref.shape
    blocks = members // MB
    regions = send_ref.shape[0]
    per = MB * slot
    count = regions * per
    recv = rows_ref.shape[1]
    row = iota((count, recv), 0)
    wanted = (row // per) * slot + row % slot
    rows = rows_ref[...].astype(F32)
    chosen = jnp.sum(jnp.where(iota((count, recv), 1) == wanted, rows, 0.0), axis=1, keepdims=True)
    lane = iota((count, MB * grid), 1)
    member = (iota((count, MB * grid), 0) // slot) % MB
    select = one_hot((lane // grid == member) & ((lane % grid).astype(F32) == chosen))
    for block in range(blocks):
        x = x_ref[block * MB : (block + 1) * MB].reshape(MB * grid, hours).astype(BF)
        y = mm(select, x).astype(BF).reshape(regions, per, hours)
        core, inner = divmod(block, blocks // 2)
        send_ref[:, core, inner * per : (inner + 1) * per, :] = y


def raw_kernel(idx_ref, w_ref, cls_ref, outl_ref, inc_ref, raw_ref):
    raw_ref[...] = jnp.zeros_like(raw_ref)
    raw_ref[0 : idx_ref.shape[0], :] = idx_ref[...].astype(F32)
    raw_ref[8 : 8 + w_ref.shape[0], :] = w_ref[...]
    raw_ref[16:17, :] = cls_ref[...].astype(F32)
    raw_ref[24:25, 0 : outl_ref.shape[1]] = outl_ref[...].astype(F32)
    raw_ref[32:, :] = inc_ref[...].astype(F32)


def prep_kernel(
    slot, columns, core_ref, own_ref, other_ref, rate_ref, shape_ref,
    table_ref, mix_ref, pass_ref, cls_out_ref, wide_ref, link_ref, cls_target_ref, cls_own_ref,
):
    core = core_ref[0]
    class_count, hours = shape_ref.shape
    padded = -(-hours // LANES) * LANES
    kap = mix_ref.shape[1] // 2
    recv = kap // SUB
    per = SUB * slot
    outs = own_ref.shape[0] - 32
    reaches = own_ref.shape[1]
    wide = MB * outs
    narrow = SUB * outs

    lag = iota((class_count, hours), 1).astype(F32)
    square = (class_count, class_count)
    rate = jnp.where(iota(square, 0) == iota(square, 1), rate_ref[...], 0.0)
    rate = jnp.sum(rate, axis=1, keepdims=True)
    hydro = (rate * shape_ref[...] * jnp.exp(-rate * lag)).astype(BF)
    reverse = one_hot((iota((hours, padded), 0) + iota((hours, padded), 1)) % padded == 0)
    turned = mm(hydro, reverse)
    later = iota((padded, LANES), 1) <= iota((padded, LANES), 0)
    for k in range(class_count):
        rolled = pltpu.roll(
            jnp.broadcast_to(turned[k : k + 1, :], (padded, padded)), 0, 1, stride=1, stride_axis=0
        )
        rolled = jnp.where(later, rolled[:, :LANES], 0.0)
        table_ref[:, k * LANES : (k + 1) * LANES] = rolled[:hours].astype(BF)

    row_p = iota((kap, recv), 0)
    expand = one_hot((row_p // per) * slot + row_p % slot == iota((kap, recv), 1))

    def owner(width):
        return (iota((kap, width), 0) // slot) % SUB

    def tile(width):
        return one_hot(iota((outs, width), 0) == iota((outs, width), 1) % outs)

    def weights(raw):
        total = jnp.zeros((recv, reaches), F32)
        for j in range(columns):
            hit = iota((recv, reaches), 0).astype(F32) == raw[j : j + 1, :]
            total = total + jnp.where(hit, raw[8 + j : 9 + j, :], 0.0)
        return split(total)

    own = own_ref[...]
    for level in range(2):
        raw = jnp.where(core == level, own, other_ref[...])
        lanes = mm(raw[24:32, :outs].astype(BF), tile(wide))[0:1, :]
        pick = one_hot(iota((reaches, wide), 0).astype(F32) == lanes)
        for part, weight in enumerate(weights(raw)):
            spread = mm(expand, mm(weight, pick[:, :narrow]).astype(BF))
            spread = jnp.where(owner(narrow) == iota((kap, narrow), 1) // outs, spread, 0.0)
            mix_ref[level, part * kap : (part + 1) * kap] = spread.astype(BF)
        moved = jnp.concatenate([mm(raw[32:, :].astype(BF), pick)] * MB, axis=0)
        here = iota((wide, wide), 0) // outs == iota((wide, wide), 1) // outs
        pass_ref[level] = jnp.where(here, moved, 0.0).astype(BF)
        cls_out_ref[level] = mm(raw[16:24, :].astype(BF), pick)

    for part, weight in enumerate(weights(own)):
        spread = mm(expand, weight)
        for m in range(SUB):
            piece = jnp.where(owner(reaches) == m, spread, 0.0).astype(BF)
            wide_ref[part * kap : (part + 1) * kap, m * reaches : (m + 1) * reaches] = piece
    cls_own_ref[...] = own[16:24, :]
    cls_target_ref[...] = lax.dot_general(
        own[16:24, :].astype(BF),
        jnp.concatenate([own[32:, :]] * MB, axis=0).astype(BF),
        (((1,), (1,)), ((), ())),
        preferred_element_type=F32,
    )
    stacked = jnp.concatenate([own[32:, :]] * SUB, axis=0)
    who = iota((narrow, reaches), 0) // outs
    for m in range(SUB):
        piece = jnp.where(who == m, stacked, 0.0).astype(BF)
        for part in range(2):
            link_ref[part * narrow : (part + 1) * narrow, m * reaches : (m + 1) * reaches] = piece


def twice(rows_ref, sub, size):
    rows = rows_ref[:, sub * size : (sub + 1) * size, :]
    rows = rows.reshape(rows.shape[0] * size, rows.shape[2])
    return jnp.concatenate([rows, rows], axis=0)


def pass_on(panel, pass_matrix):
    width = pass_matrix.shape[0]
    parts = [
        mm(panel[:, start : start + width], pass_matrix).astype(BF)
        for start in range(0, panel.shape[1], width)
    ]
    return jnp.concatenate(parts, axis=1)


def tiled(classes, width):
    return jnp.concatenate([classes] * (width // classes.shape[1]), axis=1)


def head_kernel(
    class_count, core_ref, rows_ref, table_ref, mix_ref, pass_ref, cls_ref,
    even_ref, odd_ref, panel_ref, own_ref, send_ref,
):
    first = core_ref[0] == 0
    rows = [rows_ref[:, level] for level in range(2)]
    own_ref[...] = jnp.where(first, rows[0], rows[1])
    send_ref[...] = jnp.where(first, rows[1], rows[0])
    regions, _, total, _ = rows_ref.shape
    size = mix_ref.shape[1] // 2 // regions
    wide = even_ref.shape[1]
    lateral = [
        jnp.concatenate(
            [
                tmm(twice(rows_ref.at[:, level], sub, size), mix_ref[level])
                for sub in range(total // size)
            ],
            axis=1,
        )
        for level in range(2)
    ]
    classes = [tiled(cls_ref[level, 0:1, :], wide) for level in range(2)]
    even = convolve(table_ref[...], lateral[0].astype(BF), classes[0], class_count)
    even_ref[...] = even
    odd_ref[...] = lateral[1]
    inflow = lateral[1] + pass_on(even.astype(BF), pass_ref[1]).astype(F32)
    panel_ref[...] = convolve(table_ref[...], inflow.astype(BF), classes[1], class_count).astype(BF)


def hop_kernel(class_count, inflow_ref, table_ref, pass_ref, cls_ref, even_ref, odd_ref, panel_ref):
    classes = [tiled(cls_ref[level, 0:1, :], even_ref.shape[1]) for level in range(2)]
    moved = pass_on(inflow_ref[...], pass_ref[0])
    even = even_ref[...] + convolve(table_ref[...], moved, classes[0], class_count)
    moved = odd_ref[...] + pass_on(even.astype(BF), pass_ref[1]).astype(F32)
    panel_ref[...] = convolve(table_ref[...], moved.astype(BF), classes[1], class_count).astype(BF)


def last_hop_kernel(class_count, core_ref, inflow_ref, table_ref, pass_ref, cls_ref, even_ref, *rest):
    own_ref, send_ref = rest[-2:]
    arrived = inflow_ref[...]
    classes = tiled(cls_ref[0, 0:1, :], even_ref.shape[1])
    moved = pass_on(arrived, pass_ref[0])
    even = even_ref[...] + convolve(table_ref[...], moved, classes, class_count)
    even = even.astype(BF)
    first = core_ref[0] == 0
    own_ref[...] = jnp.where(first, arrived, even)
    send_ref[...] = jnp.where(first, even, arrived)


def base_kernel(class_count, rows_ref, table_ref, wide_ref, cls_ref, base_ref):
    regions, total, _ = rows_ref.shape
    size = wide_ref.shape[0] // 2 // regions
    width = wide_ref.shape[1]
    classes = tiled(cls_ref[0:1, :], width)
    for sub in range(total // size):
        lateral = tmm(twice(rows_ref, sub, size), wide_ref[...]).astype(BF)
        base_ref[:, sub * width : (sub + 1) * width] = convolve(
            table_ref[...], lateral, classes, class_count
        )


def final_kernel(class_count, place_ref, inflow_ref, base_ref, table_ref, link_ref, cls_ref, *rest):
    out_ref, scratch = rest[-2:]
    hours, members, reaches = out_ref.shape
    lanes, width = link_ref.shape[0] // 2, link_ref.shape[1]
    classes = tiled(cls_ref[0:1, :], inflow_ref.shape[1])
    routed = convolve(table_ref[...], inflow_ref[...], classes, class_count)
    high, low = split(routed)
    for part in range(routed.shape[1] // lanes):
        cut = slice(part * lanes, (part + 1) * lanes)
        spread = mm(jnp.concatenate([high[:, cut], low[:, cut]], axis=1), link_ref[...])
        total = spread + base_ref[:, part * width : (part + 1) * width]
        for j in range(width // reaches):
            member = part * (width // reaches) + j
            scratch[pl.ds(member, hours, stride=members), :] = total[
                :, j * reaches : (j + 1) * reaches
            ]
    out_ref[...] = scratch[...].reshape(hours, members, reaches).astype(BF)


def local(
    runoff, send_rows, remap_index, remap_weight, class_id, kernel_shape, kernel_rate, outlets, incidence
):
    hours, members, grid = runoff.shape
    regions = lax.axis_size("region")
    pairs = lax.axis_size("pair")
    class_count = kernel_shape.shape[0]
    reaches, columns = remap_index.shape
    recv = send_rows.size
    slot = recv // regions
    outs = outlets.size
    half = members // 2
    kap = recv * SUB
    wide = half * outs
    core = lax.axis_index("core").astype(jnp.int32)
    core_arg = core.reshape(1)
    swap = [(0, 1), (1, 0)]
    anywhere = pl.BlockSpec(memory_space=pl.ANY)
    conv_flops = 2 * hours * class_count * hours * wide

    def struct(shape, dtype):
        return jax.ShapeDtypeStruct(shape, dtype)

    send = call(
        functools.partial(pack_kernel, slot),
        struct((regions, 2, half * slot, hours), BF),
        2 * recv * MB * grid * hours * members,
        limit=SEND_VMEM,
        in_specs=vmem(2),
        out_specs=vmem(1)[0],
    )(jnp.transpose(runoff, (1, 2, 0)), send_rows.reshape(1, recv))
    received = lax.all_to_all(
        send.reshape(regions * 2, half * slot, hours), ("region", "core"), 0, 0
    ).reshape(regions, 2, half * slot, hours)
    raw = call(
        raw_kernel,
        struct((32 + outs, reaches), F32),
        1000,
        limit=SEND_VMEM,
        in_specs=vmem(5),
        out_specs=vmem(1)[0],
    )(
        remap_index.T,
        remap_weight.T,
        class_id.T,
        outlets.reshape(1, outs),
        incidence.reshape(outs, reaches),
    )
    other = lax.ppermute(raw, "core", swap)
    table, mix, passing, cls_out, wide_mix, link, cls_target, cls_own = call(
        functools.partial(prep_kernel, slot, columns),
        (
            struct((hours, class_count * LANES), BF),
            struct((2, 2 * kap, SUB * outs), BF),
            struct((2, MB * outs, MB * outs), BF),
            struct((2, 8, MB * outs), F32),
            struct((2 * kap, SUB * reaches), BF),
            struct((2 * SUB * outs, SUB * reaches), BF),
            struct((8, MB * outs), F32),
            struct((8, reaches), F32),
        ),
        10_000_000,
        in_specs=[SCALAR] + vmem(4),
        out_specs=tuple(vmem(8)),
    )(core_arg, raw, other, kernel_rate.reshape(1, class_count), kernel_shape)

    panel_shape = struct((hours, wide), BF)
    rows_shape = struct((regions, half * slot, hours), BF)
    even, odd, panel, rows_own, rows_send = call(
        functools.partial(head_kernel, class_count),
        (struct((hours, wide), F32), struct((hours, wide), F32), panel_shape, rows_shape, rows_shape),
        2 * conv_flops,
        in_specs=[SCALAR] + vmem(5),
        out_specs=tuple(vmem(5)),
    )(core_arg, received, table, mix, passing, cls_out)

    inflow = jnp.zeros(panel_shape.shape, BF)
    for step in range(pairs - 1):
        arrived = lax.ppermute(panel, "pair", [(step, step + 1)])
        inflow = arrived if step == 0 else inflow + arrived
        if step < pairs - 2:
            panel = call(
                functools.partial(hop_kernel, class_count),
                panel_shape,
                2 * conv_flops,
                in_specs=vmem(6),
                out_specs=vmem(1)[0],
            )(inflow, table, passing, cls_out, even, odd)
    rows_other = lax.ppermute(rows_send, "core", swap)

    def base(rows):
        return call(
            functools.partial(base_kernel, class_count),
            struct((hours, half * reaches), F32),
            conv_flops * reaches // outs,
            in_specs=vmem(4),
            out_specs=vmem(1)[0],
        )(rows, table, wide_mix, cls_own)

    base_own = base(rows_own)
    base_other = base(rows_other)
    own, given = call(
        functools.partial(last_hop_kernel, class_count),
        (panel_shape, panel_shape),
        conv_flops,
        in_specs=[SCALAR] + vmem(5) + [anywhere] * 2,
        out_specs=tuple(vmem(2)),
    )(core_arg, inflow, table, passing, cls_out, even, base_own, base_other)
    gotten = lax.ppermute(given, "core", swap)

    def final(place, panel_rows, base_flow, before):
        extra = [] if before is None else [before]
        return call(
            functools.partial(final_kernel, class_count),
            struct((hours, members, reaches), BF),
            2 * conv_flops,
            grid_spec=pltpu.PrefetchScalarGridSpec(
                num_scalar_prefetch=1,
                grid=(1,),
                in_specs=vmem(5) + [anywhere] * len(extra),
                out_specs=pl.BlockSpec((hours, half, reaches), lambda g, place: (0, place[0], 0)),
                scratch_shapes=[pltpu.VMEM((hours * half, reaches), F32)],
            ),
            input_output_aliases={6: 0} if extra else {},
        )(place, panel_rows, base_flow, table, link, cls_target, *extra)

    out = final(core_arg, own, base_own, None)
    return final(1 - core_arg, gotten, base_other, out)


def solution(mesh):
    regions, orders = mesh.shape["region"], mesh.shape["order"]
    split_mesh = Mesh(mesh.devices.reshape(regions, orders // 2, 2), ("region", "pair", "core"))
    order = ("pair", "core")
    every = ("region", "pair", "core")
    return jax.shard_map(
        local,
        mesh=split_mesh,
        in_specs=(
            P(None, None, every),
            P("region", order, None),
            P(every, None),
            P(every, None),
            P(every, None),
            P(),
            P(),
            P("region", order, None),
            P("region", order, None, None),
        ),
        out_specs=P(None, None, every),
        check_vma=False,
    )
```

time: 47.3 us -> 42.2 us (0.89)
  Pallas kernels: 20.5 us -> 15.8 us
  starting transfers between devices: 12.9 us -> 12 us
  waiting for transfers between devices: 12.5 us -> 13.1 us
    pallas_call x6 -> x7, Pallas kernels: 18.6 us -> 13.9 us  [the longest x2 4.97 us: base(): call(functools.partial(base_kernel, class_count), struct((hours, half * r...]
    all_to_all x1, waiting for transfers between devices: 10.8 us -> 11.6 us  [local(): lax.all_to_all(send.reshape(regions * 2, half * slot, hours), ('region',...]
    ppermute x1, starting transfers between devices: 1.4 us -> 0.86 us  [local(): gotten = lax.ppermute(given, 'core', swap)]
  transfers between devices with their start and end apart: 5 -> 5, of which waited for: 3 -> 3; matrix products, arithmetic and copies ran while one was open for 0% -> 0% of each run, Pallas kernels for 26% -> 20%
where the time goes in v3:
time: 42.2 us; the launch traced here: 41.7 us
  Pallas kernels  15.8 us (37%)
  waiting for transfers between devices  13.1 us (31%)
  starting transfers between devices  12 us (28%)
  local copies, waits for them, and re-layouts  0.72 us (2%)
    all_to_all x1, waiting for transfers between devices, local(): lax.all_to_all(send.reshape(regions * 2, half * slot, hours), ('region',...  11.6 us
    all_to_all x1, starting transfers between devices, local(): lax.all_to_all(send.reshape(regions * 2, half * slot, hours), ('region',...  7.32 us
    pallas_call x2, Pallas kernels, base(): call(functools.partial(base_kernel, class_count), struct((hours, half * r...  4.97 us
    pallas_call x2, Pallas kernels, final(): call(functools.partial(final_kernel, class_count), struct((hours, members...  4.69 us
    ppermute x1, starting transfers between devices, local(): arrived = lax.ppermute(panel, 'pair', [(step, step + 1)])  3.14 us
    pallas_call x1, Pallas kernels, local(): call(functools.partial(pack_kernel, slot), struct((regions, 2, half * slo...  2.41 us
    pallas_call x1, Pallas kernels, local(): call(functools.partial(head_kernel, class_count), (struct((hours, wide),...  1.88 us
    pallas_call x1, Pallas kernels, local(): call(functools.partial(prep_kernel, slot, columns), (struct((hours, class...  1.11 us
  transfers between devices with their start and end apart: 5, of which 3 were waited for; matrix products, arithmetic and copies ran while one was open for 0% of the time, Pallas kernels for 20%

profile of v3, /device:TPU:1, one launch (start us, length us, event | category | flops | bytes accessed | tf_op | source)
XLA Modules:
  0.0 41.7 jit_solution(17629766153379918614)
XLA Ops:
  0.0 0.0 copy-start.2
  0.0 0.0 copy-start.3
  0.0 0.0 copy-start
  0.0 0.0 copy-start.1
  0.0 0.0 copy-start.4
  0.0 0.7 %copy-done.4 = s32[1,1,32]{2,1,0:T(1,128)S(1)} copy-done((s32[1,1,32]{2,1,0:T(1,128)S(1)}, s32[1,1,32]{2,1,0:T(1,128)}, u32[]{:S(2)}) %copy-start.4) | copy-done | bytes 152
  0.7 0.0 copy-start.5
  0.7 2.4 %shard_map.91 = bf16[8,2,64,240]{3,2,1,0:T(8,128)(2,1)} custom-call(f32[32,32,240]{2,1,0:T(8,128)} %bitcast.19, s32[1,32]{1,0:T(1,128)S(1)} %bitcast.15), custom_call_target="tpu_custom_call" | custom-call | flops 125829120 | bytes 983040 | tf_op jit(solution)/shard_map/pallas_call | solution.py:307
  3.1 7.3 %all-to-all-start = ((bf16[16,64,240]{2,1,0:T(8,128)(2,1)}), bf16[16,64,240]{2,1,0:T(8,128)(2,1)S(1)}, u32[]{:S(2)}, u32[]{:S(2)}) async-start(bf16[16,64,240]{2,1,0:T(8,128)(2,1)} %bitcast.3), calls=%async_computation | async-start | bytes 1048576 | tf_op jit(solution)/shard_map/all_to_all | solution.py:315
  10.5 0.0 copy-done.2
  10.5 0.0 copy-done.3
  10.5 0.0 copy-done
  10.5 0.0 copy-done.5
  10.5 0.0 copy-done.6
  10.5 0.2 collective-permute-start
  10.7 1.1 %collective-permute-done.other_ref = f32[64,128]{1,0:T(8,128)S(1)} collective-permute-done((f32[64,128]{1,0:T(8,128)S(1)}, f32[64,128]{1,0:T(8,128)S(1)}, u32[]{:S(2)}, u32[]{:S(2)}) %collective-permute-start) | collective-permute-done | bytes 32800 | tf_op jit(solution)/shard_map/ppermute | solution.py:332
  11.8 0.0 copy-done.1
  11.8 0.0 copy-done.7
  11.8 1.1 %shard_map.93 = (bf16[240,1024]{1,0:T(8,128)(2,1)S(1)}, bf16[2,256,128]{2,1,0:T(8,128)(2,1)S(1)}, bf16[2,256,256]{2,1,0:T(8,128)(2,1)S(1)}, f32[2,8,256]{2,1,0:T...) custom-call(s32[1]{0:T(128)} %bitcast.core_ref.place_ref, ...), custom_call_target="tpu_custom_call" | custom-call | flops 10000000 | bytes 2875392 | tf_op jit(solution)/shard_map/pallas_call | solution.py:333
  12.9 11.6 %all-to-all-done = bf16[16,64,240]{2,1,0:T(8,128)(2,1)S(1)} async-done(((bf16[16,64,240]{2,1,0:T(8,128)(2,1)}), bf16[16,64,240]{2,1,0:T(8,128)(2,1)S(1)}, u32[]{:S(2)}, u32[]{:S(2)}) %all-to-all-start) | async-done | bytes 491552 | tf_op jit(solution)/shard_map/all_to_all | solution.py:315
  24.5 1.9 %shard_map.94 = (f32[240,512]{1,0:T(8,128)S(1)}, f32[240,512]{1,0:T(8,128)}, bf16[240,512]{1,0:T(8,128)(2,1)S(1)}, bf16[8,64,240]{2,1,0:T(8,128)(2,1)S(1)}, bf16[8,64,240]{2,1,0:T(8,128)(2,1)S(1)}) custom-call(s32[1]{0:T(128)} %bitcast.core_ref.place_ref, bf16[8,2,64,240]{3,2,1,0:T(8,128)(2,1)S(1)} %bitcast.11, ...), custom_call_target="tpu_custom_call" | custom-call | flops 943718400 | bytes 3440640 | tf_op jit(solution)/shard_map/pallas_call | solution.py:352
  26.4 0.5 %collective-permute-start.2 = (bf16[8,64,240]{2,1,0:T(8,128)(2,1)S(1)}, bf16[8,64,240]{2,1,0:T(8,128)(2,1)S(1)}, u32[]{:S(2)}, u32[]{:S(2)}) collective-permute-start(bf16[8,64,240]{2,1,0:T(8,128)(2,1)S(1)} %get-tuple-element.28), channel_id=1, source_target_pairs={{0,1},{1,0},{2,3},{3,2},{4,5},{5,4},{6,7},{7,6},{8,9},{9,8},{10,11... | collective-permute-start | bytes 737288 | tf_op jit(solution)/shard_map/ppermute | solution.py:372
  26.9 3.1 %collective-permute-start.1 = (bf16[240,512]{1,0:T(8,128)(2,1)S(1)}, bf16[240,512]{1,0:T(8,128)(2,1)S(1)}, u32[]{:S(2)}, u32[]{:S(2)}) collective-permute-start(bf16[240,512]{1,0:T(8,128)(2,1)S(1)} %get-tuple-element.23), channel_id=1, source_target_pairs={{0,2},{1,3},{4,6},{5,7},{8,10},{9,11},{12,14},{13,15},{16,18},{17,... | collective-permute-start | bytes 737288 | tf_op jit(solution)/shard_map/ppermute | solution.py:362
  30.1 2.5 %shard_map.95.rest_0_.base_ref = f32[240,2048]{1,0:T(8,128)S(1)} custom-call(bf16[8,64,240]{2,1,0:T(8,128)(2,1)S(1)} %get-tuple-element.25.rows_ref, bf16[240,1024]{1,0:T(8,128)(2,1)S(1)} %get-tuple-element.19.table_ref, bf16[256,512]{1,0:T(8,128)(2,1)S(1)} %get-tuple-element.26.wide_ref, f32[8,128]{1,0:T(8,128)S(1)} %get-tuple-element.27.cls_ref), custom_call_target="tpu_custom_call" | custom-call | flops 1887436800 | bytes 3932160 | tf_op jit(solution)/shard_map/pallas_call | solution.py:375
  32.6 0.0 collective-permute-done.2.rows_ref
  32.6 2.5 %shard_map.96.rest_1_.base_ref = f32[240,2048]{1,0:T(8,128)S(1)} custom-call(bf16[8,64,240]{2,1,0:T(8,128)(2,1)S(1)} %collective-permute-done.2.rows_ref, bf16[240,1024]{1,0:T(8,128)(2,1)S(1)} %get-tuple-element.19.table_ref, bf16[256,512]{1,0:T(8,128)(2,1)S(1)} %get-tuple-element.26.wide_ref, f32[8,128]{1,0:T(8,128)S(1)} %get-tuple-element.27.cls_ref), custom_call_target="tpu_custom_call" | custom-call | flops 1887436800 | bytes 3932160 | tf_op jit(solution)/shard_map/pallas_call | solution.py:375
  35.0 0.3 collective-permute-done.1.inflow_ref
  35.4 0.8 %shard_map.97 = (bf16[240,512]{1,0:T(8,128)(2,1)S(1)}, bf16[240,512]{1,0:T(8,128)(2,1)S(1)}) custom-call(s32[1]{0:T(128)} %bitcast.core_ref.place_ref, bf16[240,512]{1,0:T(8,128)(2,1)S(1)} %collective-permute-done.1.inflow_ref, bf16[240,1024]{1,0:T(8,128)(2,1)S(1)} %get-tuple-element.19.table_ref, bf16[2,256,256]{2,1,0:T(8,128)(2,1)S(1)} %get-tuple-element.21.pass_ref, ...), custom_call_target="tpu_custom_call" | custom-call | flops 471859200 | bytes 983040 | tf_op jit(solution)/shard_map/pallas_call | solution.py:385
  36.2 0.9 %collective-permute-start.3 = (bf16[240,512]{1,0:T(8,128)(2,1)S(1)}, bf16[240,512]{1,0:T(8,128)(2,1)S(1)}, u32[]{:S(2)}, u32[]{:S(2)}) collective-permute-start(bf16[240,512]{1,0:T(8,128)(2,1)S(1)} %get-tuple-element.29), channel_id=1, source_target_pairs={{0,1},{1,0},{2,3},{3,2},{4,5},{5,4},{6,7},{7,6},{8,9},{9,8},{10,11... | collective-permute-start | bytes 737288 | tf_op jit(solution)/shard_map/ppermute | solution.py:392
  37.0 2.3 %shard_map.98.rest_0_ = bf16[240,32,128]{2,1,0:T(8,128)(2,1)} custom-call(s32[1]{0:T(128)} %bitcast.core_ref.place_ref, bf16[240,512]{1,0:T(8,128)(2,1)S(1)} %get-tuple-element.32.inflow_ref, f32[240,2048]{1,0:T(8,128)S(1)} %shard_map.95.rest_0_.base_ref, bf16[240,1024]{1,0:T(8,128)(2,1)S(1)} %get-tuple-element.19.table_ref, ...), custom_call_target="tpu_custom_call" | custom-call | flops 943718400 | bytes 3932160 | tf_op jit(solution)/shard_map/pallas_call | solution.py:396
  39.4 0.0 collective-permute-done.3.inflow_ref
  39.4 2.3 %shard_map.99 = bf16[240,32,128]{2,1,0:T(8,128)(2,1)} custom-call(s32[1]{0:T(128)S(6)} %sub.3.place_ref, bf16[240,512]{1,0:T(8,128)(2,1)S(1)} %collective-permute-done.3.inflow_ref, f32[240,2048]{1,0:T(8,128)S(1)} %shard_map.96.rest_1_.base_ref, bf16[240,1024]{1,0:T(8,128)(2,1)S(1)} %get-tuple-element.19.table_ref, ...), custom_call_target="tpu_custom_call", output_to_operand_aliasing={{}: (6, {})} | custom-call | flops 943718400 | bytes 3932160 | tf_op jit(solution)/shard_map/pallas_call | solution.py:396
  (3 shorter events, 0.0 us)
Async XLA Ops:
  0.0 10.5 %copy-start.2 = (s32[128,4]{0,1:T(4,128)S(1)}, s32[128,4]{0,1:T(4,128)}, u32[]{:S(2)}) copy-start(s32[128,4]{0,1:T(4,128)} %param.11) | copy-start | bytes 6148
  0.0 10.5 %copy-start.3 = (f32[128,4]{0,1:T(4,128)S(1)}, f32[128,4]{0,1:T(4,128)}, u32[]{:S(2)}) copy-start(f32[128,4]{0,1:T(4,128)} %param.12) | copy-start | bytes 6148
  0.0 10.5 %copy-start = (s32[1,1,32,128]{3,2,1,0:T(8,128)S(1)}, s32[1,1,32,128]{3,2,1,0:T(8,128)}, u32[]{:S(2)}) copy-start(s32[1,1,32,128]{3,2,1,0:T(8,128)} %param.17) | copy-start | bytes 49156
  0.0 11.8 %copy-start.1 = (f32[8,240]{1,0:T(8,128)S(1)}, f32[8,240]{1,0:T(8,128)}, u32[]{:S(2)}) copy-start(f32[8,240]{1,0:T(8,128)} %shape_ref.1) | copy-start | bytes 23044
  0.0 0.7 %copy-start.4 = (s32[1,1,32]{2,1,0:T(1,128)S(1)}, s32[1,1,32]{2,1,0:T(1,128)}, u32[]{:S(2)}) copy-start(s32[1,1,32]{2,1,0:T(1,128)} %param.10) | copy-start | bytes 388
  0.7 9.8 %copy-start.5 = (s32[128,1]{0,1:T(1,128)S(1)}, s32[128,1]{0,1:T(1,128)}, u32[]{:S(2)}) copy-start(s32[128,1]{0,1:T(1,128)} %param.13) | copy-start | bytes 1540
  0.7 9.8 %copy-start.6 = (s32[1,1,32]{2,1,0:T(1,128)S(1)}, s32[1,1,32]{2,1,0:T(1,128)}, u32[]{:S(2)}) copy-start(s32[1,1,32]{2,1,0:T(1,128)} %param.16) | copy-start | bytes 388
  0.7 11.1 %copy-start.7 = (f32[8]{0:T(128)S(1)}, f32[8]{0:T(128)}, u32[]{:S(2)}) copy-start(f32[8]{0:T(128)} %param.15) | copy-start | bytes 100
  3.1 21.4 %all-to-all-start = ((bf16[16,64,240]{2,1,0:T(8,128)(2,1)}), bf16[16,64,240]{2,1,0:T(8,128)(2,1)S(1)}, u32[]{:S(2)}, u32[]{:S(2)}) async-start(bf16[16,64,240]{2,1,0:T(8,128)(2,1)} %bitcast.3), calls=%async_computation | async-start | bytes 1048576 | tf_op jit(solution)/shard_map/all_to_all | solution.py:315
  10.5 1.3 %collective-permute-start = (f32[64,128]{1,0:T(8,128)S(1)}, f32[64,128]{1,0:T(8,128)S(1)}, u32[]{:S(2)}, u32[]{:S(2)}) collective-permute-start(f32[64,128]{1,0:T(8,128)S(1)} %shard_map.92.own_ref), channel_id=1, source_target_pairs={{0,1},{1,0},{2,3},{3,2},{4,5},{5,4},{6,7},{7,6},{8,9},{9,8},{10,11... | collective-permute-start | bytes 98312 | tf_op jit(solution)/shard_map/ppermute | solution.py:332
  26.4 6.2 %collective-permute-start.2 = (bf16[8,64,240]{2,1,0:T(8,128)(2,1)S(1)}, bf16[8,64,240]{2,1,0:T(8,128)(2,1)S(1)}, u32[]{:S(2)}, u32[]{:S(2)}) collective-permute-start(bf16[8,64,240]{2,1,0:T(8,128)(2,1)S(1)} %get-tuple-element.28), channel_id=1, source_target_pairs={{0,1},{1,0},{2,3},{3,2},{4,5},{5,4},{6,7},{7,6},{8,9},{9,8},{10,11... | collective-permute-start | bytes 737288 | tf_op jit(solution)/shard_map/ppermute | solution.py:372
  26.9 8.5 %collective-permute-start.1 = (bf16[240,512]{1,0:T(8,128)(2,1)S(1)}, bf16[240,512]{1,0:T(8,128)(2,1)S(1)}, u32[]{:S(2)}, u32[]{:S(2)}) collective-permute-start(bf16[240,512]{1,0:T(8,128)(2,1)S(1)} %get-tuple-element.23), channel_id=1, source_target_pairs={{0,2},{1,3},{4,6},{5,7},{8,10},{9,11},{12,14},{13,15},{16,18},{17,... | collective-permute-start | bytes 737288 | tf_op jit(solution)/shard_map/ppermute | solution.py:362
  36.2 3.2 %collective-permute-start.3 = (bf16[240,512]{1,0:T(8,128)(2,1)S(1)}, bf16[240,512]{1,0:T(8,128)(2,1)S(1)}, u32[]{:S(2)}, u32[]{:S(2)}) collective-permute-start(bf16[240,512]{1,0:T(8,128)(2,1)S(1)} %get-tuple-element.29), channel_id=1, source_target_pairs={{0,1},{1,0},{2,3},{3,2},{4,5},{5,4},{6,7},{7,6},{8,9},{9,8},{10,11... | collective-permute-start | bytes 737288 | tf_op jit(solution)/shard_map/ppermute | solution.py:392

commit v4 on v3

--- a/solution.py
+++ b/solution.py
@@ -12,7 +12,7 @@
 SUB = 4
 LANES = 128
 VMEM_LIMIT = 20 * 1024 * 1024
-SEND_VMEM = 53760 * 1024
+FULL_VMEM = 56 * 1024 * 1024
 
 
 def iota(shape, dim):
@@ -72,25 +72,45 @@
     return total
 
 
-def pack_kernel(slot, x_ref, rows_ref, send_ref):
+def pack_kernel(slot, x_ref, rows_ref, send_ref, held, rows_held, ready, arrived, sent):
     members, grid, hours = x_ref.shape
     blocks = members // MB
     regions = send_ref.shape[0]
     per = MB * slot
+
+    half = members // 2
+
+    def fetch(core):
+        place = pl.ds(core * half, half)
+        return pltpu.make_async_copy(x_ref.at[place], held.at[place], arrived.at[core])
+
+    def deliver(core):
+        return pltpu.make_async_copy(ready.at[:, core], send_ref.at[:, core], sent.at[core])
+
+    first = pltpu.make_async_copy(rows_ref, rows_held, arrived.at[2])
+    first.start()
+    for core in range(2):
+        fetch(core).start()
+    first.wait()
     count = regions * per
     recv = rows_ref.shape[1]
     row = iota((count, recv), 0)
     wanted = (row // per) * slot + row % slot
-    rows = rows_ref[...].astype(F32)
+    rows = rows_held[...].astype(F32)
     chosen = jnp.sum(jnp.where(iota((count, recv), 1) == wanted, rows, 0.0), axis=1, keepdims=True)
     lane = iota((count, MB * grid), 1)
     member = (iota((count, MB * grid), 0) // slot) % MB
     select = one_hot((lane // grid == member) & ((lane % grid).astype(F32) == chosen))
-    for block in range(blocks):
-        x = x_ref[block * MB : (block + 1) * MB].reshape(MB * grid, hours).astype(BF)
-        y = mm(select, x).astype(BF).reshape(regions, per, hours)
-        core, inner = divmod(block, blocks // 2)
-        send_ref[:, core, inner * per : (inner + 1) * per, :] = y
+    for core in range(2):
+        fetch(core).wait()
+        for inner in range(blocks // 2):
+            begin = core * half + inner * MB
+            x = held[begin : begin + MB].reshape(MB * grid, hours).astype(BF)
+            y = mm(select, x).astype(BF).reshape(regions, per, hours)
+            ready[:, core, inner * per : (inner + 1) * per, :] = y
+        deliver(core).start()
+    for core in range(2):
+        deliver(core).wait()
 
 
 def raw_kernel(idx_ref, w_ref, cls_ref, outl_ref, inc_ref, raw_ref):
@@ -238,9 +258,9 @@
     panel_ref[...] = convolve(table_ref[...], moved.astype(BF), classes[1], class_count).astype(BF)
 
 
-def last_hop_kernel(class_count, core_ref, inflow_ref, table_ref, pass_ref, cls_ref, even_ref, *rest):
+def last_hop_kernel(class_count, core_ref, valid_ref, inflow_ref, table_ref, pass_ref, cls_ref, even_ref, *rest):
     own_ref, send_ref = rest[-2:]
-    arrived = inflow_ref[...]
+    arrived = jnp.where(valid_ref[0] == 1, inflow_ref[...], jnp.zeros((), BF))
     classes = tiled(cls_ref[0, 0:1, :], even_ref.shape[1])
     moved = pass_on(arrived, pass_ref[0])
     even = even_ref[...] + convolve(table_ref[...], moved, classes, class_count)
@@ -262,23 +282,60 @@
         )
 
 
-def final_kernel(class_count, place_ref, inflow_ref, base_ref, table_ref, link_ref, cls_ref, *rest):
-    out_ref, scratch = rest[-2:]
-    hours, members, reaches = out_ref.shape
+def routed_parts(class_count, inflow_ref, table_ref, cls_ref):
+    classes = tiled(cls_ref[0:1, :], inflow_ref.shape[1])
+    return split(convolve(table_ref[...], inflow_ref[...], classes, class_count))
+
+
+def assemble(hours, high, low, base_ref, link_ref, scratch, members, reaches):
     lanes, width = link_ref.shape[0] // 2, link_ref.shape[1]
-    classes = tiled(cls_ref[0:1, :], inflow_ref.shape[1])
-    routed = convolve(table_ref[...], inflow_ref[...], classes, class_count)
-    high, low = split(routed)
-    for part in range(routed.shape[1] // lanes):
+    count = hours.stop - hours.start
+    for part in range(high.shape[1] // lanes):
         cut = slice(part * lanes, (part + 1) * lanes)
-        spread = mm(jnp.concatenate([high[:, cut], low[:, cut]], axis=1), link_ref[...])
-        total = spread + base_ref[:, part * width : (part + 1) * width]
+        both = jnp.concatenate([high[hours, cut], low[hours, cut]], axis=1)
+        total = mm(both, link_ref[...]) + base_ref[hours, part * width : (part + 1) * width]
         for j in range(width // reaches):
             member = part * (width // reaches) + j
-            scratch[pl.ds(member, hours, stride=members), :] = total[
+            scratch[pl.ds(hours.start * members + member, count, stride=members), :] = total[
                 :, j * reaches : (j + 1) * reaches
             ]
-    out_ref[...] = scratch[...].reshape(hours, members, reaches).astype(BF)
+    flow = scratch[hours.start * members : hours.stop * members, :]
+    return flow.reshape(count, members, reaches).astype(BF)
+
+
+def early_kernel(class_count, inflow_ref, base_ref, table_ref, link_ref, cls_ref, out_ref, scratch):
+    hours, members, reaches = out_ref.shape
+    high, low = routed_parts(class_count, inflow_ref, table_ref, cls_ref)
+    out_ref[...] = assemble(
+        slice(0, hours), high, low, base_ref, link_ref, scratch, members, reaches
+    )
+
+
+def late_kernel(
+    class_count, core_ref, done_ref, inflow_ref, base_ref, table_ref, link_ref, cls_ref,
+    out_ref, scratch, ready, sems,
+):
+    hours, members, reaches = done_ref.shape
+    core = core_ref[0]
+
+    def place(which):
+        return pl.ds(pl.multiple_of(which * members, members), members)
+
+    copies = [pltpu.make_async_copy(done_ref, out_ref.at[:, place(core)], sems.at[0])]
+    copies[0].start()
+    high, low = routed_parts(class_count, inflow_ref, table_ref, cls_ref)
+    for start in range(0, hours, LANES):
+        part = slice(start, min(start + LANES, hours))
+        ready[part] = assemble(part, high, low, base_ref, link_ref, scratch, members, reaches)
+        span = pl.ds(start, part.stop - start)
+        copies.append(
+            pltpu.make_async_copy(
+                ready.at[span], out_ref.at[span, place(1 - core)], sems.at[len(copies)]
+            )
+        )
+        copies[-1].start()
+    for copy in copies:
+        copy.wait()
 
 
 def local(
@@ -297,6 +354,8 @@
     wide = half * outs
     core = lax.axis_index("core").astype(jnp.int32)
     core_arg = core.reshape(1)
+    pair = lax.axis_index("pair")
+    valid = (pair > 0).astype(jnp.int32).reshape(1)
     swap = [(0, 1), (1, 0)]
     anywhere = pl.BlockSpec(memory_space=pl.ANY)
     conv_flops = 2 * hours * class_count * hours * wide
@@ -308,9 +367,16 @@
         functools.partial(pack_kernel, slot),
         struct((regions, 2, half * slot, hours), BF),
         2 * recv * MB * grid * hours * members,
-        limit=SEND_VMEM,
-        in_specs=vmem(2),
-        out_specs=vmem(1)[0],
+        limit=FULL_VMEM,
+        in_specs=[anywhere] * 2,
+        out_specs=anywhere,
+        scratch_shapes=[
+            pltpu.VMEM((members, grid, hours), F32),
+            pltpu.VMEM((1, recv), jnp.int32),
+            pltpu.VMEM((regions, 2, half * slot, hours), BF),
+            pltpu.SemaphoreType.DMA((3,)),
+            pltpu.SemaphoreType.DMA((2,)),
+        ],
     )(jnp.transpose(runoff, (1, 2, 0)), send_rows.reshape(1, recv))
     received = lax.all_to_all(
         send.reshape(regions * 2, half * slot, hours), ("region", "core"), 0, 0
@@ -319,7 +385,6 @@
         raw_kernel,
         struct((32 + outs, reaches), F32),
         1000,
-        limit=SEND_VMEM,
         in_specs=vmem(5),
         out_specs=vmem(1)[0],
     )(
@@ -359,8 +424,11 @@
 
     inflow = jnp.zeros(panel_shape.shape, BF)
     for step in range(pairs - 1):
-        arrived = lax.ppermute(panel, "pair", [(step, step + 1)])
-        inflow = arrived if step == 0 else inflow + arrived
+        arrived = lax.ppermute(panel, "pair", [(step, step + 1), (step + 1, step)])
+        if pairs == 2:
+            inflow = arrived
+        else:
+            inflow = jnp.where(pair == step + 1, arrived, inflow)
         if step < pairs - 2:
             panel = call(
                 functools.partial(hop_kernel, class_count),
@@ -386,29 +454,33 @@
         functools.partial(last_hop_kernel, class_count),
         (panel_shape, panel_shape),
         conv_flops,
-        in_specs=[SCALAR] + vmem(5) + [anywhere] * 2,
+        in_specs=[SCALAR] * 2 + vmem(5) + [anywhere] * 2,
         out_specs=tuple(vmem(2)),
-    )(core_arg, inflow, table, passing, cls_out, even, base_own, base_other)
+    )(core_arg, valid, inflow, table, passing, cls_out, even, base_own, base_other)
     gotten = lax.ppermute(given, "core", swap)
 
-    def final(place, panel_rows, base_flow, before):
-        extra = [] if before is None else [before]
-        return call(
-            functools.partial(final_kernel, class_count),
-            struct((hours, members, reaches), BF),
-            2 * conv_flops,
-            grid_spec=pltpu.PrefetchScalarGridSpec(
-                num_scalar_prefetch=1,
-                grid=(1,),
-                in_specs=vmem(5) + [anywhere] * len(extra),
-                out_specs=pl.BlockSpec((hours, half, reaches), lambda g, place: (0, place[0], 0)),
-                scratch_shapes=[pltpu.VMEM((hours * half, reaches), F32)],
-            ),
-            input_output_aliases={6: 0} if extra else {},
-        )(place, panel_rows, base_flow, table, link, cls_target, *extra)
-
-    out = final(core_arg, own, base_own, None)
-    return final(1 - core_arg, gotten, base_other, out)
+    flow_shape = struct((hours, half, reaches), BF)
+    flat = pltpu.VMEM((hours * half, reaches), F32)
+    done = call(
+        functools.partial(early_kernel, class_count),
+        flow_shape,
+        2 * conv_flops,
+        in_specs=vmem(5),
+        out_specs=vmem(1)[0],
+        scratch_shapes=[flat],
+    )(own, base_own, table, link, cls_target)
+    return call(
+        functools.partial(late_kernel, class_count),
+        struct((hours, members, reaches), BF),
+        2 * conv_flops,
+        in_specs=[SCALAR] + vmem(6),
+        out_specs=anywhere,
+        scratch_shapes=[
+            flat,
+            pltpu.VMEM((hours, half, reaches), BF),
+            pltpu.SemaphoreType.DMA((1 + -(-hours // LANES),)),
+        ],
+    )(core_arg, done, gotten, base_other, table, link, cls_target)
 
 
 def solution(mesh):

time: 42.2 us -> 39.2 us (0.929)
  starting transfers between devices: 12 us -> 10.1 us
  Pallas kernels: 15.8 us -> 14.5 us
  waiting for transfers between devices: 13.1 us -> 14.1 us
  local copies, waits for them, and re-layouts: 0.72 us -> 0.03 us
    ppermute x1, starting transfers between devices: 3.14 us -> 1.25 us  [local(): arrived = lax.ppermute(panel, 'pair', [(step, step + 1), (step + 1, step)])]
    pallas_call x3, Pallas kernels: 4.7 us -> 3.46 us  [the longest x1 2.12 us: local(): call(functools.partial(late_kernel, class_count), struct((hours, members,...]
    ppermute x1, waiting for transfers between devices: 0.35 us -> 1.34 us  [local(): arrived = lax.ppermute(panel, 'pair', [(step, step + 1), (step + 1, step)])]
    unnamed x16 -> x14, local copies, waits for them, and re-layouts: 0.72 us -> 0.03 us
  transfers between devices with their start and end apart: 5 -> 5, of which waited for: 3 -> 3; matrix products, arithmetic and copies ran while one was open for 0% -> 0% of each run, Pallas kernels for 20% -> 19%
where the time goes in v4:
time: 39.2 us; the launch traced here: 38.8 us
  Pallas kernels  14.5 us (37%)
  waiting for transfers between devices  14.1 us (36%)
  starting transfers between devices  10.1 us (26%)
    all_to_all x1, waiting for transfers between devices, local(): lax.all_to_all(send.reshape(regions * 2, half * slot, hours), ('region',...  11.6 us
    all_to_all x1, starting transfers between devices, local(): lax.all_to_all(send.reshape(regions * 2, half * slot, hours), ('region',...  7.34 us
    pallas_call x2, Pallas kernels, base(): call(functools.partial(base_kernel, class_count), struct((hours, half * r...  4.96 us
    pallas_call x1, Pallas kernels, local(): call(functools.partial(pack_kernel, slot), struct((regions, 2, half * slo...  2.32 us
    pallas_call x1, Pallas kernels, local(): call(functools.partial(late_kernel, class_count), struct((hours, members,...  2.12 us
    pallas_call x1, Pallas kernels, local(): call(functools.partial(head_kernel, class_count), (struct((hours, wide),...  1.89 us
    ppermute x1, waiting for transfers between devices, local(): arrived = lax.ppermute(panel, 'pair', [(step, step + 1), (step + 1, step)])  1.34 us
    pallas_call x1, Pallas kernels, local(): call(functools.partial(early_kernel, class_count), flow_shape, 2 * conv_f...  1.33 us
  transfers between devices with their start and end apart: 5, of which 3 were waited for; matrix products, arithmetic and copies ran while one was open for 0% of the time, Pallas kernels for 19%

profile of v4, /device:TPU:1, one launch (start us, length us, event | category | flops | bytes accessed | tf_op | source)
XLA Modules:
  0.0 38.8 jit_solution(18249271520139501343)
XLA Ops:
  0.0 0.0 copy-start
  0.0 0.0 copy-start.5
  0.0 0.0 copy-start.4
  0.0 0.0 copy-start.3
  0.0 0.0 copy-start.2
  0.0 0.0 copy-start.6
  0.0 0.0 copy-start.1
  0.0 2.3 %shard_map.91 = bf16[8,2,64,240]{3,2,1,0:T(8,128)(2,1)} custom-call(f32[32,32,240]{2,1,0:T(8,128)} %bitcast.20, s32[1,32]{1,0:T(1,128)} %bitcast.21), custom_call_target="tpu_custom_call" | custom-call | flops 125829120 | bytes 983040 | tf_op jit(solution)/shard_map/pallas_call | solution.py:366
  2.4 7.3 %all-to-all-start = ((bf16[16,64,240]{2,1,0:T(8,128)(2,1)}), bf16[16,64,240]{2,1,0:T(8,128)(2,1)S(1)}, u32[]{:S(2)}, u32[]{:S(2)}) async-start(bf16[16,64,240]{2,1,0:T(8,128)(2,1)} %bitcast.19), calls=%async_computation | async-start | bytes 1048576 | tf_op jit(solution)/shard_map/all_to_all | solution.py:381
  9.7 0.0 copy-done
  9.7 0.0 copy-done.5
  9.7 0.0 copy-done.4
  9.7 0.0 copy-done.3
  9.8 0.0 copy-done.2
  9.8 0.2 collective-permute-start
  9.9 1.1 %collective-permute-done.other_ref = f32[64,128]{1,0:T(8,128)S(1)} collective-permute-done((f32[64,128]{1,0:T(8,128)S(1)}, f32[64,128]{1,0:T(8,128)S(1)}, u32[]{:S(2)}, u32[]{:S(2)}) %collective-permute-start) | collective-permute-done | bytes 32800 | tf_op jit(solution)/shard_map/ppermute | solution.py:397
  11.0 0.0 copy-done.6
  11.1 0.0 copy-done.1
  11.1 1.1 %shard_map.93 = (bf16[240,1024]{1,0:T(8,128)(2,1)S(1)}, bf16[2,256,128]{2,1,0:T(8,128)(2,1)S(1)}, bf16[2,256,256]{2,1,0:T(8,128)(2,1)S(1)}, f32[2,8,256]{2,1,0:T...) custom-call(s32[1]{0:T(128)} %bitcast.core_ref, ...), custom_call_target="tpu_custom_call" | custom-call | flops 10000000 | bytes 2875392 | tf_op jit(solution)/shard_map/pallas_call | solution.py:398
  12.2 11.6 %all-to-all-done = bf16[16,64,240]{2,1,0:T(8,128)(2,1)S(1)} async-done(((bf16[16,64,240]{2,1,0:T(8,128)(2,1)}), bf16[16,64,240]{2,1,0:T(8,128)(2,1)S(1)}, u32[]{:S(2)}, u32[]{:S(2)}) %all-to-all-start) | async-done | bytes 491552 | tf_op jit(solution)/shard_map/all_to_all | solution.py:381
  23.8 1.9 %shard_map.94 = (f32[240,512]{1,0:T(8,128)S(1)}, f32[240,512]{1,0:T(8,128)}, bf16[240,512]{1,0:T(8,128)(2,1)S(1)}, bf16[8,64,240]{2,1,0:T(8,128)(2,1)S(1)}, bf16[8,64,240]{2,1,0:T(8,128)(2,1)S(1)}) custom-call(s32[1]{0:T(128)} %bitcast.core_ref, bf16[8,2,64,240]{3,2,1,0:T(8,128)(2,1)S(1)} %bitcast.12, bf16[240,1024]{1,0:T(8,128)(2,1)S(1)} %get-tuple-element.19.table_ref, ...), custom_call_target="tpu_custom_call" | custom-call | flops 943718400 | bytes 3440640 | tf_op jit(solution)/shard_map/pallas_call | solution.py:417
  25.7 0.5 %collective-permute-start.2 = (bf16[8,64,240]{2,1,0:T(8,128)(2,1)S(1)}, bf16[8,64,240]{2,1,0:T(8,128)(2,1)S(1)}, u32[]{:S(2)}, u32[]{:S(2)}) collective-permute-start(bf16[8,64,240]{2,1,0:T(8,128)(2,1)S(1)} %get-tuple-element.28), channel_id=1, source_target_pairs={{0,1},{1,0},{2,3},{3,2},{4,5},{5,4},{6,7},{7,6},{8,9},{9,8},{10,11... | collective-permute-start | bytes 737288 | tf_op jit(solution)/shard_map/ppermute | solution.py:440
  26.2 1.2 %collective-permute-start.1 = (bf16[240,512]{1,0:T(8,128)(2,1)S(1)}, bf16[240,512]{1,0:T(8,128)(2,1)S(1)}, u32[]{:S(2)}, u32[]{:S(2)}) collective-permute-start(bf16[240,512]{1,0:T(8,128)(2,1)S(1)} %get-tuple-element.23), channel_id=1, source_target_pairs={{0,2},{2,0},{1,3},{3,1},{4,6},{6,4},{5,7},{7,5},{8,10},{10,8},{9,1... | collective-permute-start | bytes 737288 | tf_op jit(solution)/shard_map/ppermute | solution.py:427
  27.4 2.5 %shard_map.95.rest_0_.base_ref = f32[240,2048]{1,0:T(8,128)S(1)} custom-call(bf16[8,64,240]{2,1,0:T(8,128)(2,1)S(1)} %get-tuple-element.25.rows_ref, bf16[240,1024]{1,0:T(8,128)(2,1)S(1)} %get-tuple-element.19.table_ref, bf16[256,512]{1,0:T(8,128)(2,1)S(1)} %get-tuple-element.26.wide_ref, f32[8,128]{1,0:T(8,128)S(1)} %get-tuple-element.27.cls_ref), custom_call_target="tpu_custom_call" | custom-call | flops 1887436800 | bytes 3932160 | tf_op jit(solution)/shard_map/pallas_call | solution.py:443
  29.9 0.0 collective-permute-done.2.rows_ref
  29.9 2.5 %shard_map.96.rest_1_.base_ref = f32[240,2048]{1,0:T(8,128)S(1)} custom-call(bf16[8,64,240]{2,1,0:T(8,128)(2,1)S(1)} %collective-permute-done.2.rows_ref, bf16[240,1024]{1,0:T(8,128)(2,1)S(1)} %get-tuple-element.19.table_ref, bf16[256,512]{1,0:T(8,128)(2,1)S(1)} %get-tuple-element.26.wide_ref, f32[8,128]{1,0:T(8,128)S(1)} %get-tuple-element.27.cls_ref), custom_call_target="tpu_custom_call" | custom-call | flops 1887436800 | bytes 3932160 | tf_op jit(solution)/shard_map/pallas_call | solution.py:443
  32.4 1.3 %collective-permute-done.1.inflow_ref = bf16[240,512]{1,0:T(8,128)(2,1)S(1)} collective-permute-done((bf16[240,512]{1,0:T(8,128)(2,1)S(1)}, bf16[240,512]{1,0:T(8,128)(2,1)S(1)}, u32[]{:S(2)}, u32[]{:S(2)}) %collective-permute-start.1) | collective-permute-done | bytes 245792 | tf_op jit(solution)/shard_map/ppermute | solution.py:427
  33.7 0.8 %shard_map.97 = (bf16[240,512]{1,0:T(8,128)(2,1)S(1)}, bf16[240,512]{1,0:T(8,128)(2,1)S(1)}) custom-call(s32[1]{0:T(128)} %bitcast.core_ref, s32[1]{0:T(128)} %bitcast.1.valid_ref, bf16[240,512]{1,0:T(8,128)(2,1)S(1)} %collective-permute-done.1.inflow_ref, bf16[240,1024]{1,0:T(8,128)(2,1)S(1)} %get-tuple-element.19.table_ref, ...), custom_call_target="tpu_custom_call" | custom-call | flops 471859200 | bytes 983040 | tf_op jit(solution)/shard_map/pallas_call | solution.py:453
  34.5 0.9 %collective-permute-start.3 = (bf16[240,512]{1,0:T(8,128)(2,1)S(1)}, bf16[240,512]{1,0:T(8,128)(2,1)S(1)}, u32[]{:S(2)}, u32[]{:S(2)}) collective-permute-start(bf16[240,512]{1,0:T(8,128)(2,1)S(1)} %get-tuple-element.32), channel_id=1, source_target_pairs={{0,1},{1,0},{2,3},{3,2},{4,5},{5,4},{6,7},{7,6},{8,9},{9,8},{10,11... | collective-permute-start | bytes 737288 | tf_op jit(solution)/shard_map/ppermute | solution.py:460
  35.4 1.3 %shard_map.98.done_ref = bf16[240,16,128]{2,1,0:T(8,128)(2,1)S(1)} custom-call(bf16[240,512]{1,0:T(8,128)(2,1)S(1)} %get-tuple-element.29.inflow_ref, f32[240,2048]{1,0:T(8,128)S(1)} %shard_map.95.rest_0_.base_ref, bf16[240,1024]{1,0:T(8,128)(2,1)S(1)} %get-tuple-element.19.table_ref, bf16[256,512]{1,0:T(8,128)(2,1)S(1)} %get-tuple-element.30.link_ref, ...), custom_call_target="tpu_custom_call" | custom-call | flops 943718400 | bytes 1966080 | tf_op jit(solution)/shard_map/pallas_call | solution.py:464
  36.7 0.0 collective-permute-done.3.inflow_ref
  36.7 2.1 %shard_map.99 = bf16[240,32,128]{2,1,0:T(8,128)(2,1)} custom-call(s32[1]{0:T(128)} %bitcast.core_ref, bf16[240,16,128]{2,1,0:T(8,128)(2,1)S(1)} %shard_map.98.done_ref, bf16[240,512]{1,0:T(8,128)(2,1)S(1)} %collective-permute-done.3.inflow_ref, f32[240,2048]{1,0:T(8,128)S(1)} %shard_map.96.rest_1_.base_ref, ...), custom_call_target="tpu_custom_call" | custom-call | flops 943718400 | bytes 3932160 | tf_op jit(solution)/shard_map/pallas_call | solution.py:472
  (1 shorter events, 0.0 us)
Async XLA Ops:
  0.0 9.7 %copy-start = (s32[1,1,32,128]{3,2,1,0:T(8,128)S(1)}, s32[1,1,32,128]{3,2,1,0:T(8,128)}, u32[]{:S(2)}) copy-start(s32[1,1,32,128]{3,2,1,0:T(8,128)} %param.17) | copy-start | bytes 49156
  0.0 9.7 %copy-start.5 = (s32[1,1,32]{2,1,0:T(1,128)S(1)}, s32[1,1,32]{2,1,0:T(1,128)}, u32[]{:S(2)}) copy-start(s32[1,1,32]{2,1,0:T(1,128)} %param.16) | copy-start | bytes 388
  0.0 9.7 %copy-start.4 = (s32[128,1]{0,1:T(1,128)S(1)}, s32[128,1]{0,1:T(1,128)}, u32[]{:S(2)}) copy-start(s32[128,1]{0,1:T(1,128)} %param.13) | copy-start | bytes 1540
  0.0 9.7 %copy-start.3 = (f32[128,4]{0,1:T(4,128)S(1)}, f32[128,4]{0,1:T(4,128)}, u32[]{:S(2)}) copy-start(f32[128,4]{0,1:T(4,128)} %param.12) | copy-start | bytes 6148
  0.0 9.7 %copy-start.2 = (s32[128,4]{0,1:T(4,128)S(1)}, s32[128,4]{0,1:T(4,128)}, u32[]{:S(2)}) copy-start(s32[128,4]{0,1:T(4,128)} %param.11) | copy-start | bytes 6148
  0.0 11.0 %copy-start.6 = (f32[8]{0:T(128)S(1)}, f32[8]{0:T(128)}, u32[]{:S(2)}) copy-start(f32[8]{0:T(128)} %param.15) | copy-start | bytes 100
  0.0 11.0 %copy-start.1 = (f32[8,240]{1,0:T(8,128)S(1)}, f32[8,240]{1,0:T(8,128)}, u32[]{:S(2)}) copy-start(f32[8,240]{1,0:T(8,128)} %shape_ref.1) | copy-start | bytes 23044
  2.4 21.4 %all-to-all-start = ((bf16[16,64,240]{2,1,0:T(8,128)(2,1)}), bf16[16,64,240]{2,1,0:T(8,128)(2,1)S(1)}, u32[]{:S(2)}, u32[]{:S(2)}) async-start(bf16[16,64,240]{2,1,0:T(8,128)(2,1)} %bitcast.19), calls=%async_computation | async-start | bytes 1048576 | tf_op jit(solution)/shard_map/all_to_all | solution.py:381
  9.8 1.3 %collective-permute-start = (f32[64,128]{1,0:T(8,128)S(1)}, f32[64,128]{1,0:T(8,128)S(1)}, u32[]{:S(2)}, u32[]{:S(2)}) collective-permute-start(f32[64,128]{1,0:T(8,128)S(1)} %shard_map.92.own_ref), channel_id=1, source_target_pairs={{0,1},{1,0},{2,3},{3,2},{4,5},{5,4},{6,7},{7,6},{8,9},{9,8},{10,11... | collective-permute-start | bytes 98312 | tf_op jit(solution)/shard_map/ppermute | solution.py:397
  25.7 4.2 %collective-permute-start.2 = (bf16[8,64,240]{2,1,0:T(8,128)(2,1)S(1)}, bf16[8,64,240]{2,1,0:T(8,128)(2,1)S(1)}, u32[]{:S(2)}, u32[]{:S(2)}) collective-permute-start(bf16[8,64,240]{2,1,0:T(8,128)(2,1)S(1)} %get-tuple-element.28), channel_id=1, source_target_pairs={{0,1},{1,0},{2,3},{3,2},{4,5},{5,4},{6,7},{7,6},{8,9},{9,8},{10,11... | collective-permute-start | bytes 737288 | tf_op jit(solution)/shard_map/ppermute | solution.py:440
  26.2 7.6 %collective-permute-start.1 = (bf16[240,512]{1,0:T(8,128)(2,1)S(1)}, bf16[240,512]{1,0:T(8,128)(2,1)S(1)}, u32[]{:S(2)}, u32[]{:S(2)}) collective-permute-start(bf16[240,512]{1,0:T(8,128)(2,1)S(1)} %get-tuple-element.23), channel_id=1, source_target_pairs={{0,2},{2,0},{1,3},{3,1},{4,6},{6,4},{5,7},{7,5},{8,10},{10,8},{9,1... | collective-permute-start | bytes 737288 | tf_op jit(solution)/shard_map/ppermute | solution.py:427
  34.5 2.2 %collective-permute-start.3 = (bf16[240,512]{1,0:T(8,128)(2,1)S(1)}, bf16[240,512]{1,0:T(8,128)(2,1)S(1)}, u32[]{:S(2)}, u32[]{:S(2)}) collective-permute-start(bf16[240,512]{1,0:T(8,128)(2,1)S(1)} %get-tuple-element.32), channel_id=1, source_target_pairs={{0,1},{1,0},{2,3},{3,2},{4,5},{5,4},{6,7},{7,6},{8,9},{9,8},{10,11... | collective-permute-start | bytes 737288 | tf_op jit(solution)/shard_map/ppermute | solution.py:460

commit v5 on v4

--- a/solution.py
+++ b/solution.py
@@ -11,6 +11,8 @@
 MB = 8
 SUB = 4
 LANES = 128
+BLOCK = 64
+CHUNK = 256
 VMEM_LIMIT = 20 * 1024 * 1024
 FULL_VMEM = 56 * 1024 * 1024
 
@@ -36,13 +38,12 @@
     return high, (value - high.astype(F32)).astype(BF)
 
 
-def call(kernel, out_shape, flops, limit=VMEM_LIMIT, **extra):
-    nbytes = sum(s.size * s.dtype.itemsize for s in jax.tree.leaves(out_shape))
+def call(kernel, out_shape, limit=VMEM_LIMIT, **extra):
     return pl.pallas_call(
         kernel,
         out_shape=out_shape,
         compiler_params=pltpu.CompilerParams(vmem_limit_bytes=limit),
-        cost_estimate=pl.CostEstimate(flops=flops, bytes_accessed=2 * nbytes, transcendentals=0),
+        cost_estimate=pl.CostEstimate(flops=1, bytes_accessed=1, transcendentals=0),
         **extra,
     )
 
@@ -55,21 +56,25 @@
 
 
 def convolve(table, value, classes, class_count):
-    hours = table.shape[0]
-    masks = [one_hot(classes == float(k)) for k in range(class_count)]
-    total = None
-    for start in range(0, hours, LANES):
-        block = value[start : start + LANES]
-        short = LANES - block.shape[0]
-        if short:
-            block = jnp.concatenate([block, jnp.zeros((short, block.shape[1]), BF)], axis=0)
-        parts = jnp.concatenate([block * mask for mask in masks], axis=0)
-        added = mm(table[: hours - start], parts)
-        if start == 0:
-            total = added
-        else:
-            total = jnp.concatenate([total[:start], total[start:] + added], axis=0)
-    return total
+    hours, width = value.shape
+    columns = []
+    for begin in range(0, width, CHUNK):
+        cut = slice(begin, min(begin + CHUNK, width))
+        masks = [one_hot(classes[:, cut] == float(k)) for k in range(class_count)]
+        total = None
+        for start in range(0, hours, BLOCK):
+            block = value[start : start + BLOCK, cut]
+            short = BLOCK - block.shape[0]
+            if short:
+                block = jnp.concatenate([block, jnp.zeros((short, block.shape[1]), BF)], axis=0)
+            parts = jnp.concatenate([block * mask for mask in masks], axis=0)
+            added = mm(table[: hours - start], parts)
+            if start == 0:
+                total = added
+            else:
+                total = jnp.concatenate([total[:start], total[start:] + added], axis=0)
+        columns.append(total)
+    return jnp.concatenate(columns, axis=1)
 
 
 def pack_kernel(slot, x_ref, rows_ref, send_ref, held, rows_held, ready, arrived, sent):
@@ -144,13 +149,13 @@
     hydro = (rate * shape_ref[...] * jnp.exp(-rate * lag)).astype(BF)
     reverse = one_hot((iota((hours, padded), 0) + iota((hours, padded), 1)) % padded == 0)
     turned = mm(hydro, reverse)
-    later = iota((padded, LANES), 1) <= iota((padded, LANES), 0)
+    later = iota((padded, BLOCK), 1) <= iota((padded, BLOCK), 0)
     for k in range(class_count):
         rolled = pltpu.roll(
             jnp.broadcast_to(turned[k : k + 1, :], (padded, padded)), 0, 1, stride=1, stride_axis=0
         )
-        rolled = jnp.where(later, rolled[:, :LANES], 0.0)
-        table_ref[:, k * LANES : (k + 1) * LANES] = rolled[:hours].astype(BF)
+        rolled = jnp.where(later, rolled[:, :BLOCK], 0.0)
+        table_ref[:, k * BLOCK : (k + 1) * BLOCK] = rolled[:hours].astype(BF)
 
     row_p = iota((kap, recv), 0)
     expand = one_hot((row_p // per) * slot + row_p % slot == iota((kap, recv), 1))
@@ -221,17 +226,12 @@
     return jnp.concatenate([classes] * (width // classes.shape[1]), axis=1)
 
 
-def head_kernel(
-    class_count, core_ref, rows_ref, table_ref, mix_ref, pass_ref, cls_ref,
-    even_ref, odd_ref, panel_ref, own_ref, send_ref,
-):
-    first = core_ref[0] == 0
-    rows = [rows_ref[:, level] for level in range(2)]
-    own_ref[...] = jnp.where(first, rows[0], rows[1])
-    send_ref[...] = jnp.where(first, rows[1], rows[0])
+def head_kernel(class_count, core_ref, rows_ref, table_ref, mix_ref, pass_ref, cls_ref, *outs):
+    panel_ref, even_ref, first_ref, send_ref = outs[:4]
     regions, _, total, _ = rows_ref.shape
     size = mix_ref.shape[1] // 2 // regions
-    wide = even_ref.shape[1]
+    wide = panel_ref.shape[1]
+    classes = [tiled(cls_ref[level, 0:1, :], wide) for level in range(2)]
     lateral = [
         jnp.concatenate(
             [
@@ -242,12 +242,15 @@
         )
         for level in range(2)
     ]
-    classes = [tiled(cls_ref[level, 0:1, :], wide) for level in range(2)]
     even = convolve(table_ref[...], lateral[0].astype(BF), classes[0], class_count)
     even_ref[...] = even
-    odd_ref[...] = lateral[1]
-    inflow = lateral[1] + pass_on(even.astype(BF), pass_ref[1]).astype(F32)
+    first = even.astype(BF)
+    first_ref[...] = first
+    inflow = lateral[1] + pass_on(first, pass_ref[1]).astype(F32)
     panel_ref[...] = convolve(table_ref[...], inflow.astype(BF), classes[1], class_count).astype(BF)
+    send_ref[...] = jnp.where(core_ref[0] == 0, rows_ref[:, 1], rows_ref[:, 0])
+    if len(outs) > 4:
+        outs[4][...] = lateral[1]
 
 
 def hop_kernel(class_count, inflow_ref, table_ref, pass_ref, cls_ref, even_ref, odd_ref, panel_ref):
@@ -258,33 +261,49 @@
     panel_ref[...] = convolve(table_ref[...], moved.astype(BF), classes[1], class_count).astype(BF)
 
 
-def last_hop_kernel(class_count, core_ref, valid_ref, inflow_ref, table_ref, pass_ref, cls_ref, even_ref, *rest):
+def last_hop_kernel(class_count, core_ref, pair_ref, inflow_ref, table_ref, pass_ref, cls_ref, even_ref, *rest):
     own_ref, send_ref = rest[-2:]
-    arrived = jnp.where(valid_ref[0] == 1, inflow_ref[...], jnp.zeros((), BF))
-    classes = tiled(cls_ref[0, 0:1, :], even_ref.shape[1])
-    moved = pass_on(arrived, pass_ref[0])
-    even = even_ref[...] + convolve(table_ref[...], moved, classes, class_count)
-    even = even.astype(BF)
-    first = core_ref[0] == 0
-    own_ref[...] = jnp.where(first, arrived, even)
-    send_ref[...] = jnp.where(first, even, arrived)
-
-
-def base_kernel(class_count, rows_ref, table_ref, wide_ref, cls_ref, base_ref):
+
+    @pl.when(pair_ref[0] > 0)
+    def _():
+        arrived = inflow_ref[...]
+        classes = tiled(cls_ref[0, 0:1, :], even_ref.shape[1])
+        moved = pass_on(arrived, pass_ref[0])
+        even = even_ref[...] + convolve(table_ref[...], moved, classes, class_count)
+        even = even.astype(BF)
+        first = core_ref[0] == 0
+        own_ref[...] = jnp.where(first, arrived, even)
+        send_ref[...] = jnp.where(first, even, arrived)
+
+
+def base_kernel(class_count, core_ref, rows_ref, table_ref, wide_ref, cls_ref, base_ref):
+    if len(rows_ref.shape) == 4:
+        rows_ref = rows_ref.at[:, core_ref[0]]
     regions, total, _ = rows_ref.shape
     size = wide_ref.shape[0] // 2 // regions
     width = wide_ref.shape[1]
-    classes = tiled(cls_ref[0:1, :], width)
+    step = max(cls_ref.shape[1], 256)
+    classes = tiled(cls_ref[0:1, :], step)
     for sub in range(total // size):
-        lateral = tmm(twice(rows_ref, sub, size), wide_ref[...]).astype(BF)
-        base_ref[:, sub * width : (sub + 1) * width] = convolve(
-            table_ref[...], lateral, classes, class_count
-        )
-
-
-def routed_parts(class_count, inflow_ref, table_ref, cls_ref):
-    classes = tiled(cls_ref[0:1, :], inflow_ref.shape[1])
-    return split(convolve(table_ref[...], inflow_ref[...], classes, class_count))
+        rows = twice(rows_ref, sub, size)
+        for start in range(0, width, step):
+            lateral = tmm(rows, wide_ref[:, start : start + step]).astype(BF)
+            place = sub * width + start
+            base_ref[:, place : place + step] = convolve(
+                table_ref[...], lateral, classes, class_count
+            )
+
+
+def routed_parts(class_count, top, core_ref, inflow_ref, table_ref, cls_ref):
+    inflow = inflow_ref[...]
+    if top:
+        inflow = jnp.where(core_ref[0] == 0, jnp.zeros((), BF), inflow)
+    classes = tiled(cls_ref[0:1, :], inflow.shape[1])
+    return split(convolve(table_ref[...], inflow, classes, class_count))
+
+
+def mine(top, pair_ref):
+    return pl.when((pair_ref[0] == 0) == top)
 
 
 def assemble(hours, high, low, base_ref, link_ref, scratch, members, reaches):
@@ -303,39 +322,49 @@
     return flow.reshape(count, members, reaches).astype(BF)
 
 
-def early_kernel(class_count, inflow_ref, base_ref, table_ref, link_ref, cls_ref, out_ref, scratch):
+def early_kernel(
+    class_count, top, core_ref, pair_ref, inflow_ref, base_ref, table_ref, link_ref, cls_ref,
+    out_ref, scratch,
+):
     hours, members, reaches = out_ref.shape
-    high, low = routed_parts(class_count, inflow_ref, table_ref, cls_ref)
-    out_ref[...] = assemble(
-        slice(0, hours), high, low, base_ref, link_ref, scratch, members, reaches
-    )
+
+    @mine(top, pair_ref)
+    def _():
+        high, low = routed_parts(class_count, top, core_ref, inflow_ref, table_ref, cls_ref)
+        out_ref[...] = assemble(
+            slice(0, hours), high, low, base_ref, link_ref, scratch, members, reaches
+        )
 
 
 def late_kernel(
-    class_count, core_ref, done_ref, inflow_ref, base_ref, table_ref, link_ref, cls_ref,
-    out_ref, scratch, ready, sems,
+    class_count, top, core_ref, pair_ref, done_ref, inflow_ref, base_ref, table_ref, link_ref,
+    cls_ref, *rest,
 ):
+    out_ref, scratch, ready, sems = rest[-4:]
     hours, members, reaches = done_ref.shape
-    core = core_ref[0]
-
-    def place(which):
-        return pl.ds(pl.multiple_of(which * members, members), members)
-
-    copies = [pltpu.make_async_copy(done_ref, out_ref.at[:, place(core)], sems.at[0])]
-    copies[0].start()
-    high, low = routed_parts(class_count, inflow_ref, table_ref, cls_ref)
-    for start in range(0, hours, LANES):
-        part = slice(start, min(start + LANES, hours))
-        ready[part] = assemble(part, high, low, base_ref, link_ref, scratch, members, reaches)
-        span = pl.ds(start, part.stop - start)
-        copies.append(
-            pltpu.make_async_copy(
-                ready.at[span], out_ref.at[span, place(1 - core)], sems.at[len(copies)]
+
+    @mine(top, pair_ref)
+    def _():
+        core = core_ref[0]
+
+        def place(which):
+            return pl.ds(pl.multiple_of(which * members, members), members)
+
+        copies = [pltpu.make_async_copy(done_ref, out_ref.at[:, place(core)], sems.at[0])]
+        copies[0].start()
+        high, low = routed_parts(class_count, top, core_ref, inflow_ref, table_ref, cls_ref)
+        for start in range(0, hours, LANES):
+            part = slice(start, min(start + LANES, hours))
+            ready[part] = assemble(part, high, low, base_ref, link_ref, scratch, members, reaches)
+            span = pl.ds(start, part.stop - start)
+            copies.append(
+                pltpu.make_async_copy(
+                    ready.at[span], out_ref.at[span, place(1 - core)], sems.at[len(copies)]
+                )
             )
-        )
-        copies[-1].start()
-    for copy in copies:
-        copy.wait()
+            copies[-1].start()
+        for copy in copies:
+            copy.wait()
 
 
 def local(
@@ -355,10 +384,9 @@
     core = lax.axis_index("core").astype(jnp.int32)
     core_arg = core.reshape(1)
     pair = lax.axis_index("pair")
-    valid = (pair > 0).astype(jnp.int32).reshape(1)
+    pair_arg = pair.astype(jnp.int32).reshape(1)
     swap = [(0, 1), (1, 0)]
     anywhere = pl.BlockSpec(memory_space=pl.ANY)
-    conv_flops = 2 * hours * class_count * hours * wide
 
     def struct(shape, dtype):
         return jax.ShapeDtypeStruct(shape, dtype)
@@ -366,7 +394,6 @@
     send = call(
         functools.partial(pack_kernel, slot),
         struct((regions, 2, half * slot, hours), BF),
-        2 * recv * MB * grid * hours * members,
         limit=FULL_VMEM,
         in_specs=[anywhere] * 2,
         out_specs=anywhere,
@@ -384,7 +411,6 @@
     raw = call(
         raw_kernel,
         struct((32 + outs, reaches), F32),
-        1000,
         in_specs=vmem(5),
         out_specs=vmem(1)[0],
     )(
@@ -398,7 +424,7 @@
     table, mix, passing, cls_out, wide_mix, link, cls_target, cls_own = call(
         functools.partial(prep_kernel, slot, columns),
         (
-            struct((hours, class_count * LANES), BF),
+            struct((hours, class_count * BLOCK), BF),
             struct((2, 2 * kap, SUB * outs), BF),
             struct((2, MB * outs, MB * outs), BF),
             struct((2, 8, MB * outs), F32),
@@ -407,80 +433,82 @@
             struct((8, MB * outs), F32),
             struct((8, reaches), F32),
         ),
-        10_000_000,
         in_specs=[SCALAR] + vmem(4),
         out_specs=tuple(vmem(8)),
     )(core_arg, raw, other, kernel_rate.reshape(1, class_count), kernel_shape)
 
     panel_shape = struct((hours, wide), BF)
-    rows_shape = struct((regions, half * slot, hours), BF)
-    even, odd, panel, rows_own, rows_send = call(
+    float_shape = struct((hours, wide), F32)
+    shapes = [panel_shape, float_shape, panel_shape, struct((regions, half * slot, hours), BF)]
+    if pairs > 2:
+        shapes.append(float_shape)
+    heads = call(
         functools.partial(head_kernel, class_count),
-        (struct((hours, wide), F32), struct((hours, wide), F32), panel_shape, rows_shape, rows_shape),
-        2 * conv_flops,
+        tuple(shapes),
         in_specs=[SCALAR] + vmem(5),
-        out_specs=tuple(vmem(5)),
+        out_specs=tuple(vmem(len(shapes))),
     )(core_arg, received, table, mix, passing, cls_out)
+    panel, even, first, rows_send = heads[:4]
 
     inflow = jnp.zeros(panel_shape.shape, BF)
     for step in range(pairs - 1):
         arrived = lax.ppermute(panel, "pair", [(step, step + 1), (step + 1, step)])
-        if pairs == 2:
-            inflow = arrived
-        else:
-            inflow = jnp.where(pair == step + 1, arrived, inflow)
+        inflow = arrived if pairs == 2 else jnp.where(pair == step + 1, arrived, inflow)
         if step < pairs - 2:
             panel = call(
                 functools.partial(hop_kernel, class_count),
                 panel_shape,
-                2 * conv_flops,
                 in_specs=vmem(6),
                 out_specs=vmem(1)[0],
-            )(inflow, table, passing, cls_out, even, odd)
-    rows_other = lax.ppermute(rows_send, "core", swap)
+            )(inflow, table, passing, cls_out, even, heads[4])
 
     def base(rows):
         return call(
             functools.partial(base_kernel, class_count),
             struct((hours, half * reaches), F32),
-            conv_flops * reaches // outs,
-            in_specs=vmem(4),
+            in_specs=[SCALAR] + vmem(4),
             out_specs=vmem(1)[0],
-        )(rows, table, wide_mix, cls_own)
-
-    base_own = base(rows_own)
+        )(core_arg, rows, table, wide_mix, cls_own)
+
+    flat = pltpu.VMEM((hours * half, reaches), F32)
+    rows_other = lax.ppermute(rows_send, "core", swap)
+    first_other = lax.ppermute(first, "core", swap)
+    base_own = base(received)
     base_other = base(rows_other)
+
+    def early(top, own):
+        return call(
+            functools.partial(early_kernel, class_count, top),
+            struct((hours, half, reaches), BF),
+            in_specs=[SCALAR] * 2 + vmem(5),
+            out_specs=vmem(1)[0],
+            scratch_shapes=[flat],
+        )(core_arg, pair_arg, own, base_own, table, link, cls_target)
+
+    def late(top, done, gotten, before):
+        return call(
+            functools.partial(late_kernel, class_count, top),
+            struct((hours, members, reaches), BF),
+            in_specs=[SCALAR] * 2 + vmem(6) + [anywhere] * len(before),
+            out_specs=anywhere,
+            scratch_shapes=[
+                flat,
+                pltpu.VMEM((hours, half, reaches), BF),
+                pltpu.SemaphoreType.DMA((1 + -(-hours // LANES),)),
+            ],
+            input_output_aliases={8: 0} if before else {},
+        )(core_arg, pair_arg, done, gotten, base_other, table, link, cls_target, *before)
+
+    done_first = early(True, first)
     own, given = call(
         functools.partial(last_hop_kernel, class_count),
         (panel_shape, panel_shape),
-        conv_flops,
         in_specs=[SCALAR] * 2 + vmem(5) + [anywhere] * 2,
         out_specs=tuple(vmem(2)),
-    )(core_arg, valid, inflow, table, passing, cls_out, even, base_own, base_other)
+    )(core_arg, pair_arg, inflow, table, passing, cls_out, even, done_first, base_other)
     gotten = lax.ppermute(given, "core", swap)
-
-    flow_shape = struct((hours, half, reaches), BF)
-    flat = pltpu.VMEM((hours * half, reaches), F32)
-    done = call(
-        functools.partial(early_kernel, class_count),
-        flow_shape,
-        2 * conv_flops,
-        in_specs=vmem(5),
-        out_specs=vmem(1)[0],
-        scratch_shapes=[flat],
-    )(own, base_own, table, link, cls_target)
-    return call(
-        functools.partial(late_kernel, class_count),
-        struct((hours, members, reaches), BF),
-        2 * conv_flops,
-        in_specs=[SCALAR] + vmem(6),
-        out_specs=anywhere,
-        scratch_shapes=[
-            flat,
-            pltpu.VMEM((hours, half, reaches), BF),
-            pltpu.SemaphoreType.DMA((1 + -(-hours // LANES),)),
-        ],
-    )(core_arg, done, gotten, base_other, table, link, cls_target)
+    out = late(True, done_first, first_other, [])
+    return late(False, early(False, own), gotten, [out])
 
 
 def solution(mesh):

time: 39.2 us -> 37.7 us (0.962)
  the two profiles are of different devices: /device:TPU:1 before, /device:TPU:5 now
where the time goes in v5:
time: 37.7 us; the launch traced here: 37.5 us
  waiting for transfers between devices  15 us (40%)
  Pallas kernels  13.6 us (36%)
  starting transfers between devices  8.73 us (23%)
    all_to_all x1, waiting for transfers between devices, local(): lax.all_to_all(send.reshape(regions * 2, half * slot, hours), ('region',...  11.6 us
    all_to_all x1, starting transfers between devices, local(): lax.all_to_all(send.reshape(regions * 2, half * slot, hours), ('region',...  6.51 us
    pallas_call x2, Pallas kernels, base(): call(functools.partial(base_kernel, class_count), struct((hours, half * r...  4.69 us
    pallas_call x1, Pallas kernels, local(): call(functools.partial(pack_kernel, slot), struct((regions, 2, half * slo...  2.32 us
    ppermute x1, waiting for transfers between devices, local(): arrived = lax.ppermute(panel, 'pair', [(step, step + 1), (step + 1, step)])  2.24 us
    pallas_call x2, Pallas kernels, late(): call(functools.partial(late_kernel, class_count, top), struct((hours, mem...  2.16 us
    pallas_call x1, Pallas kernels, local(): call(functools.partial(head_kernel, class_count), tuple(shapes), in_specs...  1.35 us
    pallas_call x2, Pallas kernels, early(): call(functools.partial(early_kernel, class_count, top), struct((hours, ha...  1.27 us
  transfers between devices with their start and end apart: 6, of which 3 were waited for; matrix products, arithmetic and copies ran while one was open for 0% of the time, Pallas kernels for 21%

profile of v5, /device:TPU:5, one launch (start us, length us, event | category | flops | bytes accessed | tf_op | source)
XLA Modules:
  0.0 37.5 jit_solution(15001350985881774508)
XLA Ops:
  0.0 0.0 copy-start
  0.0 0.0 copy-start.3
  0.0 0.0 copy-start.2
  0.0 0.0 copy-start.6
  0.0 0.0 copy-start.1
  0.0 2.3 %shard_map.91 = bf16[8,2,64,240]{3,2,1,0:T(8,128)(2,1)} custom-call(f32[32,32,240]{2,1,0:T(8,128)} %bitcast.21, s32[1,32]{1,0:T(1,128)} %bitcast.22), custom_call_target="tpu_custom_call" | custom-call | flops 1 | bytes 1 | tf_op jit(solution)/shard_map/pallas_call | solution.py:394
  2.4 6.5 %all-to-all-start = ((bf16[16,64,240]{2,1,0:T(8,128)(2,1)}), bf16[16,64,240]{2,1,0:T(8,128)(2,1)S(1)}, u32[]{:S(2)}, u32[]{:S(2)}) async-start(bf16[16,64,240]{2,1,0:T(8,128)(2,1)} %bitcast.20), calls=%async_computation | async-start | bytes 1048576 | tf_op jit(solution)/shard_map/all_to_all | solution.py:408
  8.9 0.0 copy-done
  8.9 0.0 copy-done.5
  8.9 0.0 copy-done.4
  8.9 0.0 copy-done.3
  8.9 0.0 copy-done.2
  8.9 0.2 collective-permute-start
  9.1 1.1 %collective-permute-done.other_ref = f32[64,128]{1,0:T(8,128)S(1)} collective-permute-done((f32[64,128]{1,0:T(8,128)S(1)}, f32[64,128]{1,0:T(8,128)S(1)}, u32[]{:S(2)}, u32[]{:S(2)}) %collective-permute-start) | collective-permute-done | bytes 32800 | tf_op jit(solution)/shard_map/ppermute | solution.py:423
  10.2 0.0 copy-done.6
  10.2 0.0 copy-done.1
  10.2 1.1 %shard_map.93 = (bf16[240,512]{1,0:T(8,128)(2,1)S(1)}, bf16[2,256,128]{2,1,0:T(8,128)(2,1)S(1)}, bf16[2,256,256]{2,1,0:T(8,128)(2,1)S(1)}, f32[2,8,256]{2,1,0:T(...) custom-call(s32[1]{0:T(128)} %bitcast.core_ref, ...), custom_call_target="tpu_custom_call" | custom-call | flops 1 | bytes 1 | tf_op jit(solution)/shard_map/pallas_call | solution.py:424
  11.3 11.6 %all-to-all-done = bf16[16,64,240]{2,1,0:T(8,128)(2,1)S(1)} async-done(((bf16[16,64,240]{2,1,0:T(8,128)(2,1)}), bf16[16,64,240]{2,1,0:T(8,128)(2,1)S(1)}, u32[]{:S(2)}, u32[]{:S(2)}) %all-to-all-start) | async-done | bytes 491552 | tf_op jit(solution)/shard_map/all_to_all | solution.py:408
  23.0 1.3 %shard_map.94 = (bf16[240,512]{1,0:T(8,128)(2,1)S(1)}, f32[240,512]{1,0:T(8,128)S(1)}, bf16[240,512]{1,0:T(8,128)(2,1)S(1)}, bf16[8,64,240]{2,1,0:T(8,128)(2,1)S(1)}) custom-call(s32[1]{0:T(128)} %bitcast.core_ref, bf16[8,2,64,240]{3,2,1,0:T(8,128)(2,1)S(1)} %bitcast.12, bf16[240,512]{1,0:T(8,128)(2,1)S(1)} %get-tuple-element.19.table_ref, ...), custom_call_target="tpu_custom_call" | custom-call | flops 1 | bytes 1 | tf_op jit(solution)/shard_map/pallas_call | solution.py:445
  24.3 0.6 %collective-permute-start.2 = (bf16[8,64,240]{2,1,0:T(8,128)(2,1)S(1)}, bf16[8,64,240]{2,1,0:T(8,128)(2,1)S(1)}, u32[]{:S(2)}, u32[]{:S(2)}) collective-permute-start(bf16[8,64,240]{2,1,0:T(8,128)(2,1)S(1)} %get-tuple-element.30), channel_id=1, source_target_pairs={{0,1},{1,0},{2,3},{3,2},{4,5},{5,4},{6,7},{7,6},{8,9},{9,8},{10,11... | collective-permute-start | bytes 737288 | tf_op jit(solution)/shard_map/ppermute | solution.py:474
  24.9 0.2 collective-permute-start.1
  25.1 0.3 collective-permute-start.4
  25.5 2.3 %shard_map.95.base_ref = f32[240,2048]{1,0:T(8,128)S(1)} custom-call(s32[1]{0:T(128)} %bitcast.core_ref, bf16[8,2,64,240]{3,2,1,0:T(8,128)(2,1)S(1)} %bitcast.13, bf16[240,512]{1,0:T(8,128)(2,1)S(1)} %get-tuple-element.19.table_ref, bf16[256,512]{1,0:T(8,128)(2,1)S(1)} %get-tuple-element.26.wide_ref, f32[8,128]{1,0:T(8,128)S(1)} %get-tuple-element.27.cls_ref), custom_call_target="tpu_custom_call" | custom-call | flops 1 | bytes 1 | tf_op jit(solution)/shard_map/pallas_call | solution.py:466
  27.8 0.0 collective-permute-done.2.rows_ref
  27.8 2.3 %shard_map.97.rest_1_.base_ref = f32[240,2048]{1,0:T(8,128)S(1)} custom-call(s32[1]{0:T(128)} %bitcast.core_ref, bf16[8,64,240]{2,1,0:T(8,128)(2,1)S(1)} %collective-permute-done.2.rows_ref, bf16[240,512]{1,0:T(8,128)(2,1)S(1)} %get-tuple-element.19.table_ref, bf16[256,512]{1,0:T(8,128)(2,1)S(1)} %get-tuple-element.26.wide_ref, ...), custom_call_target="tpu_custom_call" | custom-call | flops 1 | bytes 1 | tf_op jit(solution)/shard_map/pallas_call | solution.py:466
  30.2 2.2 %collective-permute-done.1.inflow_ref = bf16[240,512]{1,0:T(8,128)(2,1)S(1)} collective-permute-done((bf16[240,512]{1,0:T(8,128)(2,1)S(1)}, bf16[240,512]{1,0:T(8,128)(2,1)S(1)}, u32[]{:S(2)}, u32[]{:S(2)}) %collective-permute-start.1) | collective-permute-done | bytes 245792 | tf_op jit(solution)/shard_map/ppermute | solution.py:455
  32.4 0.7 %shard_map.98 = (bf16[240,512]{1,0:T(8,128)(2,1)S(1)}, bf16[240,512]{1,0:T(8,128)(2,1)S(1)}) custom-call(s32[1]{0:T(128)} %bitcast.core_ref, s32[1]{0:T(128)} %bitcast.1.pair_ref, bf16[240,512]{1,0:T(8,128)(2,1)S(1)} %collective-permute-done.1.inflow_ref, bf16[240,512]{1,0:T(8,128)(2,1)S(1)} %get-tuple-element.19.table_ref, ...), custom_call_target="tpu_custom_call" | custom-call | flops 1 | bytes 1 | tf_op jit(solution)/shard_map/pallas_call | solution.py:503
  33.1 0.9 %collective-permute-start.3 = (bf16[240,512]{1,0:T(8,128)(2,1)S(1)}, bf16[240,512]{1,0:T(8,128)(2,1)S(1)}, u32[]{:S(2)}, u32[]{:S(2)}) collective-permute-start(bf16[240,512]{1,0:T(8,128)(2,1)S(1)} %get-tuple-element.32), channel_id=1, source_target_pairs={{0,1},{1,0},{2,3},{3,2},{4,5},{5,4},{6,7},{7,6},{8,9},{9,8},{10,11... | collective-permute-start | bytes 737288 | tf_op jit(solution)/shard_map/ppermute | solution.py:509
  34.0 1.3 %shard_map.99.done_ref = bf16[240,16,128]{2,1,0:T(8,128)(2,1)S(1)} custom-call(s32[1]{0:T(128)} %bitcast.core_ref, s32[1]{0:T(128)} %bitcast.1.pair_ref, bf16[240,512]{1,0:T(8,128)(2,1)S(1)} %get-tuple-element.31.inflow_ref, f32[240,2048]{1,0:T(8,128)S(1)} %shard_map.95.base_ref, bf16[240,512]{1,0:T(8,128)(2,1)S(1)} %get-tuple-element.19.table_ref, ...), custom_call_target="tpu_custom_call" | custom-call | flops 1 | bytes 1 | tf_op jit(solution)/shard_map/pallas_call | solution.py:480
  35.3 0.0 collective-permute-done.4.inflow_ref
  35.4 0.0 collective-permute-done.3.inflow_ref
  35.4 2.1 %shard_map.101 = bf16[240,32,128]{2,1,0:T(8,128)(2,1)} custom-call(s32[1]{0:T(128)} %bitcast.core_ref, s32[1]{0:T(128)} %bitcast.1.pair_ref, bf16[240,16,128]{2,1,0:T(8,128)(2,1)S(1)} %shard_map.99.done_ref, bf16[240,512]{1,0:T(8,128)(2,1)S(1)} %collective-permute-done.3.inflow_ref, ...), custom_call_target="tpu_custom_call", output_to_operand_aliasing={{}: (8, {})} | custom-call | flops 1 | bytes 1 | tf_op jit(solution)/shard_map/pallas_call | solution.py:489
  (5 shorter events, 0.0 us)
Async XLA Ops:
  0.0 8.9 %copy-start = (s32[1,1,32,128]{3,2,1,0:T(8,128)S(1)}, s32[1,1,32,128]{3,2,1,0:T(8,128)}, u32[]{:S(2)}) copy-start(s32[1,1,32,128]{3,2,1,0:T(8,128)} %param.17) | copy-start | bytes 49156
  0.0 8.9 %copy-start.5 = (s32[1,1,32]{2,1,0:T(1,128)S(1)}, s32[1,1,32]{2,1,0:T(1,128)}, u32[]{:S(2)}) copy-start(s32[1,1,32]{2,1,0:T(1,128)} %param.16) | copy-start | bytes 388
  0.0 8.9 %copy-start.4 = (s32[128,1]{0,1:T(1,128)S(1)}, s32[128,1]{0,1:T(1,128)}, u32[]{:S(2)}) copy-start(s32[128,1]{0,1:T(1,128)} %param.13) | copy-start | bytes 1540
  0.0 8.9 %copy-start.3 = (f32[128,4]{0,1:T(4,128)S(1)}, f32[128,4]{0,1:T(4,128)}, u32[]{:S(2)}) copy-start(f32[128,4]{0,1:T(4,128)} %param.12) | copy-start | bytes 6148
  0.0 8.9 %copy-start.2 = (s32[128,4]{0,1:T(4,128)S(1)}, s32[128,4]{0,1:T(4,128)}, u32[]{:S(2)}) copy-start(s32[128,4]{0,1:T(4,128)} %param.11) | copy-start | bytes 6148
  0.0 10.2 %copy-start.6 = (f32[8]{0:T(128)S(1)}, f32[8]{0:T(128)}, u32[]{:S(2)}) copy-start(f32[8]{0:T(128)} %param.15) | copy-start | bytes 100
  0.0 10.2 %copy-start.1 = (f32[8,240]{1,0:T(8,128)S(1)}, f32[8,240]{1,0:T(8,128)}, u32[]{:S(2)}) copy-start(f32[8,240]{1,0:T(8,128)} %shape_ref.1) | copy-start | bytes 23044
  2.4 20.6 %all-to-all-start = ((bf16[16,64,240]{2,1,0:T(8,128)(2,1)}), bf16[16,64,240]{2,1,0:T(8,128)(2,1)S(1)}, u32[]{:S(2)}, u32[]{:S(2)}) async-start(bf16[16,64,240]{2,1,0:T(8,128)(2,1)} %bitcast.20), calls=%async_computation | async-start | bytes 1048576 | tf_op jit(solution)/shard_map/all_to_all | solution.py:408
  8.9 1.3 %collective-permute-start = (f32[64,128]{1,0:T(8,128)S(1)}, f32[64,128]{1,0:T(8,128)S(1)}, u32[]{:S(2)}, u32[]{:S(2)}) collective-permute-start(f32[64,128]{1,0:T(8,128)S(1)} %shard_map.92.own_ref), channel_id=1, source_target_pairs={{0,1},{1,0},{2,3},{3,2},{4,5},{5,4},{6,7},{7,6},{8,9},{9,8},{10,11... | collective-permute-start | bytes 98312 | tf_op jit(solution)/shard_map/ppermute | solution.py:423
  24.3 3.5 %collective-permute-start.2 = (bf16[8,64,240]{2,1,0:T(8,128)(2,1)S(1)}, bf16[8,64,240]{2,1,0:T(8,128)(2,1)S(1)}, u32[]{:S(2)}, u32[]{:S(2)}) collective-permute-start(bf16[8,64,240]{2,1,0:T(8,128)(2,1)S(1)} %get-tuple-element.30), channel_id=1, source_target_pairs={{0,1},{1,0},{2,3},{3,2},{4,5},{5,4},{6,7},{7,6},{8,9},{9,8},{10,11... | collective-permute-start | bytes 737288 | tf_op jit(solution)/shard_map/ppermute | solution.py:474
  24.9 7.5 %collective-permute-start.1 = (bf16[240,512]{1,0:T(8,128)(2,1)S(1)}, bf16[240,512]{1,0:T(8,128)(2,1)S(1)}, u32[]{:S(2)}, u32[]{:S(2)}) collective-permute-start(bf16[240,512]{1,0:T(8,128)(2,1)S(1)} %get-tuple-element.23), channel_id=1, source_target_pairs={{0,2},{2,0},{1,3},{3,1},{4,6},{6,4},{5,7},{7,5},{8,10},{10,8},{9,1... | collective-permute-start | bytes 737288 | tf_op jit(solution)/shard_map/ppermute | solution.py:455
  25.1 10.2 %collective-permute-start.4 = (bf16[240,512]{1,0:T(8,128)(2,1)S(1)}, bf16[240,512]{1,0:T(8,128)(2,1)S(1)}, u32[]{:S(2)}, u32[]{:S(2)}) collective-permute-start(bf16[240,512]{1,0:T(8,128)(2,1)S(1)} %get-tuple-element.25.inflow_ref), channel_id=1, source_target_pairs={{0,1},{1,0},{2,3},{3,2},{4,5},{5,4},{6,7},{7,6},{8,9},{9,8},{10,11... | collective-permute-start | bytes 737288 | tf_op jit(solution)/shard_map/ppermute | solution.py:475
  33.1 2.3 %collective-permute-start.3 = (bf16[240,512]{1,0:T(8,128)(2,1)S(1)}, bf16[240,512]{1,0:T(8,128)(2,1)S(1)}, u32[]{:S(2)}, u32[]{:S(2)}) collective-permute-start(bf16[240,512]{1,0:T(8,128)(2,1)S(1)} %get-tuple-element.32), channel_id=1, source_target_pairs={{0,1},{1,0},{2,3},{3,2},{4,5},{5,4},{6,7},{7,6},{8,9},{9,8},{10,11... | collective-permute-start | bytes 737288 | tf_op jit(solution)/shard_map/ppermute | solution.py:509

commit v6 on v5

--- a/solution.py
+++ b/solution.py
@@ -11,7 +11,7 @@
 MB = 8
 SUB = 4
 LANES = 128
-BLOCK = 64
+BLOCK = 32
 CHUNK = 256
 VMEM_LIMIT = 20 * 1024 * 1024
 FULL_VMEM = 56 * 1024 * 1024
@@ -306,41 +306,34 @@
     return pl.when((pair_ref[0] == 0) == top)
 
 
-def assemble(hours, high, low, base_ref, link_ref, scratch, members, reaches):
+def assemble(hours, high, low, base_ref, link_ref, members, reaches):
     lanes, width = link_ref.shape[0] // 2, link_ref.shape[1]
-    count = hours.stop - hours.start
+    flows = []
     for part in range(high.shape[1] // lanes):
         cut = slice(part * lanes, (part + 1) * lanes)
         both = jnp.concatenate([high[hours, cut], low[hours, cut]], axis=1)
         total = mm(both, link_ref[...]) + base_ref[hours, part * width : (part + 1) * width]
-        for j in range(width // reaches):
-            member = part * (width // reaches) + j
-            scratch[pl.ds(hours.start * members + member, count, stride=members), :] = total[
-                :, j * reaches : (j + 1) * reaches
-            ]
-    flow = scratch[hours.start * members : hours.stop * members, :]
-    return flow.reshape(count, members, reaches).astype(BF)
+        flows.append(total.astype(BF))
+    return jnp.concatenate(flows, axis=1).reshape(hours.stop - hours.start, members, reaches)
 
 
 def early_kernel(
     class_count, top, core_ref, pair_ref, inflow_ref, base_ref, table_ref, link_ref, cls_ref,
-    out_ref, scratch,
+    out_ref,
 ):
     hours, members, reaches = out_ref.shape
 
     @mine(top, pair_ref)
     def _():
         high, low = routed_parts(class_count, top, core_ref, inflow_ref, table_ref, cls_ref)
-        out_ref[...] = assemble(
-            slice(0, hours), high, low, base_ref, link_ref, scratch, members, reaches
-        )
+        out_ref[...] = assemble(slice(0, hours), high, low, base_ref, link_ref, members, reaches)
 
 
 def late_kernel(
     class_count, top, core_ref, pair_ref, done_ref, inflow_ref, base_ref, table_ref, link_ref,
     cls_ref, *rest,
 ):
-    out_ref, scratch, ready, sems = rest[-4:]
+    out_ref, ready, sems = rest[-3:]
     hours, members, reaches = done_ref.shape
 
     @mine(top, pair_ref)
@@ -355,7 +348,7 @@
         high, low = routed_parts(class_count, top, core_ref, inflow_ref, table_ref, cls_ref)
         for start in range(0, hours, LANES):
             part = slice(start, min(start + LANES, hours))
-            ready[part] = assemble(part, high, low, base_ref, link_ref, scratch, members, reaches)
+            ready[part] = assemble(part, high, low, base_ref, link_ref, members, reaches)
             span = pl.ds(start, part.stop - start)
             copies.append(
                 pltpu.make_async_copy(
@@ -470,7 +463,6 @@
             out_specs=vmem(1)[0],
         )(core_arg, rows, table, wide_mix, cls_own)
 
-    flat = pltpu.VMEM((hours * half, reaches), F32)
     rows_other = lax.ppermute(rows_send, "core", swap)
     first_other = lax.ppermute(first, "core", swap)
     base_own = base(received)
@@ -482,7 +474,6 @@
             struct((hours, half, reaches), BF),
             in_specs=[SCALAR] * 2 + vmem(5),
             out_specs=vmem(1)[0],
-            scratch_shapes=[flat],
         )(core_arg, pair_arg, own, base_own, table, link, cls_target)
 
     def late(top, done, gotten, before):
@@ -492,7 +483,6 @@
             in_specs=[SCALAR] * 2 + vmem(6) + [anywhere] * len(before),
             out_specs=anywhere,
             scratch_shapes=[
-                flat,
                 pltpu.VMEM((hours, half, reaches), BF),
                 pltpu.SemaphoreType.DMA((1 + -(-hours // LANES),)),
             ],

time: 37.7 us -> 36.9 us (0.979)
  Pallas kernels: 13.6 us -> 12.4 us
  waiting for transfers between devices: 15 us -> 15.4 us
    pallas_call x2, Pallas kernels: 2.16 us -> 1.71 us  [late(): call(functools.partial(late_kernel, class_count, top), struct((hours, mem...]
    pallas_call x2, Pallas kernels: 1.27 us -> 0.84 us  [early(): call(functools.partial(early_kernel, class_count, top), struct((hours, ha...]
  transfers between devices with their start and end apart: 6 -> 6, of which waited for: 3 -> 4; matrix products, arithmetic and copies ran while one was open for 0% -> 0% of each run, Pallas kernels for 21% -> 19%
where the time goes in v6:
time: 36.9 us; the launch traced here: 36.7 us
  waiting for transfers between devices  15.4 us (42%)
  Pallas kernels  12.4 us (34%)
  starting transfers between devices  8.71 us (24%)
    all_to_all x1, waiting for transfers between devices, local(): lax.all_to_all(send.reshape(regions * 2, half * slot, hours), ('region',...  11.6 us
    all_to_all x1, starting transfers between devices, local(): lax.all_to_all(send.reshape(regions * 2, half * slot, hours), ('region',...  6.51 us
    pallas_call x2, Pallas kernels, base(): call(functools.partial(base_kernel, class_count), struct((hours, half * r...  4.48 us
    ppermute x1, waiting for transfers between devices, local(): arrived = lax.ppermute(panel, 'pair', [(step, step + 1), (step + 1, step)])  2.45 us
    pallas_call x1, Pallas kernels, local(): call(functools.partial(pack_kernel, slot), struct((regions, 2, half * slo...  2.32 us
    pallas_call x2, Pallas kernels, late(): call(functools.partial(late_kernel, class_count, top), struct((hours, mem...  1.71 us
    pallas_call x1, Pallas kernels, local(): call(functools.partial(head_kernel, class_count), tuple(shapes), in_specs...  1.31 us
    pallas_call x1, Pallas kernels, local(): call(functools.partial(prep_kernel, slot, columns), (struct((hours, class...  1.11 us
  transfers between devices with their start and end apart: 6, of which 4 were waited for; matrix products, arithmetic and copies ran while one was open for 0% of the time, Pallas kernels for 19%

profile of v6, /device:TPU:5, one launch (start us, length us, event | category | flops | bytes accessed | tf_op | source)
XLA Modules:
  0.0 36.7 jit_solution(15184590818552150635)
XLA Ops:
  0.0 0.0 copy-start
  0.0 0.0 copy-start.3
  0.0 0.0 copy-start.2
  0.0 0.0 copy-start.6
  0.0 0.0 copy-start.1
  0.0 2.3 %shard_map.91 = bf16[8,2,64,240]{3,2,1,0:T(8,128)(2,1)} custom-call(f32[32,32,240]{2,1,0:T(8,128)} %bitcast.21, s32[1,32]{1,0:T(1,128)} %bitcast.22), custom_call_target="tpu_custom_call" | custom-call | flops 1 | bytes 1 | tf_op jit(solution)/shard_map/pallas_call | solution.py:387
  2.4 6.5 %all-to-all-start = ((bf16[16,64,240]{2,1,0:T(8,128)(2,1)}), bf16[16,64,240]{2,1,0:T(8,128)(2,1)S(1)}, u32[]{:S(2)}, u32[]{:S(2)}) async-start(bf16[16,64,240]{2,1,0:T(8,128)(2,1)} %bitcast.20), calls=%async_computation | async-start | bytes 1048576 | tf_op jit(solution)/shard_map/all_to_all | solution.py:401
  8.9 0.0 copy-done
  8.9 0.0 copy-done.5
  8.9 0.0 copy-done.4
  8.9 0.0 copy-done.3
  8.9 0.0 copy-done.2
  8.9 0.2 collective-permute-start
  9.1 1.1 %collective-permute-done.other_ref = f32[64,128]{1,0:T(8,128)S(1)} collective-permute-done((f32[64,128]{1,0:T(8,128)S(1)}, f32[64,128]{1,0:T(8,128)S(1)}, u32[]{:S(2)}, u32[]{:S(2)}) %collective-permute-start) | collective-permute-done | bytes 32800 | tf_op jit(solution)/shard_map/ppermute | solution.py:416
  10.2 0.0 copy-done.6
  10.2 0.0 copy-done.1
  10.2 1.1 %shard_map.93 = (bf16[240,256]{1,0:T(8,128)(2,1)S(1)}, bf16[2,256,128]{2,1,0:T(8,128)(2,1)S(1)}, bf16[2,256,256]{2,1,0:T(8,128)(2,1)S(1)}, f32[2,8,256]{2,1,0:T(...) custom-call(s32[1]{0:T(128)} %bitcast.core_ref, ...), custom_call_target="tpu_custom_call" | custom-call | flops 1 | bytes 1 | tf_op jit(solution)/shard_map/pallas_call | solution.py:417
  11.3 11.6 %all-to-all-done = bf16[16,64,240]{2,1,0:T(8,128)(2,1)S(1)} async-done(((bf16[16,64,240]{2,1,0:T(8,128)(2,1)}), bf16[16,64,240]{2,1,0:T(8,128)(2,1)S(1)}, u32[]{:S(2)}, u32[]{:S(2)}) %all-to-all-start) | async-done | bytes 491552 | tf_op jit(solution)/shard_map/all_to_all | solution.py:401
  23.0 1.3 %shard_map.94 = (bf16[240,512]{1,0:T(8,128)(2,1)S(1)}, f32[240,512]{1,0:T(8,128)S(1)}, bf16[240,512]{1,0:T(8,128)(2,1)S(1)}, bf16[8,64,240]{2,1,0:T(8,128)(2,1)S(1)}) custom-call(s32[1]{0:T(128)} %bitcast.core_ref, bf16[8,2,64,240]{3,2,1,0:T(8,128)(2,1)S(1)} %bitcast.12, bf16[240,256]{1,0:T(8,128)(2,1)S(1)} %get-tuple-element.19.table_ref, ...), custom_call_target="tpu_custom_call" | custom-call | flops 1 | bytes 1 | tf_op jit(solution)/shard_map/pallas_call | solution.py:438
  24.3 0.5 %collective-permute-start.2 = (bf16[8,64,240]{2,1,0:T(8,128)(2,1)S(1)}, bf16[8,64,240]{2,1,0:T(8,128)(2,1)S(1)}, u32[]{:S(2)}, u32[]{:S(2)}) collective-permute-start(bf16[8,64,240]{2,1,0:T(8,128)(2,1)S(1)} %get-tuple-element.30), channel_id=1, source_target_pairs={{0,1},{1,0},{2,3},{3,2},{4,5},{5,4},{6,7},{7,6},{8,9},{9,8},{10,11... | collective-permute-start | bytes 737288 | tf_op jit(solution)/shard_map/ppermute | solution.py:466
  24.8 0.2 collective-permute-start.1
  25.1 0.3 collective-permute-start.4
  25.4 2.2 %shard_map.95.base_ref = f32[240,2048]{1,0:T(8,128)S(1)} custom-call(s32[1]{0:T(128)} %bitcast.core_ref, bf16[8,2,64,240]{3,2,1,0:T(8,128)(2,1)S(1)} %bitcast.13, bf16[240,256]{1,0:T(8,128)(2,1)S(1)} %get-tuple-element.19.table_ref, bf16[256,512]{1,0:T(8,128)(2,1)S(1)} %get-tuple-element.26.wide_ref, f32[8,128]{1,0:T(8,128)S(1)} %get-tuple-element.27.cls_ref), custom_call_target="tpu_custom_call" | custom-call | flops 1 | bytes 1 | tf_op jit(solution)/shard_map/pallas_call | solution.py:459
  27.6 0.0 collective-permute-done.2.rows_ref
  27.6 2.3 %shard_map.97.rest_1_.base_ref = f32[240,2048]{1,0:T(8,128)S(1)} custom-call(s32[1]{0:T(128)} %bitcast.core_ref, bf16[8,64,240]{2,1,0:T(8,128)(2,1)S(1)} %collective-permute-done.2.rows_ref, bf16[240,256]{1,0:T(8,128)(2,1)S(1)} %get-tuple-element.19.table_ref, bf16[256,512]{1,0:T(8,128)(2,1)S(1)} %get-tuple-element.26.wide_ref, ...), custom_call_target="tpu_custom_call" | custom-call | flops 1 | bytes 1 | tf_op jit(solution)/shard_map/pallas_call | solution.py:459
  29.9 2.5 %collective-permute-done.1.inflow_ref = bf16[240,512]{1,0:T(8,128)(2,1)S(1)} collective-permute-done((bf16[240,512]{1,0:T(8,128)(2,1)S(1)}, bf16[240,512]{1,0:T(8,128)(2,1)S(1)}, u32[]{:S(2)}, u32[]{:S(2)}) %collective-permute-start.1) | collective-permute-done | bytes 245792 | tf_op jit(solution)/shard_map/ppermute | solution.py:448
  32.3 0.6 %shard_map.98 = (bf16[240,512]{1,0:T(8,128)(2,1)S(1)}, bf16[240,512]{1,0:T(8,128)(2,1)S(1)}) custom-call(s32[1]{0:T(128)} %bitcast.core_ref, s32[1]{0:T(128)} %bitcast.1.pair_ref, bf16[240,512]{1,0:T(8,128)(2,1)S(1)} %collective-permute-done.1.inflow_ref, bf16[240,256]{1,0:T(8,128)(2,1)S(1)} %get-tuple-element.19.table_ref, ...), custom_call_target="tpu_custom_call" | custom-call | flops 1 | bytes 1 | tf_op jit(solution)/shard_map/pallas_call | solution.py:493
  33.0 0.9 %collective-permute-start.3 = (bf16[240,512]{1,0:T(8,128)(2,1)S(1)}, bf16[240,512]{1,0:T(8,128)(2,1)S(1)}, u32[]{:S(2)}, u32[]{:S(2)}) collective-permute-start(bf16[240,512]{1,0:T(8,128)(2,1)S(1)} %get-tuple-element.32), channel_id=1, source_target_pairs={{0,1},{1,0},{2,3},{3,2},{4,5},{5,4},{6,7},{7,6},{8,9},{9,8},{10,11... | collective-permute-start | bytes 737288 | tf_op jit(solution)/shard_map/ppermute | solution.py:499
  33.9 0.8 %shard_map.99.done_ref = bf16[240,16,128]{2,1,0:T(8,128)(2,1)S(1)} custom-call(s32[1]{0:T(128)} %bitcast.core_ref, s32[1]{0:T(128)} %bitcast.1.pair_ref, bf16[240,512]{1,0:T(8,128)(2,1)S(1)} %get-tuple-element.31.inflow_ref, f32[240,2048]{1,0:T(8,128)S(1)} %shard_map.95.base_ref, bf16[240,256]{1,0:T(8,128)(2,1)S(1)} %get-tuple-element.19.table_ref, ...), custom_call_target="tpu_custom_call" | custom-call | flops 1 | bytes 1 | tf_op jit(solution)/shard_map/pallas_call | solution.py:472
  34.7 0.0 collective-permute-done.4.inflow_ref
  34.8 0.2 collective-permute-done.3.inflow_ref
  35.0 1.7 %shard_map.101 = bf16[240,32,128]{2,1,0:T(8,128)(2,1)} custom-call(s32[1]{0:T(128)} %bitcast.core_ref, s32[1]{0:T(128)} %bitcast.1.pair_ref, bf16[240,16,128]{2,1,0:T(8,128)(2,1)S(1)} %shard_map.99.done_ref, bf16[240,512]{1,0:T(8,128)(2,1)S(1)} %collective-permute-done.3.inflow_ref, ...), custom_call_target="tpu_custom_call", output_to_operand_aliasing={{}: (8, {})} | custom-call | flops 1 | bytes 1 | tf_op jit(solution)/shard_map/pallas_call | solution.py:480
  (5 shorter events, 0.0 us)
Async XLA Ops:
  0.0 8.9 %copy-start = (s32[1,1,32,128]{3,2,1,0:T(8,128)S(1)}, s32[1,1,32,128]{3,2,1,0:T(8,128)}, u32[]{:S(2)}) copy-start(s32[1,1,32,128]{3,2,1,0:T(8,128)} %param.17) | copy-start | bytes 49156
  0.0 8.9 %copy-start.5 = (s32[1,1,32]{2,1,0:T(1,128)S(1)}, s32[1,1,32]{2,1,0:T(1,128)}, u32[]{:S(2)}) copy-start(s32[1,1,32]{2,1,0:T(1,128)} %param.16) | copy-start | bytes 388
  0.0 8.9 %copy-start.4 = (s32[128,1]{0,1:T(1,128)S(1)}, s32[128,1]{0,1:T(1,128)}, u32[]{:S(2)}) copy-start(s32[128,1]{0,1:T(1,128)} %param.13) | copy-start | bytes 1540
  0.0 8.9 %copy-start.3 = (f32[128,4]{0,1:T(4,128)S(1)}, f32[128,4]{0,1:T(4,128)}, u32[]{:S(2)}) copy-start(f32[128,4]{0,1:T(4,128)} %param.12) | copy-start | bytes 6148
  0.0 8.9 %copy-start.2 = (s32[128,4]{0,1:T(4,128)S(1)}, s32[128,4]{0,1:T(4,128)}, u32[]{:S(2)}) copy-start(s32[128,4]{0,1:T(4,128)} %param.11) | copy-start | bytes 6148
  0.0 10.2 %copy-start.6 = (f32[8]{0:T(128)S(1)}, f32[8]{0:T(128)}, u32[]{:S(2)}) copy-start(f32[8]{0:T(128)} %param.15) | copy-start | bytes 100
  0.0 10.2 %copy-start.1 = (f32[8,240]{1,0:T(8,128)S(1)}, f32[8,240]{1,0:T(8,128)}, u32[]{:S(2)}) copy-start(f32[8,240]{1,0:T(8,128)} %shape_ref.1) | copy-start | bytes 23044
  2.4 20.6 %all-to-all-start = ((bf16[16,64,240]{2,1,0:T(8,128)(2,1)}), bf16[16,64,240]{2,1,0:T(8,128)(2,1)S(1)}, u32[]{:S(2)}, u32[]{:S(2)}) async-start(bf16[16,64,240]{2,1,0:T(8,128)(2,1)} %bitcast.20), calls=%async_computation | async-start | bytes 1048576 | tf_op jit(solution)/shard_map/all_to_all | solution.py:401
  8.9 1.3 %collective-permute-start = (f32[64,128]{1,0:T(8,128)S(1)}, f32[64,128]{1,0:T(8,128)S(1)}, u32[]{:S(2)}, u32[]{:S(2)}) collective-permute-start(f32[64,128]{1,0:T(8,128)S(1)} %shard_map.92.own_ref), channel_id=1, source_target_pairs={{0,1},{1,0},{2,3},{3,2},{4,5},{5,4},{6,7},{7,6},{8,9},{9,8},{10,11... | collective-permute-start | bytes 98312 | tf_op jit(solution)/shard_map/ppermute | solution.py:416
  24.3 3.4 %collective-permute-start.2 = (bf16[8,64,240]{2,1,0:T(8,128)(2,1)S(1)}, bf16[8,64,240]{2,1,0:T(8,128)(2,1)S(1)}, u32[]{:S(2)}, u32[]{:S(2)}) collective-permute-start(bf16[8,64,240]{2,1,0:T(8,128)(2,1)S(1)} %get-tuple-element.30), channel_id=1, source_target_pairs={{0,1},{1,0},{2,3},{3,2},{4,5},{5,4},{6,7},{7,6},{8,9},{9,8},{10,11... | collective-permute-start | bytes 737288 | tf_op jit(solution)/shard_map/ppermute | solution.py:466
  24.8 7.5 %collective-permute-start.1 = (bf16[240,512]{1,0:T(8,128)(2,1)S(1)}, bf16[240,512]{1,0:T(8,128)(2,1)S(1)}, u32[]{:S(2)}, u32[]{:S(2)}) collective-permute-start(bf16[240,512]{1,0:T(8,128)(2,1)S(1)} %get-tuple-element.23), channel_id=1, source_target_pairs={{0,2},{2,0},{1,3},{3,1},{4,6},{6,4},{5,7},{7,5},{8,10},{10,8},{9,1... | collective-permute-start | bytes 737288 | tf_op jit(solution)/shard_map/ppermute | solution.py:448
  25.1 9.7 %collective-permute-start.4 = (bf16[240,512]{1,0:T(8,128)(2,1)S(1)}, bf16[240,512]{1,0:T(8,128)(2,1)S(1)}, u32[]{:S(2)}, u32[]{:S(2)}) collective-permute-start(bf16[240,512]{1,0:T(8,128)(2,1)S(1)} %get-tuple-element.25.inflow_ref), channel_id=1, source_target_pairs={{0,1},{1,0},{2,3},{3,2},{4,5},{5,4},{6,7},{7,6},{8,9},{9,8},{10,11... | collective-permute-start | bytes 737288 | tf_op jit(solution)/shard_map/ppermute | solution.py:467
  33.0 2.0 %collective-permute-start.3 = (bf16[240,512]{1,0:T(8,128)(2,1)S(1)}, bf16[240,512]{1,0:T(8,128)(2,1)S(1)}, u32[]{:S(2)}, u32[]{:S(2)}) collective-permute-start(bf16[240,512]{1,0:T(8,128)(2,1)S(1)} %get-tuple-element.32), channel_id=1, source_target_pairs={{0,1},{1,0},{2,3},{3,2},{4,5},{5,4},{6,7},{7,6},{8,9},{9,8},{10,11... | collective-permute-start | bytes 737288 | tf_op jit(solution)/shard_map/ppermute | solution.py:499

commit v7 on v6

--- a/solution.py
+++ b/solution.py
@@ -23,10 +23,6 @@
 
 def mm(a, b):
     return jnp.dot(a, b, preferred_element_type=F32)
-
-
-def tmm(a, b):
-    return lax.dot_general(a, b, (((0,), (0,)), ((), ())), preferred_element_type=F32)
 
 
 def one_hot(condition):
@@ -209,8 +205,8 @@
 
 def twice(rows_ref, sub, size):
     rows = rows_ref[:, sub * size : (sub + 1) * size, :]
-    rows = rows.reshape(rows.shape[0] * size, rows.shape[2])
-    return jnp.concatenate([rows, rows], axis=0)
+    rows = rows.reshape(rows.shape[0] * size, rows.shape[2]).T
+    return jnp.concatenate([rows, rows], axis=1)
 
 
 def pass_on(panel, pass_matrix):
@@ -226,31 +222,29 @@
     return jnp.concatenate([classes] * (width // classes.shape[1]), axis=1)
 
 
-def head_kernel(class_count, core_ref, rows_ref, table_ref, mix_ref, pass_ref, cls_ref, *outs):
-    panel_ref, even_ref, first_ref, send_ref = outs[:4]
+def outlet_lateral(level, rows_ref, mix_ref):
     regions, _, total, _ = rows_ref.shape
     size = mix_ref.shape[1] // 2 // regions
-    wide = panel_ref.shape[1]
-    classes = [tiled(cls_ref[level, 0:1, :], wide) for level in range(2)]
-    lateral = [
-        jnp.concatenate(
-            [
-                tmm(twice(rows_ref.at[:, level], sub, size), mix_ref[level])
-                for sub in range(total // size)
-            ],
-            axis=1,
-        )
-        for level in range(2)
-    ]
-    even = convolve(table_ref[...], lateral[0].astype(BF), classes[0], class_count)
-    even_ref[...] = even
-    first = even.astype(BF)
-    first_ref[...] = first
-    inflow = lateral[1] + pass_on(first, pass_ref[1]).astype(F32)
-    panel_ref[...] = convolve(table_ref[...], inflow.astype(BF), classes[1], class_count).astype(BF)
+    rows_ref = rows_ref.at[:, level]
+    parts = [mm(twice(rows_ref, sub, size), mix_ref[level]) for sub in range(total // size)]
+    return jnp.concatenate(parts, axis=1)
+
+
+def head_kernel(
+    class_count, core_ref, pair_ref, rows_ref, table_ref, mix_ref, pass_ref, cls_ref,
+    panel_ref, first_ref, send_ref,
+):
     send_ref[...] = jnp.where(core_ref[0] == 0, rows_ref[:, 1], rows_ref[:, 0])
-    if len(outs) > 4:
-        outs[4][...] = lateral[1]
+
+    @pl.when(pair_ref[0] == 0)
+    def _():
+        wide = panel_ref.shape[1]
+        classes = [tiled(cls_ref[level, 0:1, :], wide) for level in range(2)]
+        lateral = [outlet_lateral(level, rows_ref, mix_ref) for level in range(2)]
+        first = convolve(table_ref[...], lateral[0].astype(BF), classes[0], class_count).astype(BF)
+        first_ref[...] = first
+        inflow = (lateral[1] + pass_on(first, pass_ref[1]).astype(F32)).astype(BF)
+        panel_ref[...] = convolve(table_ref[...], inflow, classes[1], class_count).astype(BF)
 
 
 def hop_kernel(class_count, inflow_ref, table_ref, pass_ref, cls_ref, even_ref, odd_ref, panel_ref):
@@ -287,11 +281,26 @@
     for sub in range(total // size):
         rows = twice(rows_ref, sub, size)
         for start in range(0, width, step):
-            lateral = tmm(rows, wide_ref[:, start : start + step]).astype(BF)
+            lateral = mm(rows, wide_ref[:, start : start + step]).astype(BF)
             place = sub * width + start
             base_ref[:, place : place + step] = convolve(
                 table_ref[...], lateral, classes, class_count
             )
+
+
+def base_own_kernel(
+    class_count, core_ref, pair_ref, rows_ref, table_ref, wide_ref, cls_ref, mix_ref, cls_out_ref,
+    base_ref, even_ref, *odd_ref,
+):
+    base_kernel(class_count, core_ref, rows_ref, table_ref, wide_ref, cls_ref, base_ref)
+
+    @pl.when(pair_ref[0] > 0)
+    def _():
+        lateral = outlet_lateral(0, rows_ref, mix_ref).astype(BF)
+        classes = tiled(cls_out_ref[0, 0:1, :], even_ref.shape[1])
+        even_ref[...] = convolve(table_ref[...], lateral, classes, class_count)
+        if odd_ref:
+            odd_ref[0][...] = outlet_lateral(1, rows_ref, mix_ref)
 
 
 def routed_parts(class_count, top, core_ref, inflow_ref, table_ref, cls_ref):
@@ -432,41 +441,41 @@
 
     panel_shape = struct((hours, wide), BF)
     float_shape = struct((hours, wide), F32)
-    shapes = [panel_shape, float_shape, panel_shape, struct((regions, half * slot, hours), BF)]
-    if pairs > 2:
-        shapes.append(float_shape)
-    heads = call(
+    panel, first, rows_send = call(
         functools.partial(head_kernel, class_count),
-        tuple(shapes),
-        in_specs=[SCALAR] + vmem(5),
-        out_specs=tuple(vmem(len(shapes))),
-    )(core_arg, received, table, mix, passing, cls_out)
-    panel, even, first, rows_send = heads[:4]
-
-    inflow = jnp.zeros(panel_shape.shape, BF)
-    for step in range(pairs - 1):
-        arrived = lax.ppermute(panel, "pair", [(step, step + 1), (step + 1, step)])
-        inflow = arrived if pairs == 2 else jnp.where(pair == step + 1, arrived, inflow)
-        if step < pairs - 2:
-            panel = call(
-                functools.partial(hop_kernel, class_count),
-                panel_shape,
-                in_specs=vmem(6),
-                out_specs=vmem(1)[0],
-            )(inflow, table, passing, cls_out, even, heads[4])
-
-    def base(rows):
-        return call(
-            functools.partial(base_kernel, class_count),
-            struct((hours, half * reaches), F32),
-            in_specs=[SCALAR] + vmem(4),
-            out_specs=vmem(1)[0],
-        )(core_arg, rows, table, wide_mix, cls_own)
-
+        (panel_shape, panel_shape, struct((regions, half * slot, hours), BF)),
+        in_specs=[SCALAR] * 2 + vmem(5),
+        out_specs=tuple(vmem(3)),
+    )(core_arg, pair_arg, received, table, mix, passing, cls_out)
+    inflow = lax.ppermute(panel, "pair", [(0, 1), (1, 0)]) if pairs > 1 else panel
     rows_other = lax.ppermute(rows_send, "core", swap)
     first_other = lax.ppermute(first, "core", swap)
-    base_own = base(received)
-    base_other = base(rows_other)
+
+    base_shape = struct((hours, half * reaches), F32)
+    shapes = [base_shape, float_shape] + [float_shape] * (pairs > 2)
+    base_own, even, *odd = call(
+        functools.partial(base_own_kernel, class_count),
+        tuple(shapes),
+        in_specs=[SCALAR] * 2 + vmem(6),
+        out_specs=tuple(vmem(len(shapes))),
+    )(core_arg, pair_arg, received, table, wide_mix, cls_own, mix, cls_out)
+    base_other = call(
+        functools.partial(base_kernel, class_count),
+        base_shape,
+        in_specs=[SCALAR] + vmem(4),
+        out_specs=vmem(1)[0],
+    )(core_arg, rows_other, table, wide_mix, cls_own)
+
+
+    for step in range(1, pairs - 1):
+        panel = call(
+            functools.partial(hop_kernel, class_count),
+            panel_shape,
+            in_specs=vmem(6),
+            out_specs=vmem(1)[0],
+        )(inflow, table, passing, cls_out, even, odd[0])
+        arriving = lax.ppermute(panel, "pair", [(step, step + 1), (step + 1, step)])
+        inflow = jnp.where(pair == step + 1, arriving, inflow)
 
     def early(top, own):
         return call(

time: 36.9 us -> 36 us (0.976)
  the two profiles are of different devices: /device:TPU:5 before, /device:TPU:1 now
where the time goes in v7:
time: 36 us; the launch traced here: 35.8 us
  waiting for transfers between devices  14.6 us (41%)
  Pallas kernels  11.8 us (33%)
  starting transfers between devices  9.22 us (26%)
    all_to_all x1, waiting for transfers between devices, local(): lax.all_to_all(send.reshape(regions * 2, half * slot, hours), ('region',...  11.6 us
    all_to_all x1, starting transfers between devices, local(): lax.all_to_all(send.reshape(regions * 2, half * slot, hours), ('region',...  7.34 us
    pallas_call x1, Pallas kernels, local(): call(functools.partial(pack_kernel, slot), struct((regions, 2, half * slo...  2.32 us
    pallas_call x1, Pallas kernels, local(): call(functools.partial(base_kernel, class_count), base_shape, in_specs=[S...  2.24 us
    pallas_call x1, Pallas kernels, local(): call(functools.partial(base_own_kernel, class_count), tuple(shapes), in_s...  2.23 us
    ppermute x1, waiting for transfers between devices, local(): lax.ppermute(panel, 'pair', [(0, 1), (1, 0)])  1.87 us
    pallas_call x2, Pallas kernels, late(): call(functools.partial(late_kernel, class_count, top), struct((hours, mem...  1.7 us
    pallas_call x1, Pallas kernels, local(): call(functools.partial(head_kernel, class_count), (panel_shape, panel_sha...  1.32 us
  transfers between devices with their start and end apart: 6, of which 3 were waited for; matrix products, arithmetic and copies ran while one was open for 0% of the time, Pallas kernels for 23%

profile of v7, /device:TPU:1, one launch (start us, length us, event | category | flops | bytes accessed | tf_op | source)
XLA Modules:
  0.0 35.8 jit_solution(5577421082955874319)
XLA Ops:
  0.0 0.0 copy-start
  0.0 0.0 copy-start.5
  0.0 0.0 copy-start.3
  0.0 0.0 copy-start.2
  0.0 0.0 copy-start.6
  0.0 0.0 copy-start.1
  0.0 2.3 %shard_map.91 = bf16[8,2,64,240]{3,2,1,0:T(8,128)(2,1)} custom-call(f32[32,32,240]{2,1,0:T(8,128)} %bitcast.21, s32[1,32]{1,0:T(1,128)} %bitcast.22), custom_call_target="tpu_custom_call" | custom-call | flops 1 | bytes 1 | tf_op jit(solution)/shard_map/pallas_call | solution.py:396
  2.4 7.3 %all-to-all-start = ((bf16[16,64,240]{2,1,0:T(8,128)(2,1)}), bf16[16,64,240]{2,1,0:T(8,128)(2,1)S(1)}, u32[]{:S(2)}, u32[]{:S(2)}) async-start(bf16[16,64,240]{2,1,0:T(8,128)(2,1)} %bitcast.20), calls=%async_computation | async-start | bytes 1048576 | tf_op jit(solution)/shard_map/all_to_all | solution.py:410
  9.7 0.0 copy-done
  9.7 0.0 copy-done.5
  9.7 0.0 copy-done.4
  9.7 0.0 copy-done.3
  9.8 0.0 copy-done.2
  9.8 0.2 collective-permute-start
  9.9 1.1 %collective-permute-done.other_ref = f32[64,128]{1,0:T(8,128)S(1)} collective-permute-done((f32[64,128]{1,0:T(8,128)S(1)}, f32[64,128]{1,0:T(8,128)S(1)}, u32[]{:S(2)}, u32[]{:S(2)}) %collective-permute-start) | collective-permute-done | bytes 32800 | tf_op jit(solution)/shard_map/ppermute | solution.py:425
  11.0 0.0 copy-done.6
  11.1 0.0 copy-done.1
  11.1 1.1 %shard_map.93 = (bf16[240,256]{1,0:T(8,128)(2,1)S(1)}, bf16[2,256,128]{2,1,0:T(8,128)(2,1)S(1)}, bf16[2,256,256]{2,1,0:T(8,128)(2,1)S(1)}, f32[2,8,256]{2,1,0:T(...) custom-call(s32[1]{0:T(128)} %bitcast.core_ref, ...), custom_call_target="tpu_custom_call" | custom-call | flops 1 | bytes 1 | tf_op jit(solution)/shard_map/pallas_call | solution.py:426
  12.2 11.6 %all-to-all-done = bf16[16,64,240]{2,1,0:T(8,128)(2,1)S(1)} async-done(((bf16[16,64,240]{2,1,0:T(8,128)(2,1)}), bf16[16,64,240]{2,1,0:T(8,128)(2,1)S(1)}, u32[]{:S(2)}, u32[]{:S(2)}) %all-to-all-start) | async-done | bytes 491552 | tf_op jit(solution)/shard_map/all_to_all | solution.py:410
  23.8 1.3 %shard_map.94 = (bf16[240,512]{1,0:T(8,128)(2,1)S(1)}, bf16[240,512]{1,0:T(8,128)(2,1)S(1)}, bf16[8,64,240]{2,1,0:T(8,128)(2,1)S(1)}) custom-call(s32[1]{0:T(128)} %bitcast.core_ref, s32[1]{0:T(128)} %bitcast.1.pair_ref, bf16[8,2,64,240]{3,2,1,0:T(8,128)(2,1)S(1)} %bitcast.12, bf16[240,256]{1,0:T(8,128)(2,1)S(1)} %get-tuple-element.20.table_ref, ...), custom_call_target="tpu_custom_call" | custom-call | flops 1 | bytes 1 | tf_op jit(solution)/shard_map/pallas_call | solution.py:444
  25.1 0.5 %collective-permute-start.2 = (bf16[8,64,240]{2,1,0:T(8,128)(2,1)S(1)}, bf16[8,64,240]{2,1,0:T(8,128)(2,1)S(1)}, u32[]{:S(2)}, u32[]{:S(2)}) collective-permute-start(bf16[8,64,240]{2,1,0:T(8,128)(2,1)S(1)} %get-tuple-element.32), channel_id=1, source_target_pairs={{0,1},{1,0},{2,3},{3,2},{4,5},{5,4},{6,7},{7,6},{8,9},{9,8},{10,11... | collective-permute-start | bytes 737288 | tf_op jit(solution)/shard_map/ppermute | solution.py:451
  25.7 0.0 collective-permute-start.1
  25.7 0.3 collective-permute-start.4
  26.0 2.2 %shard_map.95 = (f32[240,2048]{1,0:T(8,128)S(1)}, f32[240,512]{1,0:T(8,128)S(1)}) custom-call(s32[1]{0:T(128)} %bitcast.core_ref, s32[1]{0:T(128)} %bitcast.1.pair_ref, bf16[8,2,64,240]{3,2,1,0:T(8,128)(2,1)S(1)} %bitcast.13, bf16[240,256]{1,0:T(8,128)(2,1)S(1)} %get-tuple-element.20.table_ref, bf16[256,512]{1,0:T(8,128)(2,1)S(1)} %get-tuple-element.25.wide_ref, ...), custom_call_target="tpu_custom_call" | custom-call | flops 1 | bytes 1 | tf_op jit(solution)/shard_map/pallas_call | solution.py:456
  28.2 0.8 %shard_map.96.rest_0_.done_ref = bf16[240,16,128]{2,1,0:T(8,128)(2,1)S(1)} custom-call(s32[1]{0:T(128)} %bitcast.core_ref, s32[1]{0:T(128)} %bitcast.1.pair_ref, bf16[240,512]{1,0:T(8,128)(2,1)S(1)} %get-tuple-element.28.inflow_ref, f32[240,2048]{1,0:T(8,128)S(1)} %get-tuple-element.29.base_ref, bf16[240,256]{1,0:T(8,128)(2,1)S(1)} %get-tuple-element.20.table_ref, ...), custom_call_target="tpu_custom_call" | custom-call | flops 1 | bytes 1 | tf_op jit(solution)/shard_map/pallas_call | solution.py:481
  29.1 0.0 collective-permute-done.2.rows_ref
  29.1 2.2 %shard_map.97.rest_1_.base_ref = f32[240,2048]{1,0:T(8,128)S(1)} custom-call(s32[1]{0:T(128)} %bitcast.core_ref, bf16[8,64,240]{2,1,0:T(8,128)(2,1)S(1)} %collective-permute-done.2.rows_ref, bf16[240,256]{1,0:T(8,128)(2,1)S(1)} %get-tuple-element.20.table_ref, bf16[256,512]{1,0:T(8,128)(2,1)S(1)} %get-tuple-element.25.wide_ref, ...), custom_call_target="tpu_custom_call" | custom-call | flops 1 | bytes 1 | tf_op jit(solution)/shard_map/pallas_call | solution.py:462
  31.3 1.9 %collective-permute-done.1.inflow_ref = bf16[240,512]{1,0:T(8,128)(2,1)S(1)} collective-permute-done((bf16[240,512]{1,0:T(8,128)(2,1)S(1)}, bf16[240,512]{1,0:T(8,128)(2,1)S(1)}, u32[]{:S(2)}, u32[]{:S(2)}) %collective-permute-start.1) | collective-permute-done | bytes 245792 | tf_op jit(solution)/shard_map/ppermute | solution.py:450
  33.2 0.8 %collective-permute-start.3 = (bf16[240,512]{1,0:T(8,128)(2,1)S(1)}, bf16[240,512]{1,0:T(8,128)(2,1)S(1)}, u32[]{:S(2)}, u32[]{:S(2)}) collective-permute-start(bf16[240,512]{1,0:T(8,128)(2,1)S(1)} %get-tuple-element.34), channel_id=1, source_target_pairs={{0,1},{1,0},{2,3},{3,2},{4,5},{5,4},{6,7},{7,6},{8,9},{9,8},{10,11... | collective-permute-start | bytes 737288 | tf_op jit(solution)/shard_map/ppermute | solution.py:508
  34.0 0.0 collective-permute-done.4.inflow_ref
  34.1 1.7 %shard_map.100.rest_0_ = bf16[240,32,128]{2,1,0:T(8,128)(2,1)} custom-call(s32[1]{0:T(128)} %bitcast.core_ref, s32[1]{0:T(128)} %bitcast.1.pair_ref, bf16[240,16,128]{2,1,0:T(8,128)(2,1)S(1)} %shard_map.96.rest_0_.done_ref, bf16[240,512]{1,0:T(8,128)(2,1)S(1)} %collective-permute-done.4.inflow_ref, f32[240,2048]{1,0:T(8,128)S(1)} %shard_map.97.rest_1_.base_ref, ...), custom_call_target="tpu_custom_call" | custom-call | flops 1 | bytes 1 | tf_op jit(solution)/shard_map/pallas_call | solution.py:489
  35.7 0.0 collective-permute-done.3.inflow_ref
  (5 shorter events, 0.0 us)
Async XLA Ops:
  0.0 9.7 %copy-start = (s32[1,1,32,128]{3,2,1,0:T(8,128)S(1)}, s32[1,1,32,128]{3,2,1,0:T(8,128)}, u32[]{:S(2)}) copy-start(s32[1,1,32,128]{3,2,1,0:T(8,128)} %param.17) | copy-start | bytes 49156
  0.0 9.7 %copy-start.5 = (s32[1,1,32]{2,1,0:T(1,128)S(1)}, s32[1,1,32]{2,1,0:T(1,128)}, u32[]{:S(2)}) copy-start(s32[1,1,32]{2,1,0:T(1,128)} %param.16) | copy-start | bytes 388
  0.0 9.7 %copy-start.4 = (s32[128,1]{0,1:T(1,128)S(1)}, s32[128,1]{0,1:T(1,128)}, u32[]{:S(2)}) copy-start(s32[128,1]{0,1:T(1,128)} %param.13) | copy-start | bytes 1540
  0.0 9.7 %copy-start.3 = (f32[128,4]{0,1:T(4,128)S(1)}, f32[128,4]{0,1:T(4,128)}, u32[]{:S(2)}) copy-start(f32[128,4]{0,1:T(4,128)} %param.12) | copy-start | bytes 6148
  0.0 9.7 %copy-start.2 = (s32[128,4]{0,1:T(4,128)S(1)}, s32[128,4]{0,1:T(4,128)}, u32[]{:S(2)}) copy-start(s32[128,4]{0,1:T(4,128)} %param.11) | copy-start | bytes 6148
  0.0 11.0 %copy-start.6 = (f32[8]{0:T(128)S(1)}, f32[8]{0:T(128)}, u32[]{:S(2)}) copy-start(f32[8]{0:T(128)} %param.15) | copy-start | bytes 100
  0.0 11.0 %copy-start.1 = (f32[8,240]{1,0:T(8,128)S(1)}, f32[8,240]{1,0:T(8,128)}, u32[]{:S(2)}) copy-start(f32[8,240]{1,0:T(8,128)} %shape_ref.1) | copy-start | bytes 23044
  2.4 21.4 %all-to-all-start = ((bf16[16,64,240]{2,1,0:T(8,128)(2,1)}), bf16[16,64,240]{2,1,0:T(8,128)(2,1)S(1)}, u32[]{:S(2)}, u32[]{:S(2)}) async-start(bf16[16,64,240]{2,1,0:T(8,128)(2,1)} %bitcast.20), calls=%async_computation | async-start | bytes 1048576 | tf_op jit(solution)/shard_map/all_to_all | solution.py:410
  9.8 1.3 %collective-permute-start = (f32[64,128]{1,0:T(8,128)S(1)}, f32[64,128]{1,0:T(8,128)S(1)}, u32[]{:S(2)}, u32[]{:S(2)}) collective-permute-start(f32[64,128]{1,0:T(8,128)S(1)} %shard_map.92.own_ref), channel_id=1, source_target_pairs={{0,1},{1,0},{2,3},{3,2},{4,5},{5,4},{6,7},{7,6},{8,9},{9,8},{10,11... | collective-permute-start | bytes 98312 | tf_op jit(solution)/shard_map/ppermute | solution.py:425
  25.1 4.0 %collective-permute-start.2 = (bf16[8,64,240]{2,1,0:T(8,128)(2,1)S(1)}, bf16[8,64,240]{2,1,0:T(8,128)(2,1)S(1)}, u32[]{:S(2)}, u32[]{:S(2)}) collective-permute-start(bf16[8,64,240]{2,1,0:T(8,128)(2,1)S(1)} %get-tuple-element.32), channel_id=1, source_target_pairs={{0,1},{1,0},{2,3},{3,2},{4,5},{5,4},{6,7},{7,6},{8,9},{9,8},{10,11... | collective-permute-start | bytes 737288 | tf_op jit(solution)/shard_map/ppermute | solution.py:451
  25.7 7.5 %collective-permute-start.1 = (bf16[240,512]{1,0:T(8,128)(2,1)S(1)}, bf16[240,512]{1,0:T(8,128)(2,1)S(1)}, u32[]{:S(2)}, u32[]{:S(2)}) collective-permute-start(bf16[240,512]{1,0:T(8,128)(2,1)S(1)} %get-tuple-element.24), channel_id=1, source_target_pairs={{0,2},{2,0},{1,3},{3,1},{4,6},{6,4},{5,7},{7,5},{8,10},{10,8},{9,1... | collective-permute-start | bytes 737288 | tf_op jit(solution)/shard_map/ppermute | solution.py:450
  25.7 8.4 %collective-permute-start.4 = (bf16[240,512]{1,0:T(8,128)(2,1)S(1)}, bf16[240,512]{1,0:T(8,128)(2,1)S(1)}, u32[]{:S(2)}, u32[]{:S(2)}) collective-permute-start(bf16[240,512]{1,0:T(8,128)(2,1)S(1)} %get-tuple-element.28.inflow_ref), channel_id=1, source_target_pairs={{0,1},{1,0},{2,3},{3,2},{4,5},{5,4},{6,7},{7,6},{8,9},{9,8},{10,11... | collective-permute-start | bytes 737288 | tf_op jit(solution)/shard_map/ppermute | solution.py:452
  33.2 2.5 %collective-permute-start.3 = (bf16[240,512]{1,0:T(8,128)(2,1)S(1)}, bf16[240,512]{1,0:T(8,128)(2,1)S(1)}, u32[]{:S(2)}, u32[]{:S(2)}) collective-permute-start(bf16[240,512]{1,0:T(8,128)(2,1)S(1)} %get-tuple-element.34), channel_id=1, source_target_pairs={{0,1},{1,0},{2,3},{3,2},{4,5},{5,4},{6,7},{7,6},{8,9},{9,8},{10,11... | collective-permute-start | bytes 737288 | tf_op jit(solution)/shard_map/ppermute | solution.py:508

commit v8 on v7

--- a/solution.py
+++ b/solution.py
@@ -203,6 +203,13 @@
             link_ref[part * narrow : (part + 1) * narrow, m * reaches : (m + 1) * reaches] = piece
 
 
+def side_by_side(parts, right):
+    product = mm(jnp.concatenate(parts, axis=0), right)
+    count = parts[0].shape[0]
+    rows = [product[i * count : (i + 1) * count] for i in range(len(parts))]
+    return jnp.concatenate(rows, axis=1)
+
+
 def twice(rows_ref, sub, size):
     rows = rows_ref[:, sub * size : (sub + 1) * size, :]
     rows = rows.reshape(rows.shape[0] * size, rows.shape[2]).T
@@ -276,16 +283,13 @@
     regions, total, _ = rows_ref.shape
     size = wide_ref.shape[0] // 2 // regions
     width = wide_ref.shape[1]
-    step = max(cls_ref.shape[1], 256)
-    classes = tiled(cls_ref[0:1, :], step)
-    for sub in range(total // size):
-        rows = twice(rows_ref, sub, size)
-        for start in range(0, width, step):
-            lateral = mm(rows, wide_ref[:, start : start + step]).astype(BF)
-            place = sub * width + start
-            base_ref[:, place : place + step] = convolve(
-                table_ref[...], lateral, classes, class_count
-            )
+    parts = [twice(rows_ref, sub, size) for sub in range(total // size)]
+    classes = tiled(cls_ref[0:1, :], width)
+    lateral = side_by_side(parts, wide_ref[...]).astype(BF)
+    for start in range(0, base_ref.shape[1], width):
+        base_ref[:, start : start + width] = convolve(
+            table_ref[...], lateral[:, start : start + width], classes, class_count
+        )
 
 
 def base_own_kernel(

time: 36 us -> 36 us (level)
  Pallas kernels: 11.8 us -> 11 us
  waiting for transfers between devices: 14.6 us -> 15.4 us
    ppermute x1, waiting for transfers between devices: 1.87 us -> 2.7 us  [local(): lax.ppermute(panel, 'pair', [(0, 1), (1, 0)])]
    pallas_call x1, Pallas kernels: 2.24 us -> 1.83 us  [local(): call(functools.partial(base_kernel, class_count), base_shape, in_specs=[S...]
    pallas_call x1, Pallas kernels: 2.23 us -> 1.83 us  [local(): call(functools.partial(base_own_kernel, class_count), tuple(shapes), in_s...]
  transfers between devices with their start and end apart: 6 -> 6, of which waited for: 3 -> 3; matrix products, arithmetic and copies ran while one was open for 0% -> 0% of each run, Pallas kernels for 23% -> 20%
where the time goes in v8:
time: 36 us; the launch traced here: 35.8 us
  waiting for transfers between devices  15.4 us (43%)
  Pallas kernels  11 us (31%)
  starting transfers between devices  9.22 us (26%)
    all_to_all x1, waiting for transfers between devices, local(): lax.all_to_all(send.reshape(regions * 2, half * slot, hours), ('region',...  11.6 us
    all_to_all x1, starting transfers between devices, local(): lax.all_to_all(send.reshape(regions * 2, half * slot, hours), ('region',...  7.34 us
    ppermute x1, waiting for transfers between devices, local(): lax.ppermute(panel, 'pair', [(0, 1), (1, 0)])  2.7 us
    pallas_call x1, Pallas kernels, local(): call(functools.partial(pack_kernel, slot), struct((regions, 2, half * slo...  2.32 us
    pallas_call x1, Pallas kernels, local(): call(functools.partial(base_kernel, class_count), base_shape, in_specs=[S...  1.83 us
    pallas_call x1, Pallas kernels, local(): call(functools.partial(base_own_kernel, class_count), tuple(shapes), in_s...  1.83 us
    pallas_call x2, Pallas kernels, late(): call(functools.partial(late_kernel, class_count, top), struct((hours, mem...  1.7 us
    pallas_call x1, Pallas kernels, local(): call(functools.partial(head_kernel, class_count), (panel_shape, panel_sha...  1.32 us
  transfers between devices with their start and end apart: 6, of which 3 were waited for; matrix products, arithmetic and copies ran while one was open for 0% of the time, Pallas kernels for 20%

profile of v8, /device:TPU:1, one launch (start us, length us, event | category | flops | bytes accessed | tf_op | source)
XLA Modules:
  0.0 35.8 jit_solution(1375316273760559422)
XLA Ops:
  0.0 0.0 copy-start
  0.0 0.0 copy-start.5
  0.0 0.0 copy-start.3
  0.0 0.0 copy-start.2
  0.0 0.0 copy-start.6
  0.0 0.0 copy-start.1
  0.0 2.3 %shard_map.91 = bf16[8,2,64,240]{3,2,1,0:T(8,128)(2,1)} custom-call(f32[32,32,240]{2,1,0:T(8,128)} %bitcast.21, s32[1,32]{1,0:T(1,128)} %bitcast.22), custom_call_target="tpu_custom_call" | custom-call | flops 1 | bytes 1 | tf_op jit(solution)/shard_map/pallas_call | solution.py:400
  2.4 7.3 %all-to-all-start = ((bf16[16,64,240]{2,1,0:T(8,128)(2,1)}), bf16[16,64,240]{2,1,0:T(8,128)(2,1)S(1)}, u32[]{:S(2)}, u32[]{:S(2)}) async-start(bf16[16,64,240]{2,1,0:T(8,128)(2,1)} %bitcast.20), calls=%async_computation | async-start | bytes 1048576 | tf_op jit(solution)/shard_map/all_to_all | solution.py:414
  9.7 0.0 copy-done
  9.7 0.0 copy-done.5
  9.7 0.0 copy-done.4
  9.7 0.0 copy-done.3
  9.8 0.0 copy-done.2
  9.8 0.2 collective-permute-start
  9.9 1.1 %collective-permute-done.other_ref = f32[64,128]{1,0:T(8,128)S(1)} collective-permute-done((f32[64,128]{1,0:T(8,128)S(1)}, f32[64,128]{1,0:T(8,128)S(1)}, u32[]{:S(2)}, u32[]{:S(2)}) %collective-permute-start) | collective-permute-done | bytes 32800 | tf_op jit(solution)/shard_map/ppermute | solution.py:429
  11.0 0.0 copy-done.6
  11.1 0.0 copy-done.1
  11.1 1.1 %shard_map.93 = (bf16[240,256]{1,0:T(8,128)(2,1)S(1)}, bf16[2,256,128]{2,1,0:T(8,128)(2,1)S(1)}, bf16[2,256,256]{2,1,0:T(8,128)(2,1)S(1)}, f32[2,8,256]{2,1,0:T(...) custom-call(s32[1]{0:T(128)} %bitcast.core_ref, ...), custom_call_target="tpu_custom_call" | custom-call | flops 1 | bytes 1 | tf_op jit(solution)/shard_map/pallas_call | solution.py:430
  12.2 11.6 %all-to-all-done = bf16[16,64,240]{2,1,0:T(8,128)(2,1)S(1)} async-done(((bf16[16,64,240]{2,1,0:T(8,128)(2,1)}), bf16[16,64,240]{2,1,0:T(8,128)(2,1)S(1)}, u32[]{:S(2)}, u32[]{:S(2)}) %all-to-all-start) | async-done | bytes 491552 | tf_op jit(solution)/shard_map/all_to_all | solution.py:414
  23.8 1.3 %shard_map.94 = (bf16[240,512]{1,0:T(8,128)(2,1)S(1)}, bf16[240,512]{1,0:T(8,128)(2,1)S(1)}, bf16[8,64,240]{2,1,0:T(8,128)(2,1)S(1)}) custom-call(s32[1]{0:T(128)} %bitcast.core_ref, s32[1]{0:T(128)} %bitcast.1.pair_ref, bf16[8,2,64,240]{3,2,1,0:T(8,128)(2,1)S(1)} %bitcast.12, bf16[240,256]{1,0:T(8,128)(2,1)S(1)} %get-tuple-element.20.table_ref, ...), custom_call_target="tpu_custom_call" | custom-call | flops 1 | bytes 1 | tf_op jit(solution)/shard_map/pallas_call | solution.py:448
  25.1 0.5 %collective-permute-start.2 = (bf16[8,64,240]{2,1,0:T(8,128)(2,1)S(1)}, bf16[8,64,240]{2,1,0:T(8,128)(2,1)S(1)}, u32[]{:S(2)}, u32[]{:S(2)}) collective-permute-start(bf16[8,64,240]{2,1,0:T(8,128)(2,1)S(1)} %get-tuple-element.32), channel_id=1, source_target_pairs={{0,1},{1,0},{2,3},{3,2},{4,5},{5,4},{6,7},{7,6},{8,9},{9,8},{10,11... | collective-permute-start | bytes 737288 | tf_op jit(solution)/shard_map/ppermute | solution.py:455
  25.7 0.0 collective-permute-start.1
  25.7 0.3 collective-permute-start.4
  26.0 1.8 %shard_map.95 = (f32[240,2048]{1,0:T(8,128)S(1)}, f32[240,512]{1,0:T(8,128)S(1)}) custom-call(s32[1]{0:T(128)} %bitcast.core_ref, s32[1]{0:T(128)} %bitcast.1.pair_ref, bf16[8,2,64,240]{3,2,1,0:T(8,128)(2,1)S(1)} %bitcast.13, bf16[240,256]{1,0:T(8,128)(2,1)S(1)} %get-tuple-element.20.table_ref, bf16[256,512]{1,0:T(8,128)(2,1)S(1)} %get-tuple-element.25.wide_ref, ...), custom_call_target="tpu_custom_call" | custom-call | flops 1 | bytes 1 | tf_op jit(solution)/shard_map/pallas_call | solution.py:460
  27.8 0.8 %shard_map.96.rest_0_.done_ref = bf16[240,16,128]{2,1,0:T(8,128)(2,1)S(1)} custom-call(s32[1]{0:T(128)} %bitcast.core_ref, s32[1]{0:T(128)} %bitcast.1.pair_ref, bf16[240,512]{1,0:T(8,128)(2,1)S(1)} %get-tuple-element.28.inflow_ref, f32[240,2048]{1,0:T(8,128)S(1)} %get-tuple-element.29.base_ref, bf16[240,256]{1,0:T(8,128)(2,1)S(1)} %get-tuple-element.20.table_ref, ...), custom_call_target="tpu_custom_call" | custom-call | flops 1 | bytes 1 | tf_op jit(solution)/shard_map/pallas_call | solution.py:485
  28.7 0.0 collective-permute-done.2.rows_ref
  28.7 1.8 %shard_map.97.rest_1_.base_ref = f32[240,2048]{1,0:T(8,128)S(1)} custom-call(s32[1]{0:T(128)} %bitcast.core_ref, bf16[8,64,240]{2,1,0:T(8,128)(2,1)S(1)} %collective-permute-done.2.rows_ref, bf16[240,256]{1,0:T(8,128)(2,1)S(1)} %get-tuple-element.20.table_ref, bf16[256,512]{1,0:T(8,128)(2,1)S(1)} %get-tuple-element.25.wide_ref, ...), custom_call_target="tpu_custom_call" | custom-call | flops 1 | bytes 1 | tf_op jit(solution)/shard_map/pallas_call | solution.py:466
  30.5 2.7 %collective-permute-done.1.inflow_ref = bf16[240,512]{1,0:T(8,128)(2,1)S(1)} collective-permute-done((bf16[240,512]{1,0:T(8,128)(2,1)S(1)}, bf16[240,512]{1,0:T(8,128)(2,1)S(1)}, u32[]{:S(2)}, u32[]{:S(2)}) %collective-permute-start.1) | collective-permute-done | bytes 245792 | tf_op jit(solution)/shard_map/ppermute | solution.py:454
  33.2 0.8 %collective-permute-start.3 = (bf16[240,512]{1,0:T(8,128)(2,1)S(1)}, bf16[240,512]{1,0:T(8,128)(2,1)S(1)}, u32[]{:S(2)}, u32[]{:S(2)}) collective-permute-start(bf16[240,512]{1,0:T(8,128)(2,1)S(1)} %get-tuple-element.34), channel_id=1, source_target_pairs={{0,1},{1,0},{2,3},{3,2},{4,5},{5,4},{6,7},{7,6},{8,9},{9,8},{10,11... | collective-permute-start | bytes 737288 | tf_op jit(solution)/shard_map/ppermute | solution.py:512
  34.0 0.0 collective-permute-done.4.inflow_ref
  34.1 1.7 %shard_map.100.rest_0_ = bf16[240,32,128]{2,1,0:T(8,128)(2,1)} custom-call(s32[1]{0:T(128)} %bitcast.core_ref, s32[1]{0:T(128)} %bitcast.1.pair_ref, bf16[240,16,128]{2,1,0:T(8,128)(2,1)S(1)} %shard_map.96.rest_0_.done_ref, bf16[240,512]{1,0:T(8,128)(2,1)S(1)} %collective-permute-done.4.inflow_ref, f32[240,2048]{1,0:T(8,128)S(1)} %shard_map.97.rest_1_.base_ref, ...), custom_call_target="tpu_custom_call" | custom-call | flops 1 | bytes 1 | tf_op jit(solution)/shard_map/pallas_call | solution.py:493
  35.7 0.0 collective-permute-done.3.inflow_ref
  (5 shorter events, 0.0 us)
Async XLA Ops:
  0.0 9.7 %copy-start = (s32[1,1,32,128]{3,2,1,0:T(8,128)S(1)}, s32[1,1,32,128]{3,2,1,0:T(8,128)}, u32[]{:S(2)}) copy-start(s32[1,1,32,128]{3,2,1,0:T(8,128)} %param.17) | copy-start | bytes 49156
  0.0 9.7 %copy-start.5 = (s32[1,1,32]{2,1,0:T(1,128)S(1)}, s32[1,1,32]{2,1,0:T(1,128)}, u32[]{:S(2)}) copy-start(s32[1,1,32]{2,1,0:T(1,128)} %param.16) | copy-start | bytes 388
  0.0 9.7 %copy-start.4 = (s32[128,1]{0,1:T(1,128)S(1)}, s32[128,1]{0,1:T(1,128)}, u32[]{:S(2)}) copy-start(s32[128,1]{0,1:T(1,128)} %param.13) | copy-start | bytes 1540
  0.0 9.7 %copy-start.3 = (f32[128,4]{0,1:T(4,128)S(1)}, f32[128,4]{0,1:T(4,128)}, u32[]{:S(2)}) copy-start(f32[128,4]{0,1:T(4,128)} %param.12) | copy-start | bytes 6148
  0.0 9.7 %copy-start.2 = (s32[128,4]{0,1:T(4,128)S(1)}, s32[128,4]{0,1:T(4,128)}, u32[]{:S(2)}) copy-start(s32[128,4]{0,1:T(4,128)} %param.11) | copy-start | bytes 6148
  0.0 11.0 %copy-start.6 = (f32[8]{0:T(128)S(1)}, f32[8]{0:T(128)}, u32[]{:S(2)}) copy-start(f32[8]{0:T(128)} %param.15) | copy-start | bytes 100
  0.0 11.0 %copy-start.1 = (f32[8,240]{1,0:T(8,128)S(1)}, f32[8,240]{1,0:T(8,128)}, u32[]{:S(2)}) copy-start(f32[8,240]{1,0:T(8,128)} %shape_ref.1) | copy-start | bytes 23044
  2.4 21.4 %all-to-all-start = ((bf16[16,64,240]{2,1,0:T(8,128)(2,1)}), bf16[16,64,240]{2,1,0:T(8,128)(2,1)S(1)}, u32[]{:S(2)}, u32[]{:S(2)}) async-start(bf16[16,64,240]{2,1,0:T(8,128)(2,1)} %bitcast.20), calls=%async_computation | async-start | bytes 1048576 | tf_op jit(solution)/shard_map/all_to_all | solution.py:414
  9.8 1.3 %collective-permute-start = (f32[64,128]{1,0:T(8,128)S(1)}, f32[64,128]{1,0:T(8,128)S(1)}, u32[]{:S(2)}, u32[]{:S(2)}) collective-permute-start(f32[64,128]{1,0:T(8,128)S(1)} %shard_map.92.own_ref), channel_id=1, source_target_pairs={{0,1},{1,0},{2,3},{3,2},{4,5},{5,4},{6,7},{7,6},{8,9},{9,8},{10,11... | collective-permute-start | bytes 98312 | tf_op jit(solution)/shard_map/ppermute | solution.py:429
  25.1 3.6 %collective-permute-start.2 = (bf16[8,64,240]{2,1,0:T(8,128)(2,1)S(1)}, bf16[8,64,240]{2,1,0:T(8,128)(2,1)S(1)}, u32[]{:S(2)}, u32[]{:S(2)}) collective-permute-start(bf16[8,64,240]{2,1,0:T(8,128)(2,1)S(1)} %get-tuple-element.32), channel_id=1, source_target_pairs={{0,1},{1,0},{2,3},{3,2},{4,5},{5,4},{6,7},{7,6},{8,9},{9,8},{10,11... | collective-permute-start | bytes 737288 | tf_op jit(solution)/shard_map/ppermute | solution.py:455
  25.7 7.5 %collective-permute-start.1 = (bf16[240,512]{1,0:T(8,128)(2,1)S(1)}, bf16[240,512]{1,0:T(8,128)(2,1)S(1)}, u32[]{:S(2)}, u32[]{:S(2)}) collective-permute-start(bf16[240,512]{1,0:T(8,128)(2,1)S(1)} %get-tuple-element.24), channel_id=1, source_target_pairs={{0,2},{2,0},{1,3},{3,1},{4,6},{6,4},{5,7},{7,5},{8,10},{10,8},{9,1... | collective-permute-start | bytes 737288 | tf_op jit(solution)/shard_map/ppermute | solution.py:454
  25.7 8.4 %collective-permute-start.4 = (bf16[240,512]{1,0:T(8,128)(2,1)S(1)}, bf16[240,512]{1,0:T(8,128)(2,1)S(1)}, u32[]{:S(2)}, u32[]{:S(2)}) collective-permute-start(bf16[240,512]{1,0:T(8,128)(2,1)S(1)} %get-tuple-element.28.inflow_ref), channel_id=1, source_target_pairs={{0,1},{1,0},{2,3},{3,2},{4,5},{5,4},{6,7},{7,6},{8,9},{9,8},{10,11... | collective-permute-start | bytes 737288 | tf_op jit(solution)/shard_map/ppermute | solution.py:456
  33.2 2.5 %collective-permute-start.3 = (bf16[240,512]{1,0:T(8,128)(2,1)S(1)}, bf16[240,512]{1,0:T(8,128)(2,1)S(1)}, u32[]{:S(2)}, u32[]{:S(2)}) collective-permute-start(bf16[240,512]{1,0:T(8,128)(2,1)S(1)} %get-tuple-element.34), channel_id=1, source_target_pairs={{0,1},{1,0},{2,3},{3,2},{4,5},{5,4},{6,7},{7,6},{8,9},{9,8},{10,11... | collective-permute-start | bytes 737288 | tf_op jit(solution)/shard_map/ppermute | solution.py:512

commit v9 on v8

--- a/solution.py
+++ b/solution.py
@@ -11,6 +11,7 @@
 MB = 8
 SUB = 4
 LANES = 128
+SIDE = 2
 BLOCK = 32
 CHUNK = 256
 VMEM_LIMIT = 20 * 1024 * 1024
@@ -49,6 +50,11 @@
 
 
 SCALAR = pl.BlockSpec(memory_space=pltpu.SMEM)
+
+
+def region_at(place, regions):
+    rows = regions // SIDE
+    return (place % rows) * SIDE + place // rows
 
 
 def convolve(table, value, classes, class_count):
@@ -96,7 +102,7 @@
     count = regions * per
     recv = rows_ref.shape[1]
     row = iota((count, recv), 0)
-    wanted = (row // per) * slot + row % slot
+    wanted = region_at(row // per, regions) * slot + row % slot
     rows = rows_held[...].astype(F32)
     chosen = jnp.sum(jnp.where(iota((count, recv), 1) == wanted, rows, 0.0), axis=1, keepdims=True)
     lane = iota((count, MB * grid), 1)
@@ -154,7 +160,8 @@
         table_ref[:, k * BLOCK : (k + 1) * BLOCK] = rolled[:hours].astype(BF)
 
     row_p = iota((kap, recv), 0)
-    expand = one_hot((row_p // per) * slot + row_p % slot == iota((kap, recv), 1))
+    spot = region_at(row_p // per, recv // slot) * slot + row_p % slot
+    expand = one_hot(spot == iota((kap, recv), 1))
 
     def owner(width):
         return (iota((kap, width), 0) // slot) % SUB
@@ -377,7 +384,7 @@
     runoff, send_rows, remap_index, remap_weight, class_id, kernel_shape, kernel_rate, outlets, incidence
 ):
     hours, members, grid = runoff.shape
-    regions = lax.axis_size("region")
+    regions = lax.axis_size("row") * lax.axis_size("side")
     pairs = lax.axis_size("pair")
     class_count = kernel_shape.shape[0]
     reaches, columns = remap_index.shape
@@ -412,7 +419,7 @@
         ],
     )(jnp.transpose(runoff, (1, 2, 0)), send_rows.reshape(1, recv))
     received = lax.all_to_all(
-        send.reshape(regions * 2, half * slot, hours), ("region", "core"), 0, 0
+        send.reshape(regions * 2, half * slot, hours), ("side", "row", "core"), 0, 0
     ).reshape(regions, 2, half * slot, hours)
     raw = call(
         raw_kernel,
@@ -516,22 +523,25 @@
 
 def solution(mesh):
     regions, orders = mesh.shape["region"], mesh.shape["order"]
-    split_mesh = Mesh(mesh.devices.reshape(regions, orders // 2, 2), ("region", "pair", "core"))
+    split_mesh = Mesh(
+        mesh.devices.reshape(regions // SIDE, SIDE, orders // 2, 2), ("row", "side", "pair", "core")
+    )
+    region = ("row", "side")
     order = ("pair", "core")
-    every = ("region", "pair", "core")
+    every = region + order
     return jax.shard_map(
         local,
         mesh=split_mesh,
         in_specs=(
             P(None, None, every),
-            P("region", order, None),
+            P(region, order, None),
             P(every, None),
             P(every, None),
             P(every, None),
             P(),
             P(),
-            P("region", order, None),
-            P("region", order, None, None),
+            P(region, order, None),
+            P(region, order, None, None),
         ),
         out_specs=P(None, None, every),
         check_vma=False,

time: 36 us -> 35.8 us (level)
  waiting for transfers between devices: 15.4 us -> 14.9 us
    ppermute x1, waiting for transfers between devices: 2.7 us -> 1.91 us  [local(): lax.ppermute(panel, 'pair', [(0, 1), (1, 0)])]
    ppermute x1, starting transfers between devices: 0.55 us -> 0.09 us  [local(): rows_other = lax.ppermute(rows_send, 'core', swap)]
    ppermute x1, starting transfers between devices: 0.85 us -> 1.27 us  [local(): gotten = lax.ppermute(given, 'core', swap)]
where the time goes in v9:
time: 35.8 us; the launch traced here: 35.6 us
  waiting for transfers between devices  14.9 us (42%)
  Pallas kernels  11 us (31%)
  starting transfers between devices  9.58 us (27%)
    all_to_all x1, waiting for transfers between devices, local(): lax.all_to_all(send.reshape(regions * 2, half * slot, hours), ('side', 'r...  11.9 us
    all_to_all x1, starting transfers between devices, local(): lax.all_to_all(send.reshape(regions * 2, half * slot, hours), ('side', 'r...  7.34 us
    pallas_call x1, Pallas kernels, local(): call(functools.partial(pack_kernel, slot), struct((regions, 2, half * slo...  2.32 us
    ppermute x1, waiting for transfers between devices, local(): lax.ppermute(panel, 'pair', [(0, 1), (1, 0)])  1.91 us
    pallas_call x1, Pallas kernels, local(): call(functools.partial(base_kernel, class_count), base_shape, in_specs=[S...  1.83 us
    pallas_call x1, Pallas kernels, local(): call(functools.partial(base_own_kernel, class_count), tuple(shapes), in_s...  1.83 us
    pallas_call x2, Pallas kernels, late(): call(functools.partial(late_kernel, class_count, top), struct((hours, mem...  1.71 us
    pallas_call x1, Pallas kernels, local(): call(functools.partial(head_kernel, class_count), (panel_shape, panel_sha...  1.32 us
  transfers between devices with their start and end apart: 6, of which 3 were waited for; matrix products, arithmetic and copies ran while one was open for 0% of the time, Pallas kernels for 20%

profile of v9, /device:TPU:1, one launch (start us, length us, event | category | flops | bytes accessed | tf_op | source)
XLA Modules:
  0.0 35.6 jit_solution(2789732215674902680)
XLA Ops:
  0.0 0.0 copy-start
  0.0 0.0 copy-start.5
  0.0 0.0 copy-start.3
  0.0 0.0 copy-start.2
  0.0 0.0 copy-start.6
  0.0 0.0 copy-start.1
  0.0 2.3 %shard_map.91 = bf16[8,2,64,240]{3,2,1,0:T(8,128)(2,1)} custom-call(f32[32,32,240]{2,1,0:T(8,128)} %bitcast.21, s32[1,32]{1,0:T(1,128)} %bitcast.22), custom_call_target="tpu_custom_call" | custom-call | flops 1 | bytes 1 | tf_op jit(solution)/shard_map/pallas_call | solution.py:407
  2.4 7.3 %all-to-all-start = ((bf16[16,64,240]{2,1,0:T(8,128)(2,1)}), bf16[16,64,240]{2,1,0:T(8,128)(2,1)S(1)}, u32[]{:S(2)}, u32[]{:S(2)}) async-start(bf16[16,64,240]{2,1,0:T(8,128)(2,1)} %bitcast.20), calls=%async_computation | async-start | bytes 1048576 | tf_op jit(solution)/shard_map/all_to_all | solution.py:421
  9.7 0.0 copy-done
  9.7 0.0 copy-done.5
  9.7 0.0 copy-done.4
  9.7 0.0 copy-done.3
  9.8 0.0 copy-done.2
  9.8 0.2 collective-permute-start
  9.9 1.1 %collective-permute-done.other_ref = f32[64,128]{1,0:T(8,128)S(1)} collective-permute-done((f32[64,128]{1,0:T(8,128)S(1)}, f32[64,128]{1,0:T(8,128)S(1)}, u32[]{:S(2)}, u32[]{:S(2)}) %collective-permute-start) | collective-permute-done | bytes 32800 | tf_op jit(solution)/shard_map/ppermute | solution.py:436
  11.0 0.0 copy-done.6
  11.1 0.0 copy-done.1
  11.1 1.1 %shard_map.93 = (bf16[240,256]{1,0:T(8,128)(2,1)S(1)}, bf16[2,256,128]{2,1,0:T(8,128)(2,1)S(1)}, bf16[2,256,256]{2,1,0:T(8,128)(2,1)S(1)}, f32[2,8,256]{2,1,0:T(...) custom-call(s32[1]{0:T(128)} %bitcast.core_ref, ...), custom_call_target="tpu_custom_call" | custom-call | flops 1 | bytes 1 | tf_op jit(solution)/shard_map/pallas_call | solution.py:437
  12.2 11.9 %all-to-all-done = bf16[16,64,240]{2,1,0:T(8,128)(2,1)S(1)} async-done(((bf16[16,64,240]{2,1,0:T(8,128)(2,1)}), bf16[16,64,240]{2,1,0:T(8,128)(2,1)S(1)}, u32[]{:S(2)}, u32[]{:S(2)}) %all-to-all-start) | async-done | bytes 491552 | tf_op jit(solution)/shard_map/all_to_all | solution.py:421
  24.0 1.3 %shard_map.94 = (bf16[240,512]{1,0:T(8,128)(2,1)S(1)}, bf16[240,512]{1,0:T(8,128)(2,1)S(1)}, bf16[8,64,240]{2,1,0:T(8,128)(2,1)S(1)}) custom-call(s32[1]{0:T(128)} %bitcast.core_ref, s32[1]{0:T(128)} %bitcast.1.pair_ref, bf16[8,2,64,240]{3,2,1,0:T(8,128)(2,1)S(1)} %bitcast.12, bf16[240,256]{1,0:T(8,128)(2,1)S(1)} %get-tuple-element.20.table_ref, ...), custom_call_target="tpu_custom_call" | custom-call | flops 1 | bytes 1 | tf_op jit(solution)/shard_map/pallas_call | solution.py:455
  25.4 0.1 collective-permute-start.2
  25.5 0.0 collective-permute-start.1
  25.5 0.7 %collective-permute-start.4 = (bf16[240,512]{1,0:T(8,128)(2,1)S(1)}, bf16[240,512]{1,0:T(8,128)(2,1)S(1)}, u32[]{:S(2)}, u32[]{:S(2)}) collective-permute-start(bf16[240,512]{1,0:T(8,128)(2,1)S(1)} %get-tuple-element.28.inflow_ref), channel_id=1, source_target_pairs={{0,1},{1,0},{2,3},{3,2},{4,5},{5,4},{6,7},{7,6},{8,9},{9,8},{10,11... | collective-permute-start | bytes 737288 | tf_op jit(solution)/shard_map/ppermute | solution.py:463
  26.2 1.8 %shard_map.95 = (f32[240,2048]{1,0:T(8,128)S(1)}, f32[240,512]{1,0:T(8,128)S(1)}) custom-call(s32[1]{0:T(128)} %bitcast.core_ref, s32[1]{0:T(128)} %bitcast.1.pair_ref, bf16[8,2,64,240]{3,2,1,0:T(8,128)(2,1)S(1)} %bitcast.13, bf16[240,256]{1,0:T(8,128)(2,1)S(1)} %get-tuple-element.20.table_ref, bf16[256,512]{1,0:T(8,128)(2,1)S(1)} %get-tuple-element.25.wide_ref, ...), custom_call_target="tpu_custom_call" | custom-call | flops 1 | bytes 1 | tf_op jit(solution)/shard_map/pallas_call | solution.py:467
  28.0 0.8 %shard_map.96.rest_0_.done_ref = bf16[240,16,128]{2,1,0:T(8,128)(2,1)S(1)} custom-call(s32[1]{0:T(128)} %bitcast.core_ref, s32[1]{0:T(128)} %bitcast.1.pair_ref, bf16[240,512]{1,0:T(8,128)(2,1)S(1)} %get-tuple-element.28.inflow_ref, f32[240,2048]{1,0:T(8,128)S(1)} %get-tuple-element.29.base_ref, bf16[240,256]{1,0:T(8,128)(2,1)S(1)} %get-tuple-element.20.table_ref, ...), custom_call_target="tpu_custom_call" | custom-call | flops 1 | bytes 1 | tf_op jit(solution)/shard_map/pallas_call | solution.py:492
  28.8 0.0 collective-permute-done.2.rows_ref
  28.9 1.8 %shard_map.97.rest_1_.base_ref = f32[240,2048]{1,0:T(8,128)S(1)} custom-call(s32[1]{0:T(128)} %bitcast.core_ref, bf16[8,64,240]{2,1,0:T(8,128)(2,1)S(1)} %collective-permute-done.2.rows_ref, bf16[240,256]{1,0:T(8,128)(2,1)S(1)} %get-tuple-element.20.table_ref, bf16[256,512]{1,0:T(8,128)(2,1)S(1)} %get-tuple-element.25.wide_ref, ...), custom_call_target="tpu_custom_call" | custom-call | flops 1 | bytes 1 | tf_op jit(solution)/shard_map/pallas_call | solution.py:473
  30.7 1.9 %collective-permute-done.1.inflow_ref = bf16[240,512]{1,0:T(8,128)(2,1)S(1)} collective-permute-done((bf16[240,512]{1,0:T(8,128)(2,1)S(1)}, bf16[240,512]{1,0:T(8,128)(2,1)S(1)}, u32[]{:S(2)}, u32[]{:S(2)}) %collective-permute-start.1) | collective-permute-done | bytes 245792 | tf_op jit(solution)/shard_map/ppermute | solution.py:461
  32.6 1.3 %collective-permute-start.3 = (bf16[240,512]{1,0:T(8,128)(2,1)S(1)}, bf16[240,512]{1,0:T(8,128)(2,1)S(1)}, u32[]{:S(2)}, u32[]{:S(2)}) collective-permute-start(bf16[240,512]{1,0:T(8,128)(2,1)S(1)} %get-tuple-element.34), channel_id=1, source_target_pairs={{0,1},{1,0},{2,3},{3,2},{4,5},{5,4},{6,7},{7,6},{8,9},{9,8},{10,11... | collective-permute-start | bytes 737288 | tf_op jit(solution)/shard_map/ppermute | solution.py:519
  33.9 0.0 collective-permute-done.4.inflow_ref
  33.9 1.7 %shard_map.100.rest_0_ = bf16[240,32,128]{2,1,0:T(8,128)(2,1)} custom-call(s32[1]{0:T(128)} %bitcast.core_ref, s32[1]{0:T(128)} %bitcast.1.pair_ref, bf16[240,16,128]{2,1,0:T(8,128)(2,1)S(1)} %shard_map.96.rest_0_.done_ref, bf16[240,512]{1,0:T(8,128)(2,1)S(1)} %collective-permute-done.4.inflow_ref, f32[240,2048]{1,0:T(8,128)S(1)} %shard_map.97.rest_1_.base_ref, ...), custom_call_target="tpu_custom_call" | custom-call | flops 1 | bytes 1 | tf_op jit(solution)/shard_map/pallas_call | solution.py:500
  35.5 0.0 collective-permute-done.3.inflow_ref
  (5 shorter events, 0.0 us)
Async XLA Ops:
  0.0 9.7 %copy-start = (s32[1,1,32,128]{3,2,1,0:T(8,128)S(1)}, s32[1,1,32,128]{3,2,1,0:T(8,128)}, u32[]{:S(2)}) copy-start(s32[1,1,32,128]{3,2,1,0:T(8,128)} %param.17) | copy-start | bytes 49156
  0.0 9.7 %copy-start.5 = (s32[1,1,32]{2,1,0:T(1,128)S(1)}, s32[1,1,32]{2,1,0:T(1,128)}, u32[]{:S(2)}) copy-start(s32[1,1,32]{2,1,0:T(1,128)} %param.16) | copy-start | bytes 388
  0.0 9.7 %copy-start.4 = (s32[128,1]{0,1:T(1,128)S(1)}, s32[128,1]{0,1:T(1,128)}, u32[]{:S(2)}) copy-start(s32[128,1]{0,1:T(1,128)} %param.13) | copy-start | bytes 1540
  0.0 9.7 %copy-start.3 = (f32[128,4]{0,1:T(4,128)S(1)}, f32[128,4]{0,1:T(4,128)}, u32[]{:S(2)}) copy-start(f32[128,4]{0,1:T(4,128)} %param.12) | copy-start | bytes 6148
  0.0 9.7 %copy-start.2 = (s32[128,4]{0,1:T(4,128)S(1)}, s32[128,4]{0,1:T(4,128)}, u32[]{:S(2)}) copy-start(s32[128,4]{0,1:T(4,128)} %param.11) | copy-start | bytes 6148
  0.0 11.0 %copy-start.6 = (f32[8]{0:T(128)S(1)}, f32[8]{0:T(128)}, u32[]{:S(2)}) copy-start(f32[8]{0:T(128)} %param.15) | copy-start | bytes 100
  0.0 11.0 %copy-start.1 = (f32[8,240]{1,0:T(8,128)S(1)}, f32[8,240]{1,0:T(8,128)}, u32[]{:S(2)}) copy-start(f32[8,240]{1,0:T(8,128)} %shape_ref.1) | copy-start | bytes 23044
  2.4 21.7 %all-to-all-start = ((bf16[16,64,240]{2,1,0:T(8,128)(2,1)}), bf16[16,64,240]{2,1,0:T(8,128)(2,1)S(1)}, u32[]{:S(2)}, u32[]{:S(2)}) async-start(bf16[16,64,240]{2,1,0:T(8,128)(2,1)} %bitcast.20), calls=%async_computation | async-start | bytes 1048576 | tf_op jit(solution)/shard_map/all_to_all | solution.py:421
  9.8 1.3 %collective-permute-start = (f32[64,128]{1,0:T(8,128)S(1)}, f32[64,128]{1,0:T(8,128)S(1)}, u32[]{:S(2)}, u32[]{:S(2)}) collective-permute-start(f32[64,128]{1,0:T(8,128)S(1)} %shard_map.92.own_ref), channel_id=1, source_target_pairs={{0,1},{1,0},{2,3},{3,2},{4,5},{5,4},{6,7},{7,6},{8,9},{9,8},{10,11... | collective-permute-start | bytes 98312 | tf_op jit(solution)/shard_map/ppermute | solution.py:436
  25.4 3.5 %collective-permute-start.2 = (bf16[8,64,240]{2,1,0:T(8,128)(2,1)S(1)}, bf16[8,64,240]{2,1,0:T(8,128)(2,1)S(1)}, u32[]{:S(2)}, u32[]{:S(2)}) collective-permute-start(bf16[8,64,240]{2,1,0:T(8,128)(2,1)S(1)} %get-tuple-element.32), channel_id=1, source_target_pairs={{0,1},{1,0},{2,3},{3,2},{4,5},{5,4},{6,7},{7,6},{8,9},{9,8},{10,11... | collective-permute-start | bytes 737288 | tf_op jit(solution)/shard_map/ppermute | solution.py:462
  25.5 7.1 %collective-permute-start.1 = (bf16[240,512]{1,0:T(8,128)(2,1)S(1)}, bf16[240,512]{1,0:T(8,128)(2,1)S(1)}, u32[]{:S(2)}, u32[]{:S(2)}) collective-permute-start(bf16[240,512]{1,0:T(8,128)(2,1)S(1)} %get-tuple-element.24), channel_id=1, source_target_pairs={{0,2},{2,0},{1,3},{3,1},{4,6},{6,4},{5,7},{7,5},{8,10},{10,8},{9,1... | collective-permute-start | bytes 737288 | tf_op jit(solution)/shard_map/ppermute | solution.py:461
  25.5 8.4 %collective-permute-start.4 = (bf16[240,512]{1,0:T(8,128)(2,1)S(1)}, bf16[240,512]{1,0:T(8,128)(2,1)S(1)}, u32[]{:S(2)}, u32[]{:S(2)}) collective-permute-start(bf16[240,512]{1,0:T(8,128)(2,1)S(1)} %get-tuple-element.28.inflow_ref), channel_id=1, source_target_pairs={{0,1},{1,0},{2,3},{3,2},{4,5},{5,4},{6,7},{7,6},{8,9},{9,8},{10,11... | collective-permute-start | bytes 737288 | tf_op jit(solution)/shard_map/ppermute | solution.py:463
  32.6 3.0 %collective-permute-start.3 = (bf16[240,512]{1,0:T(8,128)(2,1)S(1)}, bf16[240,512]{1,0:T(8,128)(2,1)S(1)}, u32[]{:S(2)}, u32[]{:S(2)}) collective-permute-start(bf16[240,512]{1,0:T(8,128)(2,1)S(1)} %get-tuple-element.34), channel_id=1, source_target_pairs={{0,1},{1,0},{2,3},{3,2},{4,5},{5,4},{6,7},{7,6},{8,9},{9,8},{10,11... | collective-permute-start | bytes 737288 | tf_op jit(solution)/shard_map/ppermute | solution.py:519

commit v10 on v9

--- a/solution.py
+++ b/solution.py
@@ -347,6 +347,17 @@
     def _():
         high, low = routed_parts(class_count, top, core_ref, inflow_ref, table_ref, cls_ref)
         out_ref[...] = assemble(slice(0, hours), high, low, base_ref, link_ref, members, reaches)
+
+
+def other_kernel(
+    class_count, core_ref, pair_ref, rows_ref, table_ref, wide_ref, cls_ref, inflow_ref, base_own_ref,
+    link_ref, cls_target_ref, base_ref, done_ref,
+):
+    base_kernel(class_count, core_ref, rows_ref, table_ref, wide_ref, cls_ref, base_ref)
+    early_kernel(
+        class_count, True, core_ref, pair_ref, inflow_ref, base_own_ref, table_ref, link_ref,
+        cls_target_ref, done_ref,
+    )
 
 
 def late_kernel(
@@ -470,12 +481,12 @@
         in_specs=[SCALAR] * 2 + vmem(6),
         out_specs=tuple(vmem(len(shapes))),
     )(core_arg, pair_arg, received, table, wide_mix, cls_own, mix, cls_out)
-    base_other = call(
-        functools.partial(base_kernel, class_count),
-        base_shape,
-        in_specs=[SCALAR] + vmem(4),
-        out_specs=vmem(1)[0],
-    )(core_arg, rows_other, table, wide_mix, cls_own)
+    base_other, done_first = call(
+        functools.partial(other_kernel, class_count),
+        (base_shape, struct((hours, half, reaches), BF)),
+        in_specs=[SCALAR] * 2 + vmem(8),
+        out_specs=tuple(vmem(2)),
+    )(core_arg, pair_arg, rows_other, table, wide_mix, cls_own, first, base_own, link, cls_target)
 
 
     for step in range(1, pairs - 1):
@@ -509,13 +520,12 @@
             input_output_aliases={8: 0} if before else {},
         )(core_arg, pair_arg, done, gotten, base_other, table, link, cls_target, *before)
 
-    done_first = early(True, first)
     own, given = call(
         functools.partial(last_hop_kernel, class_count),
         (panel_shape, panel_shape),
-        in_specs=[SCALAR] * 2 + vmem(5) + [anywhere] * 2,
+        in_specs=[SCALAR] * 2 + vmem(5) + [anywhere],
         out_specs=tuple(vmem(2)),
-    )(core_arg, pair_arg, inflow, table, passing, cls_out, even, done_first, base_other)
+    )(core_arg, pair_arg, inflow, table, passing, cls_out, even, done_first)
     gotten = lax.ppermute(given, "core", swap)
     out = late(True, done_first, first_other, [])
     return late(False, early(False, own), gotten, [out])

time: 35.8 us -> 35.8 us (level)
    pallas_call x1, Pallas kernels: 1.83 us -> 2.69 us  [local(): call(functools.partial(other_kernel, class_count), (base_shape, struct((h...]
    pallas_call x2 -> x1, Pallas kernels: 0.84 us -> 0.01 us  [early(): call(functools.partial(early_kernel, class_count, top), struct((hours, ha...]
  transfers between devices with their start and end apart: 6 -> 6, of which waited for: 3 -> 3; matrix products, arithmetic and copies ran while one was open for 0% -> 0% of each run, Pallas kernels for 20% -> 21%
where the time goes in v10:
time: 35.8 us; the launch traced here: 35.6 us
  waiting for transfers between devices  14.9 us (42%)
  Pallas kernels  11 us (31%)
  starting transfers between devices  9.58 us (27%)
    all_to_all x1, waiting for transfers between devices, local(): lax.all_to_all(send.reshape(regions * 2, half * slot, hours), ('side', 'r...  11.9 us
    all_to_all x1, starting transfers between devices, local(): lax.all_to_all(send.reshape(regions * 2, half * slot, hours), ('side', 'r...  7.34 us
    pallas_call x1, Pallas kernels, local(): call(functools.partial(other_kernel, class_count), (base_shape, struct((h...  2.69 us
    pallas_call x1, Pallas kernels, local(): call(functools.partial(pack_kernel, slot), struct((regions, 2, half * slo...  2.32 us
    ppermute x1, waiting for transfers between devices, local(): lax.ppermute(panel, 'pair', [(0, 1), (1, 0)])  1.89 us
    pallas_call x1, Pallas kernels, local(): call(functools.partial(base_own_kernel, class_count), tuple(shapes), in_s...  1.83 us
    pallas_call x2, Pallas kernels, late(): call(functools.partial(late_kernel, class_count, top), struct((hours, mem...  1.71 us
    pallas_call x1, Pallas kernels, local(): call(functools.partial(head_kernel, class_count), (panel_shape, panel_sha...  1.32 us
  transfers between devices with their start and end apart: 6, of which 3 were waited for; matrix products, arithmetic and copies ran while one was open for 0% of the time, Pallas kernels for 21%

profile of v10, /device:TPU:1, one launch (start us, length us, event | category | flops | bytes accessed | tf_op | source)
XLA Modules:
  0.0 35.6 jit_solution(13375380308442771643)
XLA Ops:
  0.0 0.0 copy-start
  0.0 0.0 copy-start.5
  0.0 0.0 copy-start.4
  0.0 0.0 copy-start.3
  0.0 0.0 copy-start.2
  0.0 0.0 copy-start.6
  0.0 0.0 copy-start.1
  0.0 2.3 %shard_map.91 = bf16[8,2,64,240]{3,2,1,0:T(8,128)(2,1)} custom-call(f32[32,32,240]{2,1,0:T(8,128)} %bitcast.21, s32[1,32]{1,0:T(1,128)} %bitcast.22), custom_call_target="tpu_custom_call" | custom-call | flops 1 | bytes 1 | tf_op jit(solution)/shard_map/pallas_call | solution.py:418
  2.4 7.3 %all-to-all-start = ((bf16[16,64,240]{2,1,0:T(8,128)(2,1)}), bf16[16,64,240]{2,1,0:T(8,128)(2,1)S(1)}, u32[]{:S(2)}, u32[]{:S(2)}) async-start(bf16[16,64,240]{2,1,0:T(8,128)(2,1)} %bitcast.20), calls=%async_computation | async-start | bytes 1048576 | tf_op jit(solution)/shard_map/all_to_all | solution.py:432
  9.7 0.0 copy-done
  9.7 0.0 copy-done.5
  9.7 0.0 copy-done.4
  9.7 0.0 copy-done.3
  9.8 0.0 copy-done.2
  9.8 0.2 collective-permute-start
  9.9 1.1 %collective-permute-done.other_ref = f32[64,128]{1,0:T(8,128)S(1)} collective-permute-done((f32[64,128]{1,0:T(8,128)S(1)}, f32[64,128]{1,0:T(8,128)S(1)}, u32[]{:S(2)}, u32[]{:S(2)}) %collective-permute-start) | collective-permute-done | bytes 32800 | tf_op jit(solution)/shard_map/ppermute | solution.py:447
  11.0 0.0 copy-done.6
  11.1 0.0 copy-done.1
  11.1 1.1 %shard_map.93 = (bf16[240,256]{1,0:T(8,128)(2,1)S(1)}, bf16[2,256,128]{2,1,0:T(8,128)(2,1)S(1)}, bf16[2,256,256]{2,1,0:T(8,128)(2,1)S(1)}, f32[2,8,256]{2,1,0:T(...) custom-call(s32[1]{0:T(128)} %bitcast.core_ref, ...), custom_call_target="tpu_custom_call" | custom-call | flops 1 | bytes 1 | tf_op jit(solution)/shard_map/pallas_call | solution.py:448
  12.2 11.9 %all-to-all-done = bf16[16,64,240]{2,1,0:T(8,128)(2,1)S(1)} async-done(((bf16[16,64,240]{2,1,0:T(8,128)(2,1)}), bf16[16,64,240]{2,1,0:T(8,128)(2,1)S(1)}, u32[]{:S(2)}, u32[]{:S(2)}) %all-to-all-start) | async-done | bytes 491552 | tf_op jit(solution)/shard_map/all_to_all | solution.py:432
  24.0 1.3 %shard_map.94 = (bf16[240,512]{1,0:T(8,128)(2,1)S(1)}, bf16[240,512]{1,0:T(8,128)(2,1)S(1)}, bf16[8,64,240]{2,1,0:T(8,128)(2,1)S(1)}) custom-call(s32[1]{0:T(128)} %bitcast.core_ref, s32[1]{0:T(128)} %bitcast.1.pair_ref, bf16[8,2,64,240]{3,2,1,0:T(8,128)(2,1)S(1)} %bitcast.12, bf16[240,256]{1,0:T(8,128)(2,1)S(1)} %get-tuple-element.22.table_ref, ...), custom_call_target="tpu_custom_call" | custom-call | flops 1 | bytes 1 | tf_op jit(solution)/shard_map/pallas_call | solution.py:466
  25.4 0.1 collective-permute-start.2
  25.5 0.0 collective-permute-start.1
  25.5 0.7 %collective-permute-start.4 = (bf16[240,512]{1,0:T(8,128)(2,1)S(1)}, bf16[240,512]{1,0:T(8,128)(2,1)S(1)}, u32[]{:S(2)}, u32[]{:S(2)}) collective-permute-start(bf16[240,512]{1,0:T(8,128)(2,1)S(1)} %get-tuple-element.31.inflow_ref), channel_id=1, source_target_pairs={{0,1},{1,0},{2,3},{3,2},{4,5},{5,4},{6,7},{7,6},{8,9},{9,8},{10,11... | collective-permute-start | bytes 737288 | tf_op jit(solution)/shard_map/ppermute | solution.py:474
  26.2 1.8 %shard_map.95 = (f32[240,2048]{1,0:T(8,128)S(1)}, f32[240,512]{1,0:T(8,128)S(1)}) custom-call(s32[1]{0:T(128)} %bitcast.core_ref, s32[1]{0:T(128)} %bitcast.1.pair_ref, bf16[8,2,64,240]{3,2,1,0:T(8,128)(2,1)S(1)} %bitcast.13, bf16[240,256]{1,0:T(8,128)(2,1)S(1)} %get-tuple-element.22.table_ref, bf16[256,512]{1,0:T(8,128)(2,1)S(1)} %get-tuple-element.27.wide_ref, ...), custom_call_target="tpu_custom_call" | custom-call | flops 1 | bytes 1 | tf_op jit(solution)/shard_map/pallas_call | solution.py:478
  28.0 0.0 collective-permute-done.2.rows_ref
  28.0 2.7 %shard_map.96 = (f32[240,2048]{1,0:T(8,128)S(1)}, bf16[240,16,128]{2,1,0:T(8,128)(2,1)S(1)}) custom-call(s32[1]{0:T(128)} %bitcast.core_ref, s32[1]{0:T(128)} %bitcast.1.pair_ref, bf16[8,64,240]{2,1,0:T(8,128)(2,1)S(1)} %collective-permute-done.2.rows_ref, bf16[240,256]{1,0:T(8,128)(2,1)S(1)} %get-tuple-element.22.table_ref, ...), custom_call_target="tpu_custom_call" | custom-call | flops 1 | bytes 1 | tf_op jit(solution)/shard_map/pallas_call | solution.py:484
  30.7 1.9 %collective-permute-done.1.inflow_ref = bf16[240,512]{1,0:T(8,128)(2,1)S(1)} collective-permute-done((bf16[240,512]{1,0:T(8,128)(2,1)S(1)}, bf16[240,512]{1,0:T(8,128)(2,1)S(1)}, u32[]{:S(2)}, u32[]{:S(2)}) %collective-permute-start.1) | collective-permute-done | bytes 245792 | tf_op jit(solution)/shard_map/ppermute | solution.py:472
  32.6 1.3 %collective-permute-start.3 = (bf16[240,512]{1,0:T(8,128)(2,1)S(1)}, bf16[240,512]{1,0:T(8,128)(2,1)S(1)}, u32[]{:S(2)}, u32[]{:S(2)}) collective-permute-start(bf16[240,512]{1,0:T(8,128)(2,1)S(1)} %get-tuple-element.37), channel_id=1, source_target_pairs={{0,1},{1,0},{2,3},{3,2},{4,5},{5,4},{6,7},{7,6},{8,9},{9,8},{10,11... | collective-permute-start | bytes 737288 | tf_op jit(solution)/shard_map/ppermute | solution.py:529
  33.9 0.0 collective-permute-done.4.inflow_ref
  33.9 1.7 %shard_map.99.rest_0_ = bf16[240,32,128]{2,1,0:T(8,128)(2,1)} custom-call(s32[1]{0:T(128)} %bitcast.core_ref, s32[1]{0:T(128)} %bitcast.1.pair_ref, bf16[240,16,128]{2,1,0:T(8,128)(2,1)S(1)} %get-tuple-element.35.rest_0_.done_ref, bf16[240,512]{1,0:T(8,128)(2,1)S(1)} %collective-permute-done.4.inflow_ref, f32[240,2048]{1,0:T(8,128)S(1)} %get-tuple-element.38.base_ref, ...), custom_call_target="tpu_custom_call" | custom-call | flops 1 | bytes 1 | tf_op jit(solution)/shard_map/pallas_call | solution.py:511
  35.5 0.0 collective-permute-done.3.inflow_ref
  (4 shorter events, 0.0 us)
Async XLA Ops:
  0.0 9.7 %copy-start = (s32[1,1,32,128]{3,2,1,0:T(8,128)S(1)}, s32[1,1,32,128]{3,2,1,0:T(8,128)}, u32[]{:S(2)}) copy-start(s32[1,1,32,128]{3,2,1,0:T(8,128)} %param.17) | copy-start | bytes 49156
  0.0 9.7 %copy-start.5 = (s32[1,1,32]{2,1,0:T(1,128)S(1)}, s32[1,1,32]{2,1,0:T(1,128)}, u32[]{:S(2)}) copy-start(s32[1,1,32]{2,1,0:T(1,128)} %param.16) | copy-start | bytes 388
  0.0 9.7 %copy-start.4 = (s32[128,1]{0,1:T(1,128)S(1)}, s32[128,1]{0,1:T(1,128)}, u32[]{:S(2)}) copy-start(s32[128,1]{0,1:T(1,128)} %param.13) | copy-start | bytes 1540
  0.0 9.7 %copy-start.3 = (f32[128,4]{0,1:T(4,128)S(1)}, f32[128,4]{0,1:T(4,128)}, u32[]{:S(2)}) copy-start(f32[128,4]{0,1:T(4,128)} %param.12) | copy-start | bytes 6148
  0.0 9.7 %copy-start.2 = (s32[128,4]{0,1:T(4,128)S(1)}, s32[128,4]{0,1:T(4,128)}, u32[]{:S(2)}) copy-start(s32[128,4]{0,1:T(4,128)} %param.11) | copy-start | bytes 6148
  0.0 11.0 %copy-start.6 = (f32[8]{0:T(128)S(1)}, f32[8]{0:T(128)}, u32[]{:S(2)}) copy-start(f32[8]{0:T(128)} %param.15) | copy-start | bytes 100
  0.0 11.0 %copy-start.1 = (f32[8,240]{1,0:T(8,128)S(1)}, f32[8,240]{1,0:T(8,128)}, u32[]{:S(2)}) copy-start(f32[8,240]{1,0:T(8,128)} %shape_ref.1) | copy-start | bytes 23044
  2.4 21.7 %all-to-all-start = ((bf16[16,64,240]{2,1,0:T(8,128)(2,1)}), bf16[16,64,240]{2,1,0:T(8,128)(2,1)S(1)}, u32[]{:S(2)}, u32[]{:S(2)}) async-start(bf16[16,64,240]{2,1,0:T(8,128)(2,1)} %bitcast.20), calls=%async_computation | async-start | bytes 1048576 | tf_op jit(solution)/shard_map/all_to_all | solution.py:432
  9.8 1.3 %collective-permute-start = (f32[64,128]{1,0:T(8,128)S(1)}, f32[64,128]{1,0:T(8,128)S(1)}, u32[]{:S(2)}, u32[]{:S(2)}) collective-permute-start(f32[64,128]{1,0:T(8,128)S(1)} %shard_map.92.own_ref), channel_id=1, source_target_pairs={{0,1},{1,0},{2,3},{3,2},{4,5},{5,4},{6,7},{7,6},{8,9},{9,8},{10,11... | collective-permute-start | bytes 98312 | tf_op jit(solution)/shard_map/ppermute | solution.py:447
  25.4 2.6 %collective-permute-start.2 = (bf16[8,64,240]{2,1,0:T(8,128)(2,1)S(1)}, bf16[8,64,240]{2,1,0:T(8,128)(2,1)S(1)}, u32[]{:S(2)}, u32[]{:S(2)}) collective-permute-start(bf16[8,64,240]{2,1,0:T(8,128)(2,1)S(1)} %get-tuple-element.30), channel_id=1, source_target_pairs={{0,1},{1,0},{2,3},{3,2},{4,5},{5,4},{6,7},{7,6},{8,9},{9,8},{10,11... | collective-permute-start | bytes 737288 | tf_op jit(solution)/shard_map/ppermute | solution.py:473
  25.5 7.1 %collective-permute-start.1 = (bf16[240,512]{1,0:T(8,128)(2,1)S(1)}, bf16[240,512]{1,0:T(8,128)(2,1)S(1)}, u32[]{:S(2)}, u32[]{:S(2)}) collective-permute-start(bf16[240,512]{1,0:T(8,128)(2,1)S(1)} %get-tuple-element.26), channel_id=1, source_target_pairs={{0,2},{2,0},{1,3},{3,1},{4,6},{6,4},{5,7},{7,5},{8,10},{10,8},{9,1... | collective-permute-start | bytes 737288 | tf_op jit(solution)/shard_map/ppermute | solution.py:472
  25.5 8.4 %collective-permute-start.4 = (bf16[240,512]{1,0:T(8,128)(2,1)S(1)}, bf16[240,512]{1,0:T(8,128)(2,1)S(1)}, u32[]{:S(2)}, u32[]{:S(2)}) collective-permute-start(bf16[240,512]{1,0:T(8,128)(2,1)S(1)} %get-tuple-element.31.inflow_ref), channel_id=1, source_target_pairs={{0,1},{1,0},{2,3},{3,2},{4,5},{5,4},{6,7},{7,6},{8,9},{9,8},{10,11... | collective-permute-start | bytes 737288 | tf_op jit(solution)/shard_map/ppermute | solution.py:474
  32.6 3.0 %collective-permute-start.3 = (bf16[240,512]{1,0:T(8,128)(2,1)S(1)}, bf16[240,512]{1,0:T(8,128)(2,1)S(1)}, u32[]{:S(2)}, u32[]{:S(2)}) collective-permute-start(bf16[240,512]{1,0:T(8,128)(2,1)S(1)} %get-tuple-element.37), channel_id=1, source_target_pairs={{0,1},{1,0},{2,3},{3,2},{4,5},{5,4},{6,7},{7,6},{8,9},{9,8},{10,11... | collective-permute-start | bytes 737288 | tf_op jit(solution)/shard_map/ppermute | solution.py:529

commit v11 on v9

--- a/solution.py
+++ b/solution.py
@@ -244,12 +244,14 @@
     return jnp.concatenate(parts, axis=1)
 
 
+def rows_kernel(core_ref, rows_ref, send_ref):
+    send_ref[...] = rows_ref[:, 1 - core_ref[0]]
+
+
 def head_kernel(
-    class_count, core_ref, pair_ref, rows_ref, table_ref, mix_ref, pass_ref, cls_ref,
-    panel_ref, first_ref, send_ref,
+    class_count, pair_ref, rows_ref, table_ref, mix_ref, pass_ref, cls_ref, after_ref,
+    panel_ref, first_ref,
 ):
-    send_ref[...] = jnp.where(core_ref[0] == 0, rows_ref[:, 1], rows_ref[:, 0])
-
     @pl.when(pair_ref[0] == 0)
     def _():
         wide = panel_ref.shape[1]
@@ -452,12 +454,18 @@
 
     panel_shape = struct((hours, wide), BF)
     float_shape = struct((hours, wide), F32)
-    panel, first, rows_send = call(
+    rows_send = call(
+        rows_kernel,
+        struct((regions, half * slot, hours), BF),
+        in_specs=[SCALAR] + vmem(1),
+        out_specs=vmem(1)[0],
+    )(core_arg, received)
+    panel, first = call(
         functools.partial(head_kernel, class_count),
-        (panel_shape, panel_shape, struct((regions, half * slot, hours), BF)),
-        in_specs=[SCALAR] * 2 + vmem(5),
-        out_specs=tuple(vmem(3)),
-    )(core_arg, pair_arg, received, table, mix, passing, cls_out)
+        (panel_shape, panel_shape),
+        in_specs=[SCALAR] + vmem(6),
+        out_specs=tuple(vmem(2)),
+    )(pair_arg, received, table, mix, passing, cls_out, rows_send)
     inflow = lax.ppermute(panel, "pair", [(0, 1), (1, 0)]) if pairs > 1 else panel
     rows_other = lax.ppermute(rows_send, "core", swap)
     first_other = lax.ppermute(first, "core", swap)

time: 35.8 us -> 35.8 us (level)
  transfers between devices with their start and end apart: 6 -> 6, of which waited for: 3 -> 3; matrix products, arithmetic and copies ran while one was open for 0% -> 0% of each run, Pallas kernels for 20% -> 24%
where the time goes in v11:
time: 35.8 us; the launch traced here: 35.6 us
  waiting for transfers between devices  14.9 us (42%)
  Pallas kernels  10.9 us (30%)
  starting transfers between devices  9.62 us (27%)
    all_to_all x1, waiting for transfers between devices, local(): lax.all_to_all(send.reshape(regions * 2, half * slot, hours), ('side', 'r...  11.9 us
    all_to_all x1, starting transfers between devices, local(): lax.all_to_all(send.reshape(regions * 2, half * slot, hours), ('side', 'r...  7.34 us
    pallas_call x1, Pallas kernels, local(): call(functools.partial(pack_kernel, slot), struct((regions, 2, half * slo...  2.32 us
    ppermute x1, waiting for transfers between devices, local(): lax.ppermute(panel, 'pair', [(0, 1), (1, 0)])  1.89 us
    pallas_call x1, Pallas kernels, local(): call(functools.partial(base_own_kernel, class_count), tuple(shapes), in_s...  1.83 us
    pallas_call x1, Pallas kernels, local(): call(functools.partial(base_kernel, class_count), base_shape, in_specs=[S...  1.83 us
    pallas_call x2, Pallas kernels, late(): call(functools.partial(late_kernel, class_count, top), struct((hours, mem...  1.7 us
    ppermute x1, starting transfers between devices, local(): gotten = lax.ppermute(given, 'core', swap)  1.32 us
  transfers between devices with their start and end apart: 6, of which 3 were waited for; matrix products, arithmetic and copies ran while one was open for 0% of the time, Pallas kernels for 24%

profile of v11, /device:TPU:1, one launch (start us, length us, event | category | flops | bytes accessed | tf_op | source)
XLA Modules:
  0.0 35.6 jit_solution(17711548182375678780)
XLA Ops:
  0.0 0.0 copy-start
  0.0 0.0 copy-start.5
  0.0 0.0 copy-start.3
  0.0 0.0 copy-start.2
  0.0 0.0 copy-start.6
  0.0 0.0 copy-start.1
  0.0 2.3 %shard_map.91 = bf16[8,2,64,240]{3,2,1,0:T(8,128)(2,1)} custom-call(f32[32,32,240]{2,1,0:T(8,128)} %bitcast.22, s32[1,32]{1,0:T(1,128)} %bitcast.23), custom_call_target="tpu_custom_call" | custom-call | flops 1 | bytes 1 | tf_op jit(solution)/shard_map/pallas_call | solution.py:409
  2.4 7.3 %all-to-all-start = ((bf16[16,64,240]{2,1,0:T(8,128)(2,1)}), bf16[16,64,240]{2,1,0:T(8,128)(2,1)S(1)}, u32[]{:S(2)}, u32[]{:S(2)}) async-start(bf16[16,64,240]{2,1,0:T(8,128)(2,1)} %bitcast.21), calls=%async_computation | async-start | bytes 1048576 | tf_op jit(solution)/shard_map/all_to_all | solution.py:423
  9.7 0.0 copy-done
  9.7 0.0 copy-done.5
  9.7 0.0 copy-done.4
  9.7 0.0 copy-done.3
  9.8 0.0 copy-done.2
  9.8 0.2 collective-permute-start
  9.9 1.1 %collective-permute-done.other_ref = f32[64,128]{1,0:T(8,128)S(1)} collective-permute-done((f32[64,128]{1,0:T(8,128)S(1)}, f32[64,128]{1,0:T(8,128)S(1)}, u32[]{:S(2)}, u32[]{:S(2)}) %collective-permute-start) | collective-permute-done | bytes 32800 | tf_op jit(solution)/shard_map/ppermute | solution.py:438
  11.0 0.0 copy-done.6
  11.1 0.0 copy-done.1
  11.1 1.1 %shard_map.93 = (bf16[240,256]{1,0:T(8,128)(2,1)S(1)}, bf16[2,256,128]{2,1,0:T(8,128)(2,1)S(1)}, bf16[2,256,256]{2,1,0:T(8,128)(2,1)S(1)}, f32[2,8,256]{2,1,0:T(...) custom-call(s32[1]{0:T(128)} %bitcast.core_ref, ...), custom_call_target="tpu_custom_call" | custom-call | flops 1 | bytes 1 | tf_op jit(solution)/shard_map/pallas_call | solution.py:439
  12.2 11.9 %all-to-all-done = bf16[16,64,240]{2,1,0:T(8,128)(2,1)S(1)} async-done(((bf16[16,64,240]{2,1,0:T(8,128)(2,1)}), bf16[16,64,240]{2,1,0:T(8,128)(2,1)S(1)}, u32[]{:S(2)}, u32[]{:S(2)}) %all-to-all-start) | async-done | bytes 491552 | tf_op jit(solution)/shard_map/all_to_all | solution.py:423
  24.1 0.1 collective-permute-start.2
  24.2 1.3 %shard_map.95 = (bf16[240,512]{1,0:T(8,128)(2,1)S(1)}, bf16[240,512]{1,0:T(8,128)(2,1)S(1)}) custom-call(s32[1]{0:T(128)} %bitcast.1.pair_ref, bf16[8,2,64,240]{3,2,1,0:T(8,128)(2,1)S(1)} %bitcast.13, bf16[240,256]{1,0:T(8,128)(2,1)S(1)} %get-tuple-element.19.table_ref, bf16[2,256,128]{2,1,0:T(8,128)(2,1)S(1)} %get-tuple-element.20.mix_ref, ...), custom_call_target="tpu_custom_call" | custom-call | flops 1 | bytes 1 | tf_op jit(solution)/shard_map/pallas_call | solution.py:463
  25.5 0.1 collective-permute-start.1
  25.5 0.6 %collective-permute-start.4 = (bf16[240,512]{1,0:T(8,128)(2,1)S(1)}, bf16[240,512]{1,0:T(8,128)(2,1)S(1)}, u32[]{:S(2)}, u32[]{:S(2)}) collective-permute-start(bf16[240,512]{1,0:T(8,128)(2,1)S(1)} %get-tuple-element.27.inflow_ref), channel_id=1, source_target_pairs={{0,1},{1,0},{2,3},{3,2},{4,5},{5,4},{6,7},{7,6},{8,9},{9,8},{10,11... | collective-permute-start | bytes 737288 | tf_op jit(solution)/shard_map/ppermute | solution.py:471
  26.2 1.8 %shard_map.96 = (f32[240,2048]{1,0:T(8,128)S(1)}, f32[240,512]{1,0:T(8,128)S(1)}) custom-call(s32[1]{0:T(128)} %bitcast.core_ref, s32[1]{0:T(128)} %bitcast.1.pair_ref, bf16[8,2,64,240]{3,2,1,0:T(8,128)(2,1)S(1)} %bitcast.14, bf16[240,256]{1,0:T(8,128)(2,1)S(1)} %get-tuple-element.19.table_ref, bf16[256,512]{1,0:T(8,128)(2,1)S(1)} %get-tuple-element.24.wide_ref, ...), custom_call_target="tpu_custom_call" | custom-call | flops 1 | bytes 1 | tf_op jit(solution)/shard_map/pallas_call | solution.py:475
  28.0 0.8 %shard_map.97.rest_0_.done_ref = bf16[240,16,128]{2,1,0:T(8,128)(2,1)S(1)} custom-call(s32[1]{0:T(128)} %bitcast.core_ref, s32[1]{0:T(128)} %bitcast.1.pair_ref, bf16[240,512]{1,0:T(8,128)(2,1)S(1)} %get-tuple-element.27.inflow_ref, f32[240,2048]{1,0:T(8,128)S(1)} %get-tuple-element.28.base_ref, bf16[240,256]{1,0:T(8,128)(2,1)S(1)} %get-tuple-element.19.table_ref, ...), custom_call_target="tpu_custom_call" | custom-call | flops 1 | bytes 1 | tf_op jit(solution)/shard_map/pallas_call | solution.py:500
  28.8 0.0 collective-permute-done.2.rows_ref
  28.8 1.8 %shard_map.98.rest_1_.base_ref = f32[240,2048]{1,0:T(8,128)S(1)} custom-call(s32[1]{0:T(128)} %bitcast.core_ref, bf16[8,64,240]{2,1,0:T(8,128)(2,1)S(1)} %collective-permute-done.2.rows_ref, bf16[240,256]{1,0:T(8,128)(2,1)S(1)} %get-tuple-element.19.table_ref, bf16[256,512]{1,0:T(8,128)(2,1)S(1)} %get-tuple-element.24.wide_ref, ...), custom_call_target="tpu_custom_call" | custom-call | flops 1 | bytes 1 | tf_op jit(solution)/shard_map/pallas_call | solution.py:481
  30.7 1.9 %collective-permute-done.1.inflow_ref = bf16[240,512]{1,0:T(8,128)(2,1)S(1)} collective-permute-done((bf16[240,512]{1,0:T(8,128)(2,1)S(1)}, bf16[240,512]{1,0:T(8,128)(2,1)S(1)}, u32[]{:S(2)}, u32[]{:S(2)}) %collective-permute-start.1) | collective-permute-done | bytes 245792 | tf_op jit(solution)/shard_map/ppermute | solution.py:469
  32.6 1.3 %collective-permute-start.3 = (bf16[240,512]{1,0:T(8,128)(2,1)S(1)}, bf16[240,512]{1,0:T(8,128)(2,1)S(1)}, u32[]{:S(2)}, u32[]{:S(2)}) collective-permute-start(bf16[240,512]{1,0:T(8,128)(2,1)S(1)} %get-tuple-element.32), channel_id=1, source_target_pairs={{0,1},{1,0},{2,3},{3,2},{4,5},{5,4},{6,7},{7,6},{8,9},{9,8},{10,11... | collective-permute-start | bytes 737288 | tf_op jit(solution)/shard_map/ppermute | solution.py:527
  33.9 0.0 collective-permute-done.4.inflow_ref
  33.9 1.7 %shard_map.101.rest_0_ = bf16[240,32,128]{2,1,0:T(8,128)(2,1)} custom-call(s32[1]{0:T(128)} %bitcast.core_ref, s32[1]{0:T(128)} %bitcast.1.pair_ref, bf16[240,16,128]{2,1,0:T(8,128)(2,1)S(1)} %shard_map.97.rest_0_.done_ref, bf16[240,512]{1,0:T(8,128)(2,1)S(1)} %collective-permute-done.4.inflow_ref, f32[240,2048]{1,0:T(8,128)S(1)} %shard_map.98.rest_1_.base_ref, ...), custom_call_target="tpu_custom_call" | custom-call | flops 1 | bytes 1 | tf_op jit(solution)/shard_map/pallas_call | solution.py:508
  35.6 0.0 collective-permute-done.3.inflow_ref
  (6 shorter events, 0.1 us)
Async XLA Ops:
  0.0 9.7 %copy-start = (s32[1,1,32,128]{3,2,1,0:T(8,128)S(1)}, s32[1,1,32,128]{3,2,1,0:T(8,128)}, u32[]{:S(2)}) copy-start(s32[1,1,32,128]{3,2,1,0:T(8,128)} %param.17) | copy-start | bytes 49156
  0.0 9.7 %copy-start.5 = (s32[1,1,32]{2,1,0:T(1,128)S(1)}, s32[1,1,32]{2,1,0:T(1,128)}, u32[]{:S(2)}) copy-start(s32[1,1,32]{2,1,0:T(1,128)} %param.16) | copy-start | bytes 388
  0.0 9.7 %copy-start.4 = (s32[128,1]{0,1:T(1,128)S(1)}, s32[128,1]{0,1:T(1,128)}, u32[]{:S(2)}) copy-start(s32[128,1]{0,1:T(1,128)} %param.13) | copy-start | bytes 1540
  0.0 9.7 %copy-start.3 = (f32[128,4]{0,1:T(4,128)S(1)}, f32[128,4]{0,1:T(4,128)}, u32[]{:S(2)}) copy-start(f32[128,4]{0,1:T(4,128)} %param.12) | copy-start | bytes 6148
  0.0 9.7 %copy-start.2 = (s32[128,4]{0,1:T(4,128)S(1)}, s32[128,4]{0,1:T(4,128)}, u32[]{:S(2)}) copy-start(s32[128,4]{0,1:T(4,128)} %param.11) | copy-start | bytes 6148
  0.0 11.0 %copy-start.6 = (f32[8]{0:T(128)S(1)}, f32[8]{0:T(128)}, u32[]{:S(2)}) copy-start(f32[8]{0:T(128)} %param.15) | copy-start | bytes 100
  0.0 11.0 %copy-start.1 = (f32[8,240]{1,0:T(8,128)S(1)}, f32[8,240]{1,0:T(8,128)}, u32[]{:S(2)}) copy-start(f32[8,240]{1,0:T(8,128)} %shape_ref.1) | copy-start | bytes 23044
  2.4 21.7 %all-to-all-start = ((bf16[16,64,240]{2,1,0:T(8,128)(2,1)}), bf16[16,64,240]{2,1,0:T(8,128)(2,1)S(1)}, u32[]{:S(2)}, u32[]{:S(2)}) async-start(bf16[16,64,240]{2,1,0:T(8,128)(2,1)} %bitcast.21), calls=%async_computation | async-start | bytes 1048576 | tf_op jit(solution)/shard_map/all_to_all | solution.py:423
  9.8 1.3 %collective-permute-start = (f32[64,128]{1,0:T(8,128)S(1)}, f32[64,128]{1,0:T(8,128)S(1)}, u32[]{:S(2)}, u32[]{:S(2)}) collective-permute-start(f32[64,128]{1,0:T(8,128)S(1)} %shard_map.92.own_ref), channel_id=1, source_target_pairs={{0,1},{1,0},{2,3},{3,2},{4,5},{5,4},{6,7},{7,6},{8,9},{9,8},{10,11... | collective-permute-start | bytes 98312 | tf_op jit(solution)/shard_map/ppermute | solution.py:438
  24.1 4.8 %collective-permute-start.2 = (bf16[8,64,240]{2,1,0:T(8,128)(2,1)S(1)}, bf16[8,64,240]{2,1,0:T(8,128)(2,1)S(1)}, u32[]{:S(2)}, u32[]{:S(2)}) collective-permute-start(bf16[8,64,240]{2,1,0:T(8,128)(2,1)S(1)} %shard_map.94.after_ref), channel_id=1, source_target_pairs={{0,1},{1,0},{2,3},{3,2},{4,5},{5,4},{6,7},{7,6},{8,9},{9,8},{10,11... | collective-permute-start | bytes 737288 | tf_op jit(solution)/shard_map/ppermute | solution.py:470
  25.5 7.1 %collective-permute-start.1 = (bf16[240,512]{1,0:T(8,128)(2,1)S(1)}, bf16[240,512]{1,0:T(8,128)(2,1)S(1)}, u32[]{:S(2)}, u32[]{:S(2)}) collective-permute-start(bf16[240,512]{1,0:T(8,128)(2,1)S(1)} %get-tuple-element.23), channel_id=1, source_target_pairs={{0,2},{2,0},{1,3},{3,1},{4,6},{6,4},{5,7},{7,5},{8,10},{10,8},{9,1... | collective-permute-start | bytes 737288 | tf_op jit(solution)/shard_map/ppermute | solution.py:469
  25.5 8.4 %collective-permute-start.4 = (bf16[240,512]{1,0:T(8,128)(2,1)S(1)}, bf16[240,512]{1,0:T(8,128)(2,1)S(1)}, u32[]{:S(2)}, u32[]{:S(2)}) collective-permute-start(bf16[240,512]{1,0:T(8,128)(2,1)S(1)} %get-tuple-element.27.inflow_ref), channel_id=1, source_target_pairs={{0,1},{1,0},{2,3},{3,2},{4,5},{5,4},{6,7},{7,6},{8,9},{9,8},{10,11... | collective-permute-start | bytes 737288 | tf_op jit(solution)/shard_map/ppermute | solution.py:471
  32.6 3.0 %collective-permute-start.3 = (bf16[240,512]{1,0:T(8,128)(2,1)S(1)}, bf16[240,512]{1,0:T(8,128)(2,1)S(1)}, u32[]{:S(2)}, u32[]{:S(2)}) collective-permute-start(bf16[240,512]{1,0:T(8,128)(2,1)S(1)} %get-tuple-element.32), channel_id=1, source_target_pairs={{0,1},{1,0},{2,3},{3,2},{4,5},{5,4},{6,7},{7,6},{8,9},{9,8},{10,11... | collective-permute-start | bytes 737288 | tf_op jit(solution)/shard_map/ppermute | solution.py:527

commit v12 on v10

--- a/solution.py
+++ b/solution.py
@@ -244,12 +244,14 @@
     return jnp.concatenate(parts, axis=1)
 
 
+def rows_kernel(core_ref, rows_ref, send_ref):
+    send_ref[...] = rows_ref[:, 1 - core_ref[0]]
+
+
 def head_kernel(
-    class_count, core_ref, pair_ref, rows_ref, table_ref, mix_ref, pass_ref, cls_ref,
-    panel_ref, first_ref, send_ref,
-):
-    send_ref[...] = jnp.where(core_ref[0] == 0, rows_ref[:, 1], rows_ref[:, 0])
-
+    class_count, pair_ref, rows_ref, table_ref, mix_ref, pass_ref, cls_ref, after_ref,
+    panel_ref, first_ref,
+):
     @pl.when(pair_ref[0] == 0)
     def _():
         wide = panel_ref.shape[1]
@@ -463,12 +465,18 @@
 
     panel_shape = struct((hours, wide), BF)
     float_shape = struct((hours, wide), F32)
-    panel, first, rows_send = call(
+    rows_send = call(
+        rows_kernel,
+        struct((regions, half * slot, hours), BF),
+        in_specs=[SCALAR] + vmem(1),
+        out_specs=vmem(1)[0],
+    )(core_arg, received)
+    panel, first = call(
         functools.partial(head_kernel, class_count),
-        (panel_shape, panel_shape, struct((regions, half * slot, hours), BF)),
-        in_specs=[SCALAR] * 2 + vmem(5),
-        out_specs=tuple(vmem(3)),
-    )(core_arg, pair_arg, received, table, mix, passing, cls_out)
+        (panel_shape, panel_shape),
+        in_specs=[SCALAR] + vmem(6),
+        out_specs=tuple(vmem(2)),
+    )(pair_arg, received, table, mix, passing, cls_out, rows_send)
     inflow = lax.ppermute(panel, "pair", [(0, 1), (1, 0)]) if pairs > 1 else panel
     rows_other = lax.ppermute(rows_send, "core", swap)
     first_other = lax.ppermute(first, "core", swap)

time: 35.8 us -> 35.8 us (level)
  transfers between devices with their start and end apart: 6 -> 6, of which waited for: 3 -> 3; matrix products, arithmetic and copies ran while one was open for 0% -> 0% of each run, Pallas kernels for 21% -> 24%
where the time goes in v12:
time: 35.8 us; the launch traced here: 35.6 us
  waiting for transfers between devices  14.9 us (42%)
  Pallas kernels  11 us (31%)
  starting transfers between devices  9.62 us (27%)
    all_to_all x1, waiting for transfers between devices, local(): lax.all_to_all(send.reshape(regions * 2, half * slot, hours), ('side', 'r...  11.9 us
    all_to_all x1, starting transfers between devices, local(): lax.all_to_all(send.reshape(regions * 2, half * slot, hours), ('side', 'r...  7.34 us
    pallas_call x1, Pallas kernels, local(): call(functools.partial(other_kernel, class_count), (base_shape, struct((h...  2.69 us
    pallas_call x1, Pallas kernels, local(): call(functools.partial(pack_kernel, slot), struct((regions, 2, half * slo...  2.32 us
    ppermute x1, waiting for transfers between devices, local(): lax.ppermute(panel, 'pair', [(0, 1), (1, 0)])  1.88 us
    pallas_call x1, Pallas kernels, local(): call(functools.partial(base_own_kernel, class_count), tuple(shapes), in_s...  1.83 us
    pallas_call x2, Pallas kernels, late(): call(functools.partial(late_kernel, class_count, top), struct((hours, mem...  1.7 us
    ppermute x1, starting transfers between devices, local(): gotten = lax.ppermute(given, 'core', swap)  1.32 us
  transfers between devices with their start and end apart: 6, of which 3 were waited for; matrix products, arithmetic and copies ran while one was open for 0% of the time, Pallas kernels for 24%

profile of v12, /device:TPU:1, one launch (start us, length us, event | category | flops | bytes accessed | tf_op | source)
XLA Modules:
  0.0 35.6 jit_solution(11316481891087905851)
XLA Ops:
  0.0 0.0 copy-start
  0.0 0.0 copy-start.5
  0.0 0.0 copy-start.4
  0.0 0.0 copy-start.3
  0.0 0.0 copy-start.2
  0.0 0.0 copy-start.6
  0.0 0.0 copy-start.1
  0.0 2.3 %shard_map.91 = bf16[8,2,64,240]{3,2,1,0:T(8,128)(2,1)} custom-call(f32[32,32,240]{2,1,0:T(8,128)} %bitcast.22, s32[1,32]{1,0:T(1,128)} %bitcast.23), custom_call_target="tpu_custom_call" | custom-call | flops 1 | bytes 1 | tf_op jit(solution)/shard_map/pallas_call | solution.py:420
  2.4 7.3 %all-to-all-start = ((bf16[16,64,240]{2,1,0:T(8,128)(2,1)}), bf16[16,64,240]{2,1,0:T(8,128)(2,1)S(1)}, u32[]{:S(2)}, u32[]{:S(2)}) async-start(bf16[16,64,240]{2,1,0:T(8,128)(2,1)} %bitcast.21), calls=%async_computation | async-start | bytes 1048576 | tf_op jit(solution)/shard_map/all_to_all | solution.py:434
  9.7 0.0 copy-done
  9.7 0.0 copy-done.5
  9.7 0.0 copy-done.4
  9.7 0.0 copy-done.3
  9.8 0.0 copy-done.2
  9.8 0.2 collective-permute-start
  9.9 1.1 %collective-permute-done.other_ref = f32[64,128]{1,0:T(8,128)S(1)} collective-permute-done((f32[64,128]{1,0:T(8,128)S(1)}, f32[64,128]{1,0:T(8,128)S(1)}, u32[]{:S(2)}, u32[]{:S(2)}) %collective-permute-start) | collective-permute-done | bytes 32800 | tf_op jit(solution)/shard_map/ppermute | solution.py:449
  11.0 0.0 copy-done.6
  11.1 0.0 copy-done.1
  11.1 1.1 %shard_map.93 = (bf16[240,256]{1,0:T(8,128)(2,1)S(1)}, bf16[2,256,128]{2,1,0:T(8,128)(2,1)S(1)}, bf16[2,256,256]{2,1,0:T(8,128)(2,1)S(1)}, f32[2,8,256]{2,1,0:T(...) custom-call(s32[1]{0:T(128)} %bitcast.core_ref, ...), custom_call_target="tpu_custom_call" | custom-call | flops 1 | bytes 1 | tf_op jit(solution)/shard_map/pallas_call | solution.py:450
  12.2 11.9 %all-to-all-done = bf16[16,64,240]{2,1,0:T(8,128)(2,1)S(1)} async-done(((bf16[16,64,240]{2,1,0:T(8,128)(2,1)}), bf16[16,64,240]{2,1,0:T(8,128)(2,1)S(1)}, u32[]{:S(2)}, u32[]{:S(2)}) %all-to-all-start) | async-done | bytes 491552 | tf_op jit(solution)/shard_map/all_to_all | solution.py:434
  24.1 0.1 collective-permute-start.2
  24.2 1.3 %shard_map.95 = (bf16[240,512]{1,0:T(8,128)(2,1)S(1)}, bf16[240,512]{1,0:T(8,128)(2,1)S(1)}) custom-call(s32[1]{0:T(128)} %bitcast.1.pair_ref, bf16[8,2,64,240]{3,2,1,0:T(8,128)(2,1)S(1)} %bitcast.13, bf16[240,256]{1,0:T(8,128)(2,1)S(1)} %get-tuple-element.21.table_ref, bf16[2,256,128]{2,1,0:T(8,128)(2,1)S(1)} %get-tuple-element.22.mix_ref, ...), custom_call_target="tpu_custom_call" | custom-call | flops 1 | bytes 1 | tf_op jit(solution)/shard_map/pallas_call | solution.py:474
  25.5 0.1 collective-permute-start.1
  25.5 0.6 %collective-permute-start.4 = (bf16[240,512]{1,0:T(8,128)(2,1)S(1)}, bf16[240,512]{1,0:T(8,128)(2,1)S(1)}, u32[]{:S(2)}, u32[]{:S(2)}) collective-permute-start(bf16[240,512]{1,0:T(8,128)(2,1)S(1)} %get-tuple-element.29.inflow_ref), channel_id=1, source_target_pairs={{0,1},{1,0},{2,3},{3,2},{4,5},{5,4},{6,7},{7,6},{8,9},{9,8},{10,11... | collective-permute-start | bytes 737288 | tf_op jit(solution)/shard_map/ppermute | solution.py:482
  26.2 1.8 %shard_map.96 = (f32[240,2048]{1,0:T(8,128)S(1)}, f32[240,512]{1,0:T(8,128)S(1)}) custom-call(s32[1]{0:T(128)} %bitcast.core_ref, s32[1]{0:T(128)} %bitcast.1.pair_ref, bf16[8,2,64,240]{3,2,1,0:T(8,128)(2,1)S(1)} %bitcast.14, bf16[240,256]{1,0:T(8,128)(2,1)S(1)} %get-tuple-element.21.table_ref, bf16[256,512]{1,0:T(8,128)(2,1)S(1)} %get-tuple-element.26.wide_ref, ...), custom_call_target="tpu_custom_call" | custom-call | flops 1 | bytes 1 | tf_op jit(solution)/shard_map/pallas_call | solution.py:486
  28.0 0.0 collective-permute-done.2.rows_ref
  28.0 2.7 %shard_map.97 = (f32[240,2048]{1,0:T(8,128)S(1)}, bf16[240,16,128]{2,1,0:T(8,128)(2,1)S(1)}) custom-call(s32[1]{0:T(128)} %bitcast.core_ref, s32[1]{0:T(128)} %bitcast.1.pair_ref, bf16[8,64,240]{2,1,0:T(8,128)(2,1)S(1)} %collective-permute-done.2.rows_ref, bf16[240,256]{1,0:T(8,128)(2,1)S(1)} %get-tuple-element.21.table_ref, ...), custom_call_target="tpu_custom_call" | custom-call | flops 1 | bytes 1 | tf_op jit(solution)/shard_map/pallas_call | solution.py:492
  30.7 1.9 %collective-permute-done.1.inflow_ref = bf16[240,512]{1,0:T(8,128)(2,1)S(1)} collective-permute-done((bf16[240,512]{1,0:T(8,128)(2,1)S(1)}, bf16[240,512]{1,0:T(8,128)(2,1)S(1)}, u32[]{:S(2)}, u32[]{:S(2)}) %collective-permute-start.1) | collective-permute-done | bytes 245792 | tf_op jit(solution)/shard_map/ppermute | solution.py:480
  32.6 1.3 %collective-permute-start.3 = (bf16[240,512]{1,0:T(8,128)(2,1)S(1)}, bf16[240,512]{1,0:T(8,128)(2,1)S(1)}, u32[]{:S(2)}, u32[]{:S(2)}) collective-permute-start(bf16[240,512]{1,0:T(8,128)(2,1)S(1)} %get-tuple-element.35), channel_id=1, source_target_pairs={{0,1},{1,0},{2,3},{3,2},{4,5},{5,4},{6,7},{7,6},{8,9},{9,8},{10,11... | collective-permute-start | bytes 737288 | tf_op jit(solution)/shard_map/ppermute | solution.py:537
  33.9 0.0 collective-permute-done.4.inflow_ref
  33.9 1.7 %shard_map.100.rest_0_ = bf16[240,32,128]{2,1,0:T(8,128)(2,1)} custom-call(s32[1]{0:T(128)} %bitcast.core_ref, s32[1]{0:T(128)} %bitcast.1.pair_ref, bf16[240,16,128]{2,1,0:T(8,128)(2,1)S(1)} %get-tuple-element.33.rest_0_.done_ref, bf16[240,512]{1,0:T(8,128)(2,1)S(1)} %collective-permute-done.4.inflow_ref, f32[240,2048]{1,0:T(8,128)S(1)} %get-tuple-element.36.base_ref, ...), custom_call_target="tpu_custom_call" | custom-call | flops 1 | bytes 1 | tf_op jit(solution)/shard_map/pallas_call | solution.py:519
  35.6 0.0 collective-permute-done.3.inflow_ref
  (5 shorter events, 0.1 us)
Async XLA Ops:
  0.0 9.7 %copy-start = (s32[1,1,32,128]{3,2,1,0:T(8,128)S(1)}, s32[1,1,32,128]{3,2,1,0:T(8,128)}, u32[]{:S(2)}) copy-start(s32[1,1,32,128]{3,2,1,0:T(8,128)} %param.17) | copy-start | bytes 49156
  0.0 9.7 %copy-start.5 = (s32[1,1,32]{2,1,0:T(1,128)S(1)}, s32[1,1,32]{2,1,0:T(1,128)}, u32[]{:S(2)}) copy-start(s32[1,1,32]{2,1,0:T(1,128)} %param.16) | copy-start | bytes 388
  0.0 9.7 %copy-start.4 = (s32[128,1]{0,1:T(1,128)S(1)}, s32[128,1]{0,1:T(1,128)}, u32[]{:S(2)}) copy-start(s32[128,1]{0,1:T(1,128)} %param.13) | copy-start | bytes 1540
  0.0 9.7 %copy-start.3 = (f32[128,4]{0,1:T(4,128)S(1)}, f32[128,4]{0,1:T(4,128)}, u32[]{:S(2)}) copy-start(f32[128,4]{0,1:T(4,128)} %param.12) | copy-start | bytes 6148
  0.0 9.7 %copy-start.2 = (s32[128,4]{0,1:T(4,128)S(1)}, s32[128,4]{0,1:T(4,128)}, u32[]{:S(2)}) copy-start(s32[128,4]{0,1:T(4,128)} %param.11) | copy-start | bytes 6148
  0.0 11.0 %copy-start.6 = (f32[8]{0:T(128)S(1)}, f32[8]{0:T(128)}, u32[]{:S(2)}) copy-start(f32[8]{0:T(128)} %param.15) | copy-start | bytes 100
  0.0 11.0 %copy-start.1 = (f32[8,240]{1,0:T(8,128)S(1)}, f32[8,240]{1,0:T(8,128)}, u32[]{:S(2)}) copy-start(f32[8,240]{1,0:T(8,128)} %shape_ref.1) | copy-start | bytes 23044
  2.4 21.7 %all-to-all-start = ((bf16[16,64,240]{2,1,0:T(8,128)(2,1)}), bf16[16,64,240]{2,1,0:T(8,128)(2,1)S(1)}, u32[]{:S(2)}, u32[]{:S(2)}) async-start(bf16[16,64,240]{2,1,0:T(8,128)(2,1)} %bitcast.21), calls=%async_computation | async-start | bytes 1048576 | tf_op jit(solution)/shard_map/all_to_all | solution.py:434
  9.8 1.3 %collective-permute-start = (f32[64,128]{1,0:T(8,128)S(1)}, f32[64,128]{1,0:T(8,128)S(1)}, u32[]{:S(2)}, u32[]{:S(2)}) collective-permute-start(f32[64,128]{1,0:T(8,128)S(1)} %shard_map.92.own_ref), channel_id=1, source_target_pairs={{0,1},{1,0},{2,3},{3,2},{4,5},{5,4},{6,7},{7,6},{8,9},{9,8},{10,11... | collective-permute-start | bytes 98312 | tf_op jit(solution)/shard_map/ppermute | solution.py:449
  24.1 3.9 %collective-permute-start.2 = (bf16[8,64,240]{2,1,0:T(8,128)(2,1)S(1)}, bf16[8,64,240]{2,1,0:T(8,128)(2,1)S(1)}, u32[]{:S(2)}, u32[]{:S(2)}) collective-permute-start(bf16[8,64,240]{2,1,0:T(8,128)(2,1)S(1)} %shard_map.94.after_ref), channel_id=1, source_target_pairs={{0,1},{1,0},{2,3},{3,2},{4,5},{5,4},{6,7},{7,6},{8,9},{9,8},{10,11... | collective-permute-start | bytes 737288 | tf_op jit(solution)/shard_map/ppermute | solution.py:481
  25.5 7.1 %collective-permute-start.1 = (bf16[240,512]{1,0:T(8,128)(2,1)S(1)}, bf16[240,512]{1,0:T(8,128)(2,1)S(1)}, u32[]{:S(2)}, u32[]{:S(2)}) collective-permute-start(bf16[240,512]{1,0:T(8,128)(2,1)S(1)} %get-tuple-element.25), channel_id=1, source_target_pairs={{0,2},{2,0},{1,3},{3,1},{4,6},{6,4},{5,7},{7,5},{8,10},{10,8},{9,1... | collective-permute-start | bytes 737288 | tf_op jit(solution)/shard_map/ppermute | solution.py:480
  25.5 8.4 %collective-permute-start.4 = (bf16[240,512]{1,0:T(8,128)(2,1)S(1)}, bf16[240,512]{1,0:T(8,128)(2,1)S(1)}, u32[]{:S(2)}, u32[]{:S(2)}) collective-permute-start(bf16[240,512]{1,0:T(8,128)(2,1)S(1)} %get-tuple-element.29.inflow_ref), channel_id=1, source_target_pairs={{0,1},{1,0},{2,3},{3,2},{4,5},{5,4},{6,7},{7,6},{8,9},{9,8},{10,11... | collective-permute-start | bytes 737288 | tf_op jit(solution)/shard_map/ppermute | solution.py:482
  32.6 3.0 %collective-permute-start.3 = (bf16[240,512]{1,0:T(8,128)(2,1)S(1)}, bf16[240,512]{1,0:T(8,128)(2,1)S(1)}, u32[]{:S(2)}, u32[]{:S(2)}) collective-permute-start(bf16[240,512]{1,0:T(8,128)(2,1)S(1)} %get-tuple-element.35), channel_id=1, source_target_pairs={{0,1},{1,0},{2,3},{3,2},{4,5},{5,4},{6,7},{7,6},{8,9},{9,8},{10,11... | collective-permute-start | bytes 737288 | tf_op jit(solution)/shard_map/ppermute | solution.py:537
